TPU v7x, 32 devices: a whole 2x2x4 slice. The times are simulated.
32 devices in a mesh: dp: 16 (over z, y, core), expert: 2 (over x).
Axes of the slice: x: 2, y: 2, z: 4, core: 2. Of those that a mesh axis runs over, the one named last changes fastest.
Arguments:
- tokens: bfloat16 [31520, 512], P(('dp', 'expert')), may hold values from -6 to 6
- choices: int32 [31520, 2], P(('dp', 'expert')), may hold values from 0 to 31, all different within a row; in each aligned block of 985 rows (0 to 984, 985 to 1969, ...) at most 128 rows name the same one
- ln1_gain: float32 [512], P('dp'), may hold values from 0.5 to 1.5
- ln1_bias: float32 [512], P('dp'), may hold values from -4 to 4
- w_qkv: float32 [512, 1536], P('dp'), may hold values from -0.25 to 0.25
- w_proj: float32 [512, 512], P('dp'), may hold values from -0.5 to 0.5
- ln2_gain: float32 [512], P('dp'), may hold values from 0.5 to 1.5
- ln2_bias: float32 [512], P('dp'), may hold values from -4 to 4
- w_router: float32 [512, 32], P('dp'), may hold values from -0.1875 to 0.1875
- w_expert_in: float32 [32, 512, 2048], P('expert', 'dp'), may hold values from -0.25 to 0.25
- w_expert_out: float32 [32, 2048, 512], P('expert', 'dp'), may hold values from -2 to 2
- cotangent: bfloat16 [31520, 512], P(('dp', 'expert')), may hold values from -6 to 6
Outputs:
- output: bfloat16 [31520, 512], P(('dp', 'expert'))
- input_grad: float32 [31520, 512], P(('dp', 'expert'))
- ln1_gain_grad: float32 [512], P('dp')
- ln1_bias_grad: float32 [512], P('dp')
- qkv_grad: float32 [512, 1536], P('dp')
- proj_grad: float32 [512, 512], P('dp')
- ln2_gain_grad: float32 [512], P('dp')
- ln2_bias_grad: float32 [512], P('dp')
- router_grad: float32 [512, 32], P('dp')
- expert_in_grad: float32 [32, 512, 2048], P('expert', 'dp')
- expert_out_grad: float32 [32, 2048, 512], P('expert', 'dp')
Inputs may be any that keep to these rules, and one draw needn't show every extreme that they name: `choices`: each token names two different experts. Among the 985 tokens of one device no expert is named more than 128 times, and on some device some expert is named exactly 128 times.
All inputs are finite; a program needn't handle non-finite values.
Results may differ from a plain program's by a relative error of at most 0.025.
Values may be sent and summed in bfloat16 or wider, within the bound.
A program may use at most 256 MiB of HBM per device.

v0:
```python
import jax
import jax.numpy as jnp
from jax import lax
from jax.sharding import PartitionSpec as P

D = 512
HEADS = 8
EXPERTS = 32
SEQ = 197
CAP = 128


epsilon = 1e-06


def norm_forward(values, gain_vec, offset):
    center = values - jnp.mean(values, axis=-1, keepdims=True)
    factor = lax.rsqrt(jnp.mean(center * center, axis=-1, keepdims=True) + epsilon)
    normed = center * factor
    return (normed, factor, normed * gain_vec + offset)


def norm_backward(normed, factor, gain_vec, upstream):
    scaled = upstream * gain_vec
    inner_part = (
        scaled
        - jnp.mean(scaled, axis=-1, keepdims=True)
        - normed * jnp.mean(scaled * normed, axis=-1, keepdims=True)
    )
    return (factor * inner_part, jnp.sum(upstream * normed, axis=0), jnp.sum(upstream, axis=0))


def column_product(left, right):
    return lax.dot_general(
        left, right, (((0,), (0,)), ((), ())), preferred_element_type=jnp.float32
    )


def times_transposed(left, right):
    return lax.dot_general(
        left, right, (((1,), (1,)), ((), ())), preferred_element_type=jnp.float32
    )


def body(
    tokens,
    choices,
    ln1_gain,
    ln1_bias,
    w_qkv,
    w_proj,
    ln2_gain,
    ln2_bias,
    w_router,
    w_expert_in,
    w_expert_out,
    cotangent,
):
    low_type = jnp.bfloat16
    full_type = jnp.float32
    gathered = (
        lax.all_gather(ln1_gain.astype(low_type), "dp", axis=0, tiled=True),
        lax.all_gather(ln1_bias.astype(low_type), "dp", axis=0, tiled=True),
        lax.all_gather(w_qkv.astype(low_type), "dp", axis=0, tiled=True),
        lax.all_gather(w_proj.astype(low_type), "dp", axis=0, tiled=True),
        lax.all_gather(ln2_gain.astype(low_type), "dp", axis=0, tiled=True),
        lax.all_gather(ln2_bias.astype(low_type), "dp", axis=0, tiled=True),
        lax.all_gather(w_router.astype(low_type), "dp", axis=0, tiled=True),
    )
    gain_one = gathered[0].astype(full_type)
    bias_one = gathered[1].astype(full_type)
    qkv_weight = gathered[2]
    proj_weight = gathered[3]
    gain_two = gathered[4].astype(full_type)
    bias_two = gathered[5].astype(full_type)
    router_weight = gathered[6]
    expert_first, expert_second = (
        lax.all_gather(w_expert_in.astype(low_type), "dp", axis=1, tiled=True),
        lax.all_gather(w_expert_out.astype(low_type), "dp", axis=1, tiled=True),
    )
    images = tokens.shape[0] // SEQ
    head_size = D // HEADS
    qk_factor = head_size ** (-0.5)
    inputs = tokens.astype(full_type)
    normed_one, factor_one, hidden_one = norm_forward(inputs, gain_one, bias_one)
    attn_in = hidden_one.astype(low_type)
    mixed_rows = jnp.dot(attn_in, qkv_weight, preferred_element_type=full_type).astype(low_type)
    head_rows = mixed_rows.reshape(images, SEQ, 3, HEADS, head_size)
    queries = head_rows[:, :, 0]
    key_rows = head_rows[:, :, 1]
    value_rows = head_rows[:, :, 2]

    def attention_probs():
        scores = (
            jnp.einsum("ishd,ithd->ihst", queries, key_rows, preferred_element_type=full_type)
            * qk_factor
        )
        return jax.nn.softmax(scores, axis=-1)

    attn_probs = attention_probs()
    context = (
        jnp.einsum(
            "ihst,ithd->ishd",
            attn_probs.astype(low_type),
            value_rows,
            preferred_element_type=full_type,
        )
        .reshape(images * SEQ, D)
        .astype(low_type)
    )
    resid = inputs + jnp.dot(context, proj_weight, preferred_element_type=full_type)
    normed_two, factor_two, hidden_two = norm_forward(resid, gain_two, bias_two)
    router_in = hidden_two.astype(low_type)
    logits = jnp.dot(router_in, router_weight, preferred_element_type=full_type)
    router_probs = jax.nn.softmax(logits, axis=-1)
    pick_table = choices[:, :, None] == jnp.arange(EXPERTS, dtype=jnp.int32)[None, None, :]
    pick_float = pick_table.astype(full_type)
    gate_values = jnp.sum(router_probs[:, None, :] * pick_float, axis=-1)
    flat_picks = pick_table.astype(jnp.int32).reshape(-1, EXPERTS)
    running = jnp.cumsum(flat_picks, axis=0)
    slot_index = jnp.sum((running - 1) * flat_picks, axis=-1)
    destination = choices.reshape(-1) * CAP + slot_index
    repeated = jnp.repeat(router_in, 2, axis=0)
    outgoing = (
        jnp.zeros((EXPERTS * CAP, D), low_type)
        .at[destination]
        .set(repeated)
        .reshape(EXPERTS, CAP, D)
    )
    received = lax.all_to_all(outgoing, "expert", split_axis=0, concat_axis=1, tiled=True)
    inner_rows = jnp.einsum(
        "erd,edf->erf", received, expert_first, preferred_element_type=full_type
    )
    hidden = jax.nn.gelu(inner_rows).astype(low_type)
    returned = jnp.einsum(
        "erf,efd->erd", hidden, expert_second, preferred_element_type=full_type
    ).astype(low_type)
    combined = lax.all_to_all(returned, "expert", split_axis=1, concat_axis=0, tiled=True).reshape(
        EXPERTS * CAP, D
    )
    picked = combined[destination].reshape(-1, 2, D).astype(full_type)
    output = resid + jnp.sum(gate_values[:, :, None] * picked, axis=1)
    upstream = cotangent.astype(full_type)
    grad_gates = jnp.sum(upstream[:, None, :] * picked, axis=-1)
    grad_picked = (gate_values[:, :, None] * upstream[:, None, :]).astype(low_type).reshape(-1, D)
    grad_outgoing = (
        jnp.zeros((EXPERTS * CAP, D), low_type)
        .at[destination]
        .set(grad_picked)
        .reshape(EXPERTS, CAP, D)
    )
    grad_returned = lax.all_to_all(grad_outgoing, "expert", split_axis=0, concat_axis=1, tiled=True)
    back_first, back_second = (
        lax.all_gather(w_expert_in.astype(low_type), "dp", axis=1, tiled=True),
        lax.all_gather(w_expert_out.astype(low_type), "dp", axis=1, tiled=True),
    )
    grad_hidden = jnp.einsum(
        "erd,efd->erf", grad_returned, back_second, preferred_element_type=full_type
    )
    gelu_value, gelu_pull = jax.vjp(jax.nn.gelu, inner_rows)
    grad_inner = gelu_pull(grad_hidden)[0].astype(low_type)
    grad_second = jnp.einsum(
        "erf,erd->efd", hidden, grad_returned, preferred_element_type=full_type
    )
    grad_first = jnp.einsum("erd,erf->edf", received, grad_inner, preferred_element_type=full_type)
    grad_received = jnp.einsum(
        "erf,edf->erd", grad_inner, back_first, preferred_element_type=full_type
    ).astype(low_type)
    grad_back = lax.all_to_all(
        grad_received, "expert", split_axis=1, concat_axis=0, tiled=True
    ).reshape(EXPERTS * CAP, D)
    grad_router_in = jnp.sum(grad_back[destination].reshape(-1, 2, D).astype(full_type), axis=1)
    expert_in_grad, expert_out_grad = (
        lax.psum_scatter(
            grad_first.astype(jnp.bfloat16), "dp", scatter_dimension=1, tiled=True
        ).astype(jnp.float32),
        lax.psum_scatter(
            grad_second.astype(jnp.bfloat16), "dp", scatter_dimension=1, tiled=True
        ).astype(jnp.float32),
    )
    grad_probs = jnp.sum(grad_gates[:, :, None] * pick_float, axis=1)
    grad_logits = (
        router_probs * (grad_probs - jnp.sum(router_probs * grad_probs, axis=-1, keepdims=True))
    ).astype(low_type)
    router_grad = column_product(router_in, grad_logits)
    grad_router_in = grad_router_in + times_transposed(grad_logits, router_weight)
    grad_resid_two, gain_two_grad, bias_two_grad = norm_backward(
        normed_two, factor_two, gain_two, grad_router_in
    )
    grad_resid = upstream + grad_resid_two
    grad_attended = grad_resid.astype(low_type)
    proj_grad = column_product(context, grad_attended)
    grad_context = (
        times_transposed(grad_attended, proj_weight)
        .astype(low_type)
        .reshape(images, SEQ, HEADS, head_size)
    )
    probs_again = attention_probs()
    grad_weights = jnp.einsum(
        "ishd,ithd->ihst", grad_context, value_rows, preferred_element_type=full_type
    )
    grad_scores = (
        probs_again * (grad_weights - jnp.sum(probs_again * grad_weights, axis=-1, keepdims=True))
    ).astype(low_type)
    grad_queries = (
        jnp.einsum("ihst,ithd->ishd", grad_scores, key_rows, preferred_element_type=full_type)
        * qk_factor
    )
    grad_keys = (
        jnp.einsum("ihst,ishd->ithd", grad_scores, queries, preferred_element_type=full_type)
        * qk_factor
    )
    grad_values = jnp.einsum(
        "ihst,ishd->ithd",
        probs_again.astype(low_type),
        grad_context,
        preferred_element_type=full_type,
    )
    grad_mixed = (
        jnp.stack([grad_queries, grad_keys, grad_values], axis=2)
        .reshape(images * SEQ, 3 * D)
        .astype(low_type)
    )
    qkv_grad = column_product(attn_in, grad_mixed)
    grad_hidden_one = times_transposed(grad_mixed, qkv_weight)
    grad_input_one, gain_one_grad, bias_one_grad = norm_backward(
        normed_one, factor_one, gain_one, grad_hidden_one
    )
    input_grad = grad_resid + grad_input_one
    dense_grads = (
        gain_one_grad,
        bias_one_grad,
        qkv_grad,
        proj_grad,
        gain_two_grad,
        bias_two_grad,
        router_grad,
    )
    summed = (
        lax.psum(dense_grads[0].astype(jnp.bfloat16), "expert").astype(jnp.float32),
        lax.psum(dense_grads[1].astype(jnp.bfloat16), "expert").astype(jnp.float32),
        lax.psum(dense_grads[2].astype(jnp.bfloat16), "expert").astype(jnp.float32),
        lax.psum(dense_grads[3].astype(jnp.bfloat16), "expert").astype(jnp.float32),
        lax.psum(dense_grads[4].astype(jnp.bfloat16), "expert").astype(jnp.float32),
        lax.psum(dense_grads[5].astype(jnp.bfloat16), "expert").astype(jnp.float32),
        lax.psum(dense_grads[6].astype(jnp.bfloat16), "expert").astype(jnp.float32),
    )
    shares = (
        lax.psum_scatter(
            summed[0].astype(jnp.bfloat16), "dp", scatter_dimension=0, tiled=True
        ).astype(jnp.float32),
        lax.psum_scatter(
            summed[1].astype(jnp.bfloat16), "dp", scatter_dimension=0, tiled=True
        ).astype(jnp.float32),
        lax.psum_scatter(
            summed[2].astype(jnp.bfloat16), "dp", scatter_dimension=0, tiled=True
        ).astype(jnp.float32),
        lax.psum_scatter(
            summed[3].astype(jnp.bfloat16), "dp", scatter_dimension=0, tiled=True
        ).astype(jnp.float32),
        lax.psum_scatter(
            summed[4].astype(jnp.bfloat16), "dp", scatter_dimension=0, tiled=True
        ).astype(jnp.float32),
        lax.psum_scatter(
            summed[5].astype(jnp.bfloat16), "dp", scatter_dimension=0, tiled=True
        ).astype(jnp.float32),
        lax.psum_scatter(
            summed[6].astype(jnp.bfloat16), "dp", scatter_dimension=0, tiled=True
        ).astype(jnp.float32),
    )
    return (
        output.astype(low_type),
        input_grad,
        shares[0],
        shares[1],
        shares[2],
        shares[3],
        shares[4],
        shares[5],
        shares[6],
        expert_in_grad,
        expert_out_grad,
    )


def solution(mesh):
    placed = (
        P(("dp", "expert"), None),
        P(("dp", "expert"), None),
        P("dp"),
        P("dp"),
        P("dp", None),
        P("dp", None),
        P("dp"),
        P("dp"),
        P("dp", None),
        P("expert", "dp", None),
        P("expert", "dp", None),
        P(("dp", "expert"), None),
    )
    return jax.shard_map(
        body,
        mesh=mesh,
        in_specs=placed,
        out_specs=(
            P(("dp", "expert"), None),
            P(("dp", "expert"), None),
            P("dp"),
            P("dp"),
            P("dp", None),
            P("dp", None),
            P("dp"),
            P("dp"),
            P("dp", None),
            P("expert", "dp", None),
            P("expert", "dp", None),
        ),
        check_vma=False,
    )
```

profile of v0, /device:TPU:13, one launch (start us, length us, event | category | flops | bytes accessed | tf_op | source)
XLA Modules:
  0.0 1557.8 jit_solution(787296244313433721)
XLA Ops:
  8.9 3.8 convert_element_type.213
  12.9 3.8 convert_element_type.211
  19.0 22.7 %all-reduce.10 = (bf16[512]{0:T(512)(128)(2,1)S(1)}, bf16[512]{0:T(512)(128)(2,1)S(1)}, bf16[512]{0:T(512)(128)(2,1)S(1)}, bf16[512]{0:T(512)(128)(2,1)S(1)}) all-reduce(bf16[512]{0:T(512)(128)(2,1)S(1)} %dynamic-update-slice.1, bf16[512]{0:T(512)(128)(2,1)S(1)} %dynamic-update-slice, ...), channel_id=1, replica_groups=mesh['dp'=16,'expert'=2] {'dp'}, use_global_device_ids=true, to_apply=%add.2 | all-reduce | flops 2048 | bytes 8192
  43.0 9.1 reduce-window.6
  52.9 3.0 mul.261
  55.9 6.2 mul.262
  62.1 26.9 %all_gather.35 = bf16[512,32]{1,0:T(8,128)(2,1)S(1)} all-gather(bf16[32,32]{1,0:T(8,128)(2,1)S(1)} %convert_element_type.210), channel_id=1, replica_groups=mesh['dp'=16,'expert'=2] {'dp'}, dimensions={0}, use_global_device_ids=true | all-gather | bytes 34816 | tf_op jit(solution)/shard_map/all_gather | solution.py:68
  89.8 20.8 %all_gather.32 = bf16[512,512]{1,0:T(8,128)(2,1)S(1)} all-gather(bf16[32,512]{1,0:T(8,128)(2,1)S(1)} %convert_element_type.204), channel_id=1, replica_groups=mesh['dp'=16,'expert'=2] {'dp'}, dimensions={0}, use_global_device_ids=true | all-gather | bytes 557056 | tf_op jit(solution)/shard_map/all_gather | solution.py:65
  110.7 5.0 convolution_convert_fusion.2
  115.8 8.8 reshape.166
  124.5 5.6 fusion.66
  130.2 3.9 copy.144
  134.1 3.1 copy.146
  137.2 4.4 copy.145
  144.3 6.7 fusion.68
  151.1 3.2 copy-done.2
  158.0 3.2 convert_element_type.203
  165.3 19.3 %scatter_custom_fusion.1 = bf16[4096,512]{1,0:T(8,128)(2,1)} fusion(s32[1970]{0:T(1024)S(1)} %bitcast.115, bf16[]{:T(256)} %constant.41.clone.1, f32[1970,512]{1,0:T(8,128)} %mul.262, f32[1970]{0:T(1024)S(1)} %mul.259), kind=kCustom, calls=%fused_computation.43 | custom fusion | flops 2017280 | bytes 8237058 | tf_op jit(solution)/shard_map/scatter | solution.py:149
  184.6 5.6 all-to-all-start.2
  193.4 13.6 scatter_custom_fusion
  206.9 30.8 %all-to-all-done.2 = bf16[32,128,512]{2,1,0:T(8,128)(2,1)} async-done(((bf16[32,128,512]{2,1,0:T(8,128)(2,1)}), bf16[32,128,512]{2,1,0:T(8,128)(2,1)}, u32[]{:S(2)}, u32[]{:S(2)}) %all-to-all-start.2) | async-done | bytes 4194336 | tf_op jit(solution)/shard_map/all_to_all | solution.py:152
  237.8 5.8 all-to-all-start
  243.6 4.7 copy.125
  248.3 41.9 %all-to-all-done = bf16[32,128,512]{2,1,0:T(8,128)(2,1)} async-done(((bf16[32,128,512]{2,1,0:T(8,128)(2,1)}), bf16[32,128,512]{2,1,0:T(8,128)(2,1)}, u32[]{:S(2)}, u32[]{:S(2)}) %all-to-all-start) | async-done | bytes 4194336 | tf_op jit(solution)/shard_map/all_to_all | solution.py:130
  290.2 4.7 copy.121
  294.8 24.8 %fusion.71 = f32[16,256,2048]{2,1,0:T(8,128)} fusion(bf16[16,256,512]{2,1,0:T(8,128)(2,1)} %bitcast.105, bf16[16,2048,512]{2,1,0:T(8,128)(2,1)} %all-gather.8.cloned.1.call-done), kind=kOutput, calls=%fused_computation.122 | convolution fusion | flops 8589934592 | bytes 71303168 | tf_op jit(solution)/shard_map/erd,efd->erf/dot_general | solution.py:157
  319.6 76.7 %all-gather.6.cloned.1.call-done = bf16[16,512,2048]{2,1,0:T(8,128)(2,1)} async-done(((bf16[16,32,2048]{2,1,0:T(8,128)(2,1)}), bf16[16,512,2048]{2,1,0:T(8,128)(2,1)}) %all-gather.6.cloned.1.call-update) | async-done | bytes 33554448 | tf_op jit(solution)/shard_map/all_gather | solution.py:78
  396.4 46.7 %fusion.7 = (bf16[16,256,2048]{2,1,0:T(8,128)(2,1)}, f32[16,256,2048]{2,1,0:T(8,128)}) fusion(f32[16,256,2048]{2,1,0:T(8,128)} %fusion.71, bf16[16,256,512]{2,1,0:T(8,128)(2,1)} %bitcast.103, bf16[16,512,2048]{2,1,0:T(8,128)(2,1)} %all-gather.6.cloned.1.call-done), kind=kOutput, calls=%fused_computation.13 | convolution fusion | flops 8757706752 | bytes 121634816 | tf_op jit(solution)/shard_map/erd,edf->erf/dot_general | solution.py:131
  443.1 20.7 %convolution_convert_fusion.4 = bf16[16,256,512]{2,1,0:T(8,128)(2,1)} fusion(bf16[16,256,2048]{2,1,0:T(8,128)(2,1)} %get-tuple-element.48, bf16[16,512,2048]{2,1,0:T(8,128)(2,1)} %all-gather.6.cloned.1.call-done), kind=kOutput, calls=%fused_computation.33 | convolution fusion | flops 8592031744 | bytes 54525952 | tf_op jit(solution)/shard_map/erf,edf->erd/dot_general | solution.py:166
  463.8 6.5 copy.126
  470.2 5.8 all-to-all-start.3
  476.0 27.7 %convolution_convert_fusion.5 = bf16[16,256,512]{2,1,0:T(8,128)(2,1)} fusion(bf16[16,2048,512]{2,1,0:T(8,128)(2,1)} %all-gather.8.cloned.1.call-done, f32[16,256,2048]{2,1,0:T(8,128)} %get-tuple-element.49), kind=kOutput, calls=%fused_computation.34 | convolution fusion | flops 8667529216 | bytes 71303168 | tf_op jit(solution)/shard_map/erf,efd->erd/dot_general | solution.py:135
  503.8 6.5 copy.122
  510.2 13.0 all-to-all-done.3
  523.2 5.6 all-to-all-start.1
  529.2 6.5 copy.127
  535.7 12.3 gather_fusion.1
  548.0 5.4 reshape.177
  553.5 21.6 %all-to-all-done.1 = bf16[16,256,512]{2,0,1:T(8,128)(2,1)} async-done(((bf16[16,256,512]{2,0,1:T(8,128)(2,1)}), bf16[16,256,512]{2,0,1:T(8,128)(2,1)}, u32[]{:S(2)}, u32[]{:S(2)}) %all-to-all-start.1) | async-done | bytes 4194336 | tf_op jit(solution)/shard_map/all_to_all | solution.py:138
  575.1 6.5 copy.123
  581.6 11.9 gather_fusion
  593.5 5.5 reshape.176
  599.0 14.0 multiply_reduce_fusion.2
  617.0 8.2 reduce_sum.214
  625.3 2.9 multiply_reduce_fusion.4
  635.2 4.9 fusion.41
  640.2 5.2 multiply_reduce_fusion
  652.3 9.1 copy.134
  661.5 9.0 convert_element_type.228
  670.5 5.1 convolution_convert_fusion.3
  678.2 2.8 convolution_convert_fusion.7
  681.0 53.0 %reduce-scatter.10.cloned.1.call-done = bf16[32,1536]{1,0:T(8,128)(2,1)} async-done(((bf16[512,1536]{1,0:T(8,128)(2,1)}), bf16[32,1536]{1,0:T(8,128)(2,1)}) %reduce-scatter.10.cloned.1.call-update) | async-done | bytes 98320 | tf_op jit(solution)/shard_map/reduce_scatter | solution.py:255
  734.1 20.4 %convolution_convert_fusion.1 = bf16[16,512,2048]{2,1,0:T(8,128)(2,1)} fusion(bf16[16,256,512]{2,1,0:T(8,128)(2,1)} %bitcast.104, bf16[16,256,2048]{2,1,0:T(8,128)(2,1)} %get-tuple-element.48), kind=kOutput, calls=%fused_computation.16 | convolution fusion | flops 8606711808 | bytes 54525952 | tf_op jit(solution)/shard_map/erd,erf->edf/dot_general | solution.py:165
  754.6 27.2 %convolution_convert_fusion = bf16[16,2048,512]{2,1,0:T(8,128)(2,1)} fusion(bf16[16,256,512]{2,1,0:T(8,128)(2,1)} %bitcast.106, f32[16,256,2048]{2,1,0:T(8,128)} %get-tuple-element.49), kind=kOutput, calls=%fused_computation.15 | convolution fusion | flops 8682209280 | bytes 71303168 | tf_op jit(solution)/shard_map/erf,erd->efd/dot_general | solution.py:162
  782.5 5.7 fusion.32
  788.1 22.3 %all-reduce.9 = (bf16[512]{0:T(512)(128)(2,1)S(1)}, bf16[512]{0:T(512)(128)(2,1)S(1)}, bf16[512]{0:T(512)(128)(2,1)S(1)}, bf16[512]{0:T(512)(128)(2,1)S(1)}) all-reduce(bf16[512]{0:T(512)(128)(2,1)S(1)} %get-tuple-element.15, bf16[512]{0:T(512)(128)(2,1)S(1)} %get-tuple-element.20, ...), channel_id=2, replica_groups=mesh['dp'=16,'expert'=2] {'dp'}, use_global_device_ids=true, to_apply=%region_26.27.clone | all-reduce | flops 2048 | bytes 8192
  810.8 3.0 fusion.31
  813.8 37.3 %reduce-scatter.12.cloned.1.call-done = bf16[32,512]{1,0:T(8,128)(2,1)} async-done(((bf16[512,512]{1,0:T(8,128)(2,1)}), bf16[32,512]{1,0:T(8,128)(2,1)}) %reduce-scatter.12.cloned.1.call-update) | async-done | bytes 32784 | tf_op jit(solution)/shard_map/reduce_scatter | solution.py:258
  851.1 6.9 all-reduce.11
  861.3 13.8 all-reduce.14.cloned.1.call-done
  876.6 334.0 %reduce-scatter.6.cloned.1.call-done = bf16[16,32,2048]{2,1,0:T(8,128)(2,1)} async-done(((bf16[16,512,2048]{2,1,0:T(8,128)(2,1)}), bf16[16,32,2048]{2,1,0:T(8,128)(2,1)}) %reduce-scatter.6.cloned.1.call-update) | async-done | bytes 2097168 | tf_op jit(solution)/shard_map/reduce_scatter | solution.py:174
  1210.6 4.1 convert_element_type.244
  1214.7 331.9 %reduce-scatter.8.cloned.1.call-done = bf16[16,128,512]{2,1,0:T(8,128)(2,1)} async-done(((bf16[16,2048,512]{2,1,0:T(8,128)(2,1)}), bf16[16,128,512]{2,1,0:T(8,128)(2,1)}) %reduce-scatter.8.cloned.1.call-update) | async-done | bytes 2097168 | tf_op jit(solution)/shard_map/reduce_scatter | solution.py:177
  1546.6 4.2 convert_element_type.246
  (213 shorter events, 45.6 us)
Async XLA Ops:
  7.2 103.5 %all-gather.4.cloned.1.call-start = ((), (), s32[]{:S(2)}) async-start(), calls=%async_computation.9 | async-start | bytes 1671168 | tf_op jit(solution)/shard_map/all_gather | solution.py:64
  8.8 286.0 %all-gather.8.cloned.1.call-start = ((), (), s32[]{:S(2)}) async-start(), calls=%async_computation.11 | async-start | bytes 35651584 | tf_op jit(solution)/shard_map/all_gather | solution.py:79
  12.7 4.0 copy-start.48
  12.8 4.0 copy-start.49
  12.8 4.0 copy-start.50
  12.8 4.0 copy-start.51
  12.8 4.0 copy-start.45
  12.8 28.9 %copy-start.31 = (f32[32,512]{1,0:T(8,128)S(1)}, f32[32,512]{1,0:T(8,128)}, u32[]{:S(2)}) copy-start(f32[32,512]{1,0:T(8,128)} %param.17) | copy-start | bytes 196612
  12.8 29.0 %copy-start.26 = (s32[985,2]{0,1:T(2,128)S(1)}, s32[985,2]{0,1:T(2,128)}, u32[]{:S(2)}) copy-start(s32[985,2]{0,1:T(2,128)} %param.13) | copy-start | bytes 23644
  12.8 383.6 %all-gather.6.cloned.1.call-start = ((), (), s32[]{:S(2)}) async-start(), calls=%async_computation.10 | async-start | bytes 35651584 | tf_op jit(solution)/shard_map/all_gather | solution.py:78
  16.7 36.2 %copy-start.12 = (bf16[985,512]{1,0:T(8,128)(2,1)S(1)}, bf16[985,512]{1,0:T(8,128)(2,1)}, u32[]{:S(2)}) copy-start(bf16[985,512]{1,0:T(8,128)(2,1)} %param.23) | copy-start | bytes 3025924
  41.7 69.0 %copy-start.46 = (f32[512]{0:T(512)}, f32[512]{0:T(512)S(1)}, u32[]{:S(2)}) copy-start(f32[512]{0:T(512)S(1)} %convert_element_type.196) | copy-start | bytes 6148
  41.7 69.0 %copy-start.43 = (f32[512]{0:T(512)}, f32[512]{0:T(512)S(1)}, u32[]{:S(2)}) copy-start(f32[512]{0:T(512)S(1)} %convert_element_type.194) | copy-start | bytes 6148
  41.8 120.7 %copy-start.38 = (f32[512]{0:T(512)}, f32[512]{0:T(512)S(1)}, u32[]{:S(2)}) copy-start(f32[512]{0:T(512)S(1)} %convert_element_type.206) | copy-start | bytes 6148
  55.9 6.2 copy-start.42
  55.9 33.2 %copy-start.7 = (bf16[985,512]{1,0:T(8,128)(2,1)S(1)}, bf16[985,512]{1,0:T(8,128)(2,1)}, u32[]{:S(2)}) copy-start(bf16[985,512]{1,0:T(8,128)(2,1)} %param.12) | copy-start | bytes 3025924
  89.0 74.7 %copy-start.22 = (bf16[512,32]{1,0:T(8,128)(2,1)}, bf16[512,32]{1,0:T(8,128)(2,1)S(1)}, u32[]{:S(2)}) copy-start(bf16[512,32]{1,0:T(8,128)(2,1)S(1)} %all_gather.35) | copy-start | bytes 98308
  89.3 26.5 %copy-start.34 = (f32[985]{0:T(1024)}, f32[985]{0:T(1024)S(1)}, u32[]{:S(2)}) copy-start(f32[985]{0:T(1024)S(1)} %broadcast_multiply_fusion.6) | copy-start | bytes 11824
  89.8 26.0 %copy-start.40 = (f32[985]{0:T(1024)}, f32[985]{0:T(1024)S(1)}, u32[]{:S(2)}) copy-start(f32[985]{0:T(1024)S(1)} %add_rsqrt_fusion.1) | copy-start | bytes 11824
  110.6 50.6 %copy-start.15 = (bf16[512,512]{1,0:T(8,128)(2,1)}, bf16[512,512]{1,0:T(8,128)(2,1)S(1)}, u32[]{:S(2)}) copy-start(bf16[512,512]{1,0:T(8,128)(2,1)S(1)} %all_gather.32) | copy-start | bytes 1572868
  110.7 82.7 %copy-start.36 = (s32[1970,1]{0,1:T(1,128)}, s32[1970,1]{0,1:T(1,128)S(1)}, u32[]{:S(2)}) copy-start(s32[1970,1]{0,1:T(1,128)S(1)} %compare_select_fusion) | copy-start | bytes 23644
  137.2 7.0 copy-start.5
  144.3 10.1 copy-start.20
  151.0 3.2 copy-start.2
  151.1 3.3 copy-start.24
  161.2 1.2 copy-start.11
  162.0 1.3 copy-start
  162.0 1.3 copy-start.28
  163.3 0.9 copy-start.32
  163.7 26.6 %copy-start.10 = (bf16[985,512]{1,0:T(8,128)(2,1)}, bf16[985,512]{1,0:T(8,128)(2,1)S(1)}, u32[]{:S(2)}) copy-start(bf16[985,512]{1,0:T(8,128)(2,1)S(1)} %add_convert_fusion.1) | copy-start | bytes 3025924
  165.1 19.6 %copy-start.17 = (f32[985,2]{1,0:T(8,128)}, f32[985,2]{1,0:T(8,128)S(1)}, u32[]{:S(2)}) copy-start(f32[985,2]{1,0:T(8,128)S(1)} %copy.116) | copy-start | bytes 23644
  184.6 53.1 %all-to-all-start.2 = ((bf16[32,128,512]{2,1,0:T(8,128)(2,1)}), bf16[32,128,512]{2,1,0:T(8,128)(2,1)}, u32[]{:S(2)}, u32[]{:S(2)}) async-start(bf16[32,128,512]{2,1,0:T(8,128)(2,1)} %bitcast.107), calls=%async_computation.2 | async-start | bytes 8388608 | tf_op jit(solution)/shard_map/all_to_all | solution.py:152
  237.8 52.4 %all-to-all-start = ((bf16[32,128,512]{2,1,0:T(8,128)(2,1)}), bf16[32,128,512]{2,1,0:T(8,128)(2,1)}, u32[]{:S(2)}, u32[]{:S(2)}) async-start(bf16[32,128,512]{2,1,0:T(8,128)(2,1)} %bitcast.108), calls=%async_computation | async-start | bytes 8388608 | tf_op jit(solution)/shard_map/all_to_all | solution.py:130
  470.2 53.0 %all-to-all-start.3 = ((bf16[16,256,512]{2,0,1:T(8,128)(2,1)}), bf16[16,256,512]{2,0,1:T(8,128)(2,1)}, u32[]{:S(2)}, u32[]{:S(2)}) async-start(bf16[16,256,512]{2,0,1:T(8,128)(2,1)} %copy.126), calls=%async_computation.3 | async-start | bytes 8388608 | tf_op jit(solution)/shard_map/all_to_all | solution.py:169
  510.2 18.7 %copy-start.13 = (bf16[985,512]{1,0:T(8,128)(2,1)S(1)}, bf16[985,512]{1,0:T(8,128)(2,1)}, u32[]{:S(2)}) copy-start(bf16[985,512]{1,0:T(8,128)(2,1)} %param.23) | copy-start | bytes 3025924
  510.2 18.9 %copy-start.37 = (s32[1970,1]{0,1:T(1,128)S(1)}, s32[1970,1]{0,1:T(1,128)}, u32[]{:S(2)}) copy-start(s32[1970,1]{0,1:T(1,128)} %copy-done.36) | copy-start | bytes 23644
  523.2 51.9 %all-to-all-start.1 = ((bf16[16,256,512]{2,0,1:T(8,128)(2,1)}), bf16[16,256,512]{2,0,1:T(8,128)(2,1)}, u32[]{:S(2)}, u32[]{:S(2)}) async-start(bf16[16,256,512]{2,0,1:T(8,128)(2,1)} %copy.122), calls=%async_computation.1 | async-start | bytes 8388608 | tf_op jit(solution)/shard_map/all_to_all | solution.py:138
  528.8 205.2 %reduce-scatter.10.cloned.1.call-start = ((), (), s32[]{:S(2)}) async-start(), calls=%async_computation.14 | async-start | bytes 1671168 | tf_op jit(solution)/shard_map/reduce_scatter | solution.py:255
  593.5 5.5 copy-start.18
  613.0 12.3 copy-start.1
  613.0 12.3 copy-start.23
  613.0 12.3 copy-start.29
  613.0 12.3 copy-start.33
  613.0 12.3 copy-start.39
  625.3 2.9 copy-start.14
  628.2 3.1 copy-start.16
  630.0 1.3 copy-start.3
  632.0 3.2 copy-start.25
  635.2 5.0 copy-start.21
  635.2 10.2 slice-start
  640.2 5.2 slice-start.1
  645.4 2.1 copy-start.9
  647.5 1.4 copy-start.6
  661.4 9.0 copy-start.8
  661.4 9.0 copy-start.35
  661.5 9.0 copy-start.41
  661.5 9.0 copy-start.44
  661.5 9.0 copy-start.47
  670.5 7.7 copy-start.4
  675.7 138.1 %reduce-scatter.14.cloned.1.call-start = ((), (), s32[]{:S(2)}) async-start(), calls=%async_computation.17 | async-start | bytes 139264 | tf_op jit(solution)/shard_map/reduce_scatter | solution.py:267
  678.1 173.0 %reduce-scatter.12.cloned.1.call-start = ((), (), s32[]{:S(2)}) async-start(), calls=%async_computation.16 | async-start | bytes 557056 | tf_op jit(solution)/shard_map/reduce_scatter | solution.py:258
  681.0 194.1 %all-reduce.14.cloned.1.call-start = ((), (), s32[]{:S(2)}) async-start(), calls=%async_computation.15 | async-start | bytes 196608 | tf_op jit(solution)/shard_map/psum | solution.py:242
  734.0 476.6 %reduce-scatter.6.cloned.1.call-start = ((), (), s32[]{:S(2)}) async-start(), calls=%async_computation.12 | async-start | bytes 35651584 | tf_op jit(solution)/shard_map/reduce_scatter | solution.py:174
  754.5 792.1 %reduce-scatter.8.cloned.1.call-start = ((), (), s32[]{:S(2)}) async-start(), calls=%async_computation.13 | async-start | bytes 35651584 | tf_op jit(solution)/shard_map/reduce_scatter | solution.py:177
  (3 other events, 1.9 us)
Sparse Core Ops, SparseCore 0:
  10.9 39.2 all-gather.3
  51.7 172.3 all-gather.7
  225.7 170.6 all-gather.5
  675.8 58.1 reduce-scatter.9
  738.3 54.1 reduce-scatter.13
  796.3 54.7 reduce-scatter.11
  853.4 21.6 all-reduce.13
  879.3 331.2 reduce-scatter.5
  1214.9 331.7 reduce-scatter.7
where the time goes:
time: 1570 us; the launch traced here: 1560 us
  waiting for transfers between devices  954 us (61%)
  matrix products  209 us (13%)
  local copies, waits for them, and re-layouts  161 us (10%)
  blocking collectives  99.6 us (6%)
  other arithmetic  94.2 us (6%)
  starting transfers between devices  23.2 us (1%)
  between operations  16.6 us (1%)
    reduce_scatter x1, waiting for transfers between devices, body(): lax.psum_scatter(grad_first.astype(jnp.bfloat16), 'dp', scatter_dimension...  334 us
    reduce_scatter x1, waiting for transfers between devices, body(): lax.psum_scatter(grad_second.astype(jnp.bfloat16), 'dp', scatter_dimensio...  332 us
    all_gather x1, waiting for transfers between devices, body(): lax.all_gather(w_expert_in.astype(low_type), 'dp', axis=1, tiled=True)  76.7 us
    reduce_scatter x1, waiting for transfers between devices, body(): lax.psum_scatter(summed[2].astype(jnp.bfloat16), 'dp', scatter_dimension=...  53 us
    dot_general x1, matrix products, body(): jnp.einsum('erd,edf->erf', received, expert_first, preferred_element_type...  46.7 us
    unnamed x2, blocking collectives  45 us
    all_to_all x1, waiting for transfers between devices, body(): lax.all_to_all(outgoing, 'expert', split_axis=0, concat_axis=1, tiled=True)  41.9 us
    reduce_scatter x1, waiting for transfers between devices, body(): lax.psum_scatter(summed[3].astype(jnp.bfloat16), 'dp', scatter_dimension=...  37.3 us
  transfers between devices with their start and end apart: 13, of which 10 were waited for; matrix products, arithmetic and copies ran while one was open for 18% of the time, Pallas kernels for 0%

commit v1 on v0

--- a/solution.py
+++ b/solution.py
@@ -1,6 +1,7 @@
 import jax
 import jax.numpy as jnp
 from jax import lax
+from jax.sharding import Mesh
 from jax.sharding import PartitionSpec as P
 
 D = 512
@@ -59,13 +60,13 @@
     low_type = jnp.bfloat16
     full_type = jnp.float32
     gathered = (
-        lax.all_gather(ln1_gain.astype(low_type), "dp", axis=0, tiled=True),
-        lax.all_gather(ln1_bias.astype(low_type), "dp", axis=0, tiled=True),
-        lax.all_gather(w_qkv.astype(low_type), "dp", axis=0, tiled=True),
-        lax.all_gather(w_proj.astype(low_type), "dp", axis=0, tiled=True),
-        lax.all_gather(ln2_gain.astype(low_type), "dp", axis=0, tiled=True),
-        lax.all_gather(ln2_bias.astype(low_type), "dp", axis=0, tiled=True),
-        lax.all_gather(w_router.astype(low_type), "dp", axis=0, tiled=True),
+        lax.all_gather(ln1_gain.astype(low_type), ("replica", "part"), axis=0, tiled=True),
+        lax.all_gather(ln1_bias.astype(low_type), ("replica", "part"), axis=0, tiled=True),
+        lax.all_gather(w_qkv.astype(low_type), ("replica", "part"), axis=0, tiled=True),
+        lax.all_gather(w_proj.astype(low_type), ("replica", "part"), axis=0, tiled=True),
+        lax.all_gather(ln2_gain.astype(low_type), ("replica", "part"), axis=0, tiled=True),
+        lax.all_gather(ln2_bias.astype(low_type), ("replica", "part"), axis=0, tiled=True),
+        lax.all_gather(w_router.astype(low_type), ("replica", "part"), axis=0, tiled=True),
     )
     gain_one = gathered[0].astype(full_type)
     bias_one = gathered[1].astype(full_type)
@@ -74,10 +75,41 @@
     gain_two = gathered[4].astype(full_type)
     bias_two = gathered[5].astype(full_type)
     router_weight = gathered[6]
-    expert_first, expert_second = (
-        lax.all_gather(w_expert_in.astype(low_type), "dp", axis=1, tiled=True),
-        lax.all_gather(w_expert_out.astype(low_type), "dp", axis=1, tiled=True),
-    )
+    replicas, parts, groups = (lax.axis_size(name) for name in ("replica", "part", "expert"))
+    own = w_expert_in.shape[0] // parts
+
+    def spread(master):
+        pieces = master.astype(low_type).reshape(parts, own, *master.shape[1:])
+        pieces = jnp.concatenate([pieces] * replicas, axis=0)
+        pieces = lax.all_to_all(pieces, ("replica", "part"), split_axis=0, concat_axis=0, tiled=True)
+        return pieces.transpose(1, 0, 2, 3).reshape(own, -1, master.shape[2])
+
+    def collect(grad):
+        pieces = grad.astype(low_type).reshape(own, replicas * parts, -1, grad.shape[2])
+        pieces = lax.all_to_all(
+            pieces.transpose(1, 0, 2, 3),
+            ("replica", "part"),
+            split_axis=0,
+            concat_axis=0,
+            tiled=True,
+        )
+        pieces = pieces.reshape(replicas, parts * own, -1, grad.shape[2])
+        return jnp.sum(pieces.astype(full_type), axis=0)
+
+    def to_experts(rows):
+        rows = rows.reshape(parts * groups, own * CAP, D)
+        rows = lax.all_to_all(rows, ("part", "expert"), split_axis=0, concat_axis=0, tiled=True)
+        rows = rows.reshape(parts * groups, own, CAP, D).transpose(1, 0, 2, 3)
+        return rows.reshape(own, parts * groups * CAP, D)
+
+    def to_tokens(rows):
+        rows = rows.reshape(own, parts * groups, CAP, D).transpose(1, 0, 2, 3)
+        rows = rows.reshape(parts * groups, own * CAP, D)
+        rows = lax.all_to_all(rows, ("part", "expert"), split_axis=0, concat_axis=0, tiled=True)
+        return rows.reshape(EXPERTS * CAP, D)
+
+    expert_first = spread(w_expert_in)
+    expert_second = spread(w_expert_out)
     images = tokens.shape[0] // SEQ
     head_size = D // HEADS
     qk_factor = head_size ** (-0.5)
@@ -119,15 +151,18 @@
     flat_picks = pick_table.astype(jnp.int32).reshape(-1, EXPERTS)
     running = jnp.cumsum(flat_picks, axis=0)
     slot_index = jnp.sum((running - 1) * flat_picks, axis=-1)
-    destination = choices.reshape(-1) * CAP + slot_index
+    flat_choices = choices.reshape(-1)
+    group = flat_choices // (parts * own)
+    inside = flat_choices % (parts * own)
+    place = ((inside // own) * groups + group) * own + inside % own
+    destination = place * CAP + slot_index
     repeated = jnp.repeat(router_in, 2, axis=0)
     outgoing = (
         jnp.zeros((EXPERTS * CAP, D), low_type)
         .at[destination]
         .set(repeated)
-        .reshape(EXPERTS, CAP, D)
-    )
-    received = lax.all_to_all(outgoing, "expert", split_axis=0, concat_axis=1, tiled=True)
+    )
+    received = to_experts(outgoing)
     inner_rows = jnp.einsum(
         "erd,edf->erf", received, expert_first, preferred_element_type=full_type
     )
@@ -135,9 +170,7 @@
     returned = jnp.einsum(
         "erf,efd->erd", hidden, expert_second, preferred_element_type=full_type
     ).astype(low_type)
-    combined = lax.all_to_all(returned, "expert", split_axis=1, concat_axis=0, tiled=True).reshape(
-        EXPERTS * CAP, D
-    )
+    combined = to_tokens(returned)
     picked = combined[destination].reshape(-1, 2, D).astype(full_type)
     output = resid + jnp.sum(gate_values[:, :, None] * picked, axis=1)
     upstream = cotangent.astype(full_type)
@@ -147,15 +180,10 @@
         jnp.zeros((EXPERTS * CAP, D), low_type)
         .at[destination]
         .set(grad_picked)
-        .reshape(EXPERTS, CAP, D)
-    )
-    grad_returned = lax.all_to_all(grad_outgoing, "expert", split_axis=0, concat_axis=1, tiled=True)
-    back_first, back_second = (
-        lax.all_gather(w_expert_in.astype(low_type), "dp", axis=1, tiled=True),
-        lax.all_gather(w_expert_out.astype(low_type), "dp", axis=1, tiled=True),
-    )
+    )
+    grad_returned = to_experts(grad_outgoing)
     grad_hidden = jnp.einsum(
-        "erd,efd->erf", grad_returned, back_second, preferred_element_type=full_type
+        "erd,efd->erf", grad_returned, expert_second, preferred_element_type=full_type
     )
     gelu_value, gelu_pull = jax.vjp(jax.nn.gelu, inner_rows)
     grad_inner = gelu_pull(grad_hidden)[0].astype(low_type)
@@ -164,20 +192,11 @@
     )
     grad_first = jnp.einsum("erd,erf->edf", received, grad_inner, preferred_element_type=full_type)
     grad_received = jnp.einsum(
-        "erf,edf->erd", grad_inner, back_first, preferred_element_type=full_type
+        "erf,edf->erd", grad_inner, expert_first, preferred_element_type=full_type
     ).astype(low_type)
-    grad_back = lax.all_to_all(
-        grad_received, "expert", split_axis=1, concat_axis=0, tiled=True
-    ).reshape(EXPERTS * CAP, D)
+    grad_back = to_tokens(grad_received)
     grad_router_in = jnp.sum(grad_back[destination].reshape(-1, 2, D).astype(full_type), axis=1)
-    expert_in_grad, expert_out_grad = (
-        lax.psum_scatter(
-            grad_first.astype(jnp.bfloat16), "dp", scatter_dimension=1, tiled=True
-        ).astype(jnp.float32),
-        lax.psum_scatter(
-            grad_second.astype(jnp.bfloat16), "dp", scatter_dimension=1, tiled=True
-        ).astype(jnp.float32),
-    )
+    expert_in_grad, expert_out_grad = (collect(grad_first), collect(grad_second))
     grad_probs = jnp.sum(grad_gates[:, :, None] * pick_float, axis=1)
     grad_logits = (
         router_probs * (grad_probs - jnp.sum(router_probs * grad_probs, axis=-1, keepdims=True))
@@ -247,25 +266,25 @@
     )
     shares = (
         lax.psum_scatter(
-            summed[0].astype(jnp.bfloat16), "dp", scatter_dimension=0, tiled=True
-        ).astype(jnp.float32),
-        lax.psum_scatter(
-            summed[1].astype(jnp.bfloat16), "dp", scatter_dimension=0, tiled=True
-        ).astype(jnp.float32),
-        lax.psum_scatter(
-            summed[2].astype(jnp.bfloat16), "dp", scatter_dimension=0, tiled=True
-        ).astype(jnp.float32),
-        lax.psum_scatter(
-            summed[3].astype(jnp.bfloat16), "dp", scatter_dimension=0, tiled=True
-        ).astype(jnp.float32),
-        lax.psum_scatter(
-            summed[4].astype(jnp.bfloat16), "dp", scatter_dimension=0, tiled=True
-        ).astype(jnp.float32),
-        lax.psum_scatter(
-            summed[5].astype(jnp.bfloat16), "dp", scatter_dimension=0, tiled=True
-        ).astype(jnp.float32),
-        lax.psum_scatter(
-            summed[6].astype(jnp.bfloat16), "dp", scatter_dimension=0, tiled=True
+            summed[0].astype(jnp.bfloat16), ("replica", "part"), scatter_dimension=0, tiled=True
+        ).astype(jnp.float32),
+        lax.psum_scatter(
+            summed[1].astype(jnp.bfloat16), ("replica", "part"), scatter_dimension=0, tiled=True
+        ).astype(jnp.float32),
+        lax.psum_scatter(
+            summed[2].astype(jnp.bfloat16), ("replica", "part"), scatter_dimension=0, tiled=True
+        ).astype(jnp.float32),
+        lax.psum_scatter(
+            summed[3].astype(jnp.bfloat16), ("replica", "part"), scatter_dimension=0, tiled=True
+        ).astype(jnp.float32),
+        lax.psum_scatter(
+            summed[4].astype(jnp.bfloat16), ("replica", "part"), scatter_dimension=0, tiled=True
+        ).astype(jnp.float32),
+        lax.psum_scatter(
+            summed[5].astype(jnp.bfloat16), ("replica", "part"), scatter_dimension=0, tiled=True
+        ).astype(jnp.float32),
+        lax.psum_scatter(
+            summed[6].astype(jnp.bfloat16), ("replica", "part"), scatter_dimension=0, tiled=True
         ).astype(jnp.float32),
     )
     return (
@@ -284,36 +303,39 @@
 
 
 def solution(mesh):
+    dp, groups = mesh.shape["dp"], mesh.shape["expert"]
+    parts = min(EXPERTS // groups, dp // 2)
+    mesh = Mesh(mesh.devices.reshape(dp // parts, parts, groups), ("replica", "part", "expert"))
     placed = (
-        P(("dp", "expert"), None),
-        P(("dp", "expert"), None),
-        P("dp"),
-        P("dp"),
-        P("dp", None),
-        P("dp", None),
-        P("dp"),
-        P("dp"),
-        P("dp", None),
-        P("expert", "dp", None),
-        P("expert", "dp", None),
-        P(("dp", "expert"), None),
+        P(("replica", "part", "expert"), None),
+        P(("replica", "part", "expert"), None),
+        P(("replica", "part")),
+        P(("replica", "part")),
+        P(("replica", "part"), None),
+        P(("replica", "part"), None),
+        P(("replica", "part")),
+        P(("replica", "part")),
+        P(("replica", "part"), None),
+        P("expert", ("replica", "part"), None),
+        P("expert", ("replica", "part"), None),
+        P(("replica", "part", "expert"), None),
     )
     return jax.shard_map(
         body,
         mesh=mesh,
         in_specs=placed,
         out_specs=(
-            P(("dp", "expert"), None),
-            P(("dp", "expert"), None),
-            P("dp"),
-            P("dp"),
-            P("dp", None),
-            P("dp", None),
-            P("dp"),
-            P("dp"),
-            P("dp", None),
-            P("expert", "dp", None),
-            P("expert", "dp", None),
+            P(("replica", "part", "expert"), None),
+            P(("replica", "part", "expert"), None),
+            P(("replica", "part")),
+            P(("replica", "part")),
+            P(("replica", "part"), None),
+            P(("replica", "part"), None),
+            P(("replica", "part")),
+            P(("replica", "part")),
+            P(("replica", "part"), None),
+            P("expert", ("replica", "part"), None),
+            P("expert", ("replica", "part"), None),
         ),
         check_vma=False,
     )

time: 1570 us -> 1020 us (0.65)
  waiting for transfers between devices: 954 us -> 367 us
  blocking collectives: 99.6 us -> 170 us
  matrix products: 209 us -> 158 us
  starting transfers between devices: 23.2 us -> 44.5 us
    reduce_scatter x5 -> x3, waiting for transfers between devices: 756 us -> 134 us  [the longest x1 59 us: body(): lax.psum_scatter(summed[3].astype(jnp.bfloat16), ('replica', 'part'), sca...]
    all_to_all x4 -> x8, waiting for transfers between devices: 107 us -> 220 us  [the longest x2 96.3 us: spread(): lax.all_to_all(pieces, ('replica', 'part'), split_axis=0, concat_axis=0,...]
    unnamed x2, blocking collectives: 45 us -> 128 us
    all_gather x3 -> x1, waiting for transfers between devices: 76.8 us -> 0.02 us  [body(): lax.all_gather(w_qkv.astype(low_type), ('replica', 'part'), axis=0, tiled...]
    all_to_all x4 -> x0, local copies, waits for them, and re-layouts: 22.3 us -> none  [the longest x1 6.51 us: body(): lax.all_to_all(grad_received, 'expert', split_axis=1, concat_axis=0, tile...]
    all_to_all x4 -> x8, starting transfers between devices: 22.8 us -> 44.1 us  [the longest x2 12.9 us: to_experts(): lax.all_to_all(rows, ('part', 'expert'), split_axis=0, concat_axis=0, til...]
    dot_general x1, matrix products: 46.7 us -> 25.5 us  [body(): jnp.einsum('erd,edf->erf', received, expert_first, preferred_element_type...]
    transpose x0 -> x4, local copies, waits for them, and re-layouts: none -> 18.6 us  [the longest x2 9.35 us: spread(): return pieces.transpose(1, 0, 2, 3).reshape(own, -1, master.shape[2])]
  transfers between devices with their start and end apart: 13 -> 13, of which waited for: 10 -> 9; matrix products, arithmetic and copies ran while one was open for 18% -> 35% of each run, Pallas kernels for 0% -> 0%
where the time goes in v1:
time: 1020 us; the launch traced here: 1010 us
  waiting for transfers between devices  367 us (36%)
  blocking collectives  170 us (17%)
  matrix products  158 us (15%)
  local copies, waits for them, and re-layouts  152 us (15%)
  other arithmetic  99 us (10%)
  starting transfers between devices  44.5 us (4%)
  between operations  16.4 us (2%)
    unnamed x2, blocking collectives  128 us
    all_to_all x2, waiting for transfers between devices, spread(): lax.all_to_all(pieces, ('replica', 'part'), split_axis=0, concat_axis=0,...  96.3 us
    all_to_all x2, waiting for transfers between devices, to_experts(): lax.all_to_all(rows, ('part', 'expert'), split_axis=0, concat_axis=0, til...  79.5 us
    reduce_scatter x1, waiting for transfers between devices, body(): lax.psum_scatter(summed[3].astype(jnp.bfloat16), ('replica', 'part'), sca...  59 us
    reduce_scatter x1, waiting for transfers between devices, body(): lax.psum_scatter(summed[2].astype(jnp.bfloat16), ('replica', 'part'), sca...  44.9 us
    all_to_all x2, waiting for transfers between devices, to_tokens(): lax.all_to_all(rows, ('part', 'expert'), split_axis=0, concat_axis=0, til...  43.7 us
    dot_general x1, matrix products, body(): jnp.einsum('erd,efd->erf', grad_returned, expert_second, preferred_elemen...  35.1 us
    reduce_scatter x1, waiting for transfers between devices, body(): lax.psum_scatter(summed[6].astype(jnp.bfloat16), ('replica', 'part'), sca...  30.5 us
  transfers between devices with their start and end apart: 13, of which 9 were waited for; matrix products, arithmetic and copies ran while one was open for 35% of the time, Pallas kernels for 0%

profile of v1, /device:TPU:13, one launch (start us, length us, event | category | flops | bytes accessed | tf_op | source)
XLA Modules:
  0.0 1007.1 jit_solution(8675111675032054777)
XLA Ops:
  12.1 6.7 all-to-all-start.1
  24.4 96.3 %all-to-all-done.1 = bf16[16,2,32,2048]{3,2,1,0:T(8,128)(2,1)} async-done(((bf16[16,2,32,2048]{3,2,1,0:T(8,128)(2,1)}), bf16[16,2,32,2048]{3,2,1,0:T(8,128)(2,1)}, u32[]{:S(2)}, u32[]{:S(2)}) %all-to-all-start.1) | async-done | bytes 4194336 | tf_op jit(solution)/shard_map/all_to_all | solution.py:84
  120.7 4.9 all-to-all-start.2
  128.7 106.0 %all-reduce.10 = (bf16[512]{0:T(512)(128)(2,1)S(1)}, bf16[512]{0:T(512)(128)(2,1)S(1)}, bf16[512]{0:T(512)(128)(2,1)S(1)}, bf16[512]{0:T(512)(128)(2,1)S(1)}) all-reduce(bf16[512]{0:T(512)(128)(2,1)S(1)} %dynamic-update-slice.1, ...), channel_id=1, replica_groups=mesh['replica'=2,'part'=8,'expert'=2] {'replica','part'}, use_global_device_ids=true, to_apply=%add.2 | all-reduce | flops 2048 | bytes 8192
  234.9 9.1 reduce-window.6
  244.8 3.0 mul.279
  247.8 6.0 mul.280
  253.8 16.4 %all_gather.27 = bf16[512,32]{1,0:T(8,128)(2,1)S(1)} all-gather(bf16[32,32]{1,0:T(8,128)(2,1)S(1)} %convert_element_type.214), channel_id=1, replica_groups=mesh['replica'=2,'part'=8,'expert'=2] {'replica','part'}, dimensions={0}, use_global_device_ids=true | all-gather | bytes 34816 | tf_op jit(solution)/shard_map/all_gather | solution.py:69
  271.1 18.2 %all_gather.24 = bf16[512,512]{1,0:T(8,128)(2,1)S(1)} all-gather(bf16[32,512]{1,0:T(8,128)(2,1)S(1)} %convert_element_type.208), channel_id=1, replica_groups=mesh['replica'=2,'part'=8,'expert'=2] {'replica','part'}, dimensions={0}, use_global_device_ids=true | all-gather | bytes 557056 | tf_op jit(solution)/shard_map/all_gather | solution.py:66
  289.5 4.9 convolution_convert_fusion.4
  294.4 8.7 reshape.376
  303.1 5.5 fusion.67
  308.7 3.9 copy.159
  312.6 3.1 copy.160
  315.7 4.4 copy.158
  322.8 6.7 fusion.69
  329.5 3.1 copy-done.2
  333.8 2.7 copy.127
  336.4 3.1 convert_element_type.207
  343.7 19.2 %scatter_custom_fusion.1 = bf16[4096,512]{1,0:T(8,128)(2,1)} fusion(s32[1970]{0:T(1024)S(1)} %bitcast.150, bf16[]{:T(256)} %constant.81.clone.1, f32[1970,512]{1,0:T(8,128)} %mul.280, f32[1970]{0:T(1024)S(1)} %mul.277), kind=kCustom, calls=%fused_computation.49 | custom fusion | flops 2017280 | bytes 8237058 | tf_op jit(solution)/shard_map/scatter | solution.py:182
  363.0 8.3 all-to-all-start.4
  374.4 13.6 %scatter_custom_fusion = bf16[4096,512]{1,0:T(8,128)(2,1)} fusion(s32[1970]{0:T(1024)S(1)} %bitcast.151, bf16[1970,512]{1,0:T(8,128)(2,1)} %reshape.425, bf16[]{:T(256)} %constant.81.clone.1), kind=kCustom, calls=%fused_computation.51 | custom fusion | bytes 4194816 | tf_op jit(solution)/shard_map/scatter | solution.py:163
  388.0 38.6 %all-to-all-done.4 = bf16[16,256,512]{2,1,0:T(8,128)(2,1)} async-done(((bf16[16,256,512]{2,1,0:T(8,128)(2,1)}), bf16[16,256,512]{2,1,0:T(8,128)(2,1)}, u32[]{:S(2)}, u32[]{:S(2)}) %all-to-all-start.4) | async-done | bytes 4194336 | tf_op jit(solution)/shard_map/all_to_all | solution.py:101
  426.6 4.6 all-to-all-start
  431.2 4.8 copy.134
  436.0 4.6 copy.135
  440.6 4.6 copy.138
  445.2 40.9 %all-to-all-done = bf16[16,256,512]{2,1,0:T(8,128)(2,1)} async-done(((bf16[16,256,512]{2,1,0:T(8,128)(2,1)}), bf16[16,256,512]{2,1,0:T(8,128)(2,1)}, u32[]{:S(2)}, u32[]{:S(2)}) %all-to-all-start) | async-done | bytes 4194336 | tf_op jit(solution)/shard_map/all_to_all | solution.py:101
  486.0 4.6 copy.133
  490.7 25.5 %multiply_convert_fusion = (bf16[2,2048,2048]{2,1,0:T(8,128)(2,1)}, f32[2,2048,2048]{2,1,0:T(8,128)}) fusion(bf16[2,2048,512]{2,1,0:T(8,128)(2,1)} %bitcast.132, bf16[2,512,2048]{2,1,0:T(8,128)(2,1)} %bitcast.136), kind=kOutput, calls=%fused_computation.14 | convolution fusion | flops 8665432064 | bytes 58720256 | tf_op jit(solution)/shard_map/erd,edf->erf/dot_general | solution.py:166
  516.2 13.6 %convolution_convert_fusion.1 = bf16[2,2048,512]{2,1,0:T(8,128)(2,1)S(1)} fusion(bf16[2,2048,2048]{2,1,0:T(8,128)(2,1)} %get-tuple-element.48, bf16[2,2048,512]{2,1,0:T(8,128)(2,1)} %bitcast.138), kind=kOutput, calls=%fused_computation.33 | convolution fusion | flops 8592031744 | bytes 25165824 | tf_op jit(solution)/shard_map/erf,efd->erd/dot_general | solution.py:170
  532.0 4.8 all-to-all-start.3
  536.8 35.1 %fusion.7 = bf16[2,2048,2048]{2,1,0:T(8,128)(2,1)} fusion(f32[2,2048,2048]{2,1,0:T(8,128)} %get-tuple-element.49, bf16[2,2048,512]{2,1,0:T(8,128)(2,1)} %bitcast.134, bf16[2,2048,512]{2,1,0:T(8,128)(2,1)} %bitcast.139), kind=kOutput, calls=%fused_computation.13 | convolution fusion | flops 8757706752 | bytes 58720256 | tf_op jit(solution)/shard_map/erd,efd->erf/dot_general | solution.py:185
  571.9 12.7 %convolution_convert_fusion = bf16[2,2048,512]{2,1,0:T(8,128)(2,1)S(1)} fusion(bf16[2,2048,2048]{2,1,0:T(8,128)(2,1)} %fusion.7, bf16[2,512,2048]{2,1,0:T(8,128)(2,1)S(1)} %bitcast.137), kind=kOutput, calls=%fused_computation.32 | convolution fusion | flops 8592031744 | bytes 25165824 | tf_op jit(solution)/shard_map/erf,edf->erd/dot_general | solution.py:194
  586.9 4.7 all-to-all-done.3
  591.7 4.6 all-to-all-start.5
  596.3 13.7 %convolution_convert_fusion.2 = bf16[2,2048,512]{2,1,0:T(8,128)(2,1)S(1)} fusion(bf16[2,2048,2048]{2,1,0:T(8,128)(2,1)} %get-tuple-element.48, bf16[2,2048,512]{2,1,0:T(8,128)(2,1)} %bitcast.135), kind=kOutput, calls=%fused_computation.34 | convolution fusion | flops 8592031744 | bytes 25165824 | tf_op jit(solution)/shard_map/erf,erd->efd/dot_general | solution.py:190
  612.2 38.9 %all-to-all-done.5 = bf16[16,256,512]{2,1,0:T(8,128)(2,1)} async-done(((bf16[16,256,512]{2,1,0:T(8,128)(2,1)}), bf16[16,256,512]{2,1,0:T(8,128)(2,1)}, u32[]{:S(2)}, u32[]{:S(2)}) %all-to-all-start.5) | async-done | bytes 4194336 | tf_op jit(solution)/shard_map/all_to_all | solution.py:108
  651.1 4.6 all-to-all-start.7
  656.0 13.7 %convolution_convert_fusion.3 = bf16[2,512,2048]{2,1,0:T(8,128)(2,1)S(1)} fusion(bf16[2,2048,512]{2,1,0:T(8,128)(2,1)} %bitcast.133, bf16[2,2048,2048]{2,1,0:T(8,128)(2,1)} %fusion.7), kind=kOutput, calls=%fused_computation.35 | convolution fusion | flops 8592031744 | bytes 25165824 | tf_op jit(solution)/shard_map/erd,erf->edf/dot_general | solution.py:193
  672.4 11.9 %gather_fusion = bf16[1970,512]{1,0:T(8,128)(2,1)} fusion(bf16[4096,512]{1,0:T(8,128)(2,1)} %bitcast.23, s32[2048]{0:T(1024)S(1)} %pad_clamp_fusion), kind=kCustom, calls=%fused_computation | custom fusion | bytes 4042440 | tf_op jit(solution)/shard_map/gather | solution.py:174
  684.3 5.5 reshape.401
  689.8 13.8 %multiply_reduce_fusion.2 = (f32[985,2]{1,0:T(8,128)}, f32[985,512]{1,0:T(8,128)}) fusion(f32[985,2,512]{2,1,0:T(2,128)} %reshape.401, f32[985,512]{1,0:T(8,128)S(1)} %convert_element_type.222, f32[985,2]{1,0:T(8,128)S(1)} %copy-done.18), kind=kLoop, calls=%fused_computation.29 | loop fusion | flops 3528270 | bytes 8084880 | tf_op jit(solution)/shard_map/reduce_sum | solution.py:177
  704.9 11.9 %gather_fusion.1 = bf16[1970,512]{1,0:T(8,128)(2,1)S(1)} fusion(bf16[4096,512]{1,0:T(8,128)(2,1)} %bitcast.31, s32[2048]{0:T(1024)} %copy-done.32), kind=kCustom, calls=%fused_computation.1 | custom fusion | bytes 4042440 | tf_op jit(solution)/shard_map/gather | solution.py:198
  716.7 4.8 reshape.402
  721.6 8.4 reduce_sum.232
  730.2 2.9 multiply_reduce_fusion.4
  740.3 8.5 multiply_reduce_fusion
  748.7 5.5 all-to-all-start.6
  754.3 6.7 multiply_convert_fusion.1
  763.8 4.8 fusion.41
  771.0 9.1 copy.146
  780.1 9.0 convert_element_type.232
  789.2 5.1 convolution_convert_fusion.5
  797.5 2.8 convolution_convert_fusion.7
  800.5 4.7 fusion.32
  805.2 5.5 convert_reduce_fusion
  812.6 44.9 %reduce-scatter.4.cloned.1.call-done = bf16[32,1536]{1,0:T(8,128)(2,1)} async-done(((bf16[512,1536]{1,0:T(8,128)(2,1)}), bf16[32,1536]{1,0:T(8,128)(2,1)}) %reduce-scatter.4.cloned.1.call-update) | async-done | bytes 98320 | tf_op jit(solution)/shard_map/reduce_scatter | solution.py:274
  857.6 5.6 convert_reduce_fusion.1
  863.2 22.0 %all-reduce.9 = (bf16[512]{0:T(512)(128)(2,1)S(1)}, bf16[512]{0:T(512)(128)(2,1)S(1)}, bf16[512]{0:T(512)(128)(2,1)S(1)}, bf16[512]{0:T(512)(128)(2,1)S(1)}) all-reduce(bf16[512]{0:T(512)(128)(2,1)S(1)} %get-tuple-element.15, ...), channel_id=2, replica_groups=mesh['replica'=2,'part'=8,'expert'=2] {'replica','part'}, use_global_device_ids=true, to_apply=%region_26.27.clone | all-reduce | flops 2048 | bytes 8192
  885.5 30.5 %reduce-scatter.8.cloned.1.call-done = bf16[32,32]{1,0:T(8,128)(2,1)} async-done(((bf16[512,32]{1,0:T(8,128)(2,1)}), bf16[32,32]{1,0:T(8,128)(2,1)}) %reduce-scatter.8.cloned.1.call-update) | async-done | bytes 2064 | tf_op jit(solution)/shard_map/reduce_scatter | solution.py:286
  915.9 59.0 %reduce-scatter.6.cloned.1.call-done = bf16[32,512]{1,0:T(8,128)(2,1)} async-done(((bf16[512,512]{1,0:T(8,128)(2,1)}), bf16[32,512]{1,0:T(8,128)(2,1)}) %reduce-scatter.6.cloned.1.call-update) | async-done | bytes 32784 | tf_op jit(solution)/shard_map/reduce_scatter | solution.py:277
  975.0 7.2 all-reduce.11
  985.4 13.3 %all-reduce.14.cloned.1.call-done = bf16[32,1536]{1,0:T(8,128)(2,1)} async-done(((bf16[32,1536]{1,0:T(8,128)(2,1)}), bf16[32,1536]{1,0:T(8,128)(2,1)}) %all-reduce.14.cloned.1.call-update) | async-done | bytes 98320 | tf_op jit(solution)/shard_map/psum | solution.py:261
  (218 shorter events, 58.6 us)
Async XLA Ops:
  12.1 6.7 copy-start.25
  12.1 108.6 %all-to-all-start.1 = ((bf16[16,2,32,2048]{3,2,1,0:T(8,128)(2,1)}), bf16[16,2,32,2048]{3,2,1,0:T(8,128)(2,1)}, u32[]{:S(2)}, u32[]{:S(2)}) async-start(bf16[16,2,32,2048]{3,2,1,0:T(8,128)(2,1)} %pad_maximum_fusion), calls=%async_computation.1 | async-start | bytes 8388608 | tf_op jit(solution)/shard_map/all_to_all | solution.py:84
  18.7 270.7 %all-gather.2.cloned.1.call-start = ((), (), s32[]{:S(2)}) async-start(), calls=%async_computation.11 | async-start | bytes 1671168 | tf_op jit(solution)/shard_map/all_gather | solution.py:65
  24.3 101.3 %copy-start.33 = (s32[985,2]{0,1:T(2,128)S(1)}, s32[985,2]{0,1:T(2,128)}, u32[]{:S(2)}) copy-start(s32[985,2]{0,1:T(2,128)} %param.13) | copy-start | bytes 23644
  24.3 102.1 %copy-start.54 = (f32[32]{0:T(128)S(1)}, f32[32]{0:T(128)}, u32[]{:S(2)}) copy-start(f32[32]{0:T(128)} %param.14) | copy-start | bytes 388
  24.3 102.2 %copy-start.55 = (f32[32]{0:T(128)S(1)}, f32[32]{0:T(128)}, u32[]{:S(2)}) copy-start(f32[32]{0:T(128)} %param.15) | copy-start | bytes 388
  24.3 102.2 %copy-start.56 = (f32[32]{0:T(128)S(1)}, f32[32]{0:T(128)}, u32[]{:S(2)}) copy-start(f32[32]{0:T(128)} %param.18) | copy-start | bytes 388
  24.3 102.2 %copy-start.57 = (f32[32]{0:T(128)S(1)}, f32[32]{0:T(128)}, u32[]{:S(2)}) copy-start(f32[32]{0:T(128)} %param.19) | copy-start | bytes 388
  24.3 102.2 %copy-start.51 = (u32[32]{0:T(128)S(1)}, u32[32]{0:T(128)}, u32[]{:S(2)}) copy-start(u32[32]{0:T(128)} %constant.105) | copy-start | bytes 388
  24.3 210.4 %copy-start.37 = (f32[32,512]{1,0:T(8,128)S(1)}, f32[32,512]{1,0:T(8,128)}, u32[]{:S(2)}) copy-start(f32[32,512]{1,0:T(8,128)} %param.17) | copy-start | bytes 196612
  24.4 210.4 %copy-start.48 = (f32[32,32]{1,0:T(8,128)S(1)}, f32[32,32]{1,0:T(8,128)}, u32[]{:S(2)}) copy-start(f32[32,32]{1,0:T(8,128)} %param.20) | copy-start | bytes 12292
  120.7 242.3 %all-to-all-start.2 = ((bf16[16,2,128,512]{3,2,1,0:T(8,128)(2,1)}), bf16[16,2,128,512]{3,2,1,0:T(8,128)(2,1)}, u32[]{:S(2)}, u32[]{:S(2)}) async-start(bf16[16,2,128,512]{3,2,1,0:T(8,128)(2,1)} %pad_maximum_fusion.1), calls=%async_computation.2 | async-start | bytes 8388608 | tf_op jit(solution)/shard_map/all_to_all | solution.py:84
  125.6 119.2 %copy-start.12 = (bf16[985,512]{1,0:T(8,128)(2,1)S(1)}, bf16[985,512]{1,0:T(8,128)(2,1)}, u32[]{:S(2)}) copy-start(bf16[985,512]{1,0:T(8,128)(2,1)} %param.23) | copy-start | bytes 3025924
  234.7 54.8 %copy-start.49 = (f32[512]{0:T(512)}, f32[512]{0:T(512)S(1)}, u32[]{:S(2)}) copy-start(f32[512]{0:T(512)S(1)} %convert_element_type.198) | copy-start | bytes 6148
  234.7 54.8 %copy-start.52 = (f32[512]{0:T(512)}, f32[512]{0:T(512)S(1)}, u32[]{:S(2)}) copy-start(f32[512]{0:T(512)S(1)} %convert_element_type.200) | copy-start | bytes 6148
  234.8 106.1 %copy-start.44 = (f32[512]{0:T(512)}, f32[512]{0:T(512)S(1)}, u32[]{:S(2)}) copy-start(f32[512]{0:T(512)S(1)} %convert_element_type.210) | copy-start | bytes 6148
  247.8 22.4 %copy-start.7 = (bf16[985,512]{1,0:T(8,128)(2,1)S(1)}, bf16[985,512]{1,0:T(8,128)(2,1)}, u32[]{:S(2)}) copy-start(bf16[985,512]{1,0:T(8,128)(2,1)} %param.12) | copy-start | bytes 3025924
  270.2 71.9 %copy-start.23 = (bf16[512,32]{1,0:T(8,128)(2,1)}, bf16[512,32]{1,0:T(8,128)(2,1)S(1)}, u32[]{:S(2)}) copy-start(bf16[512,32]{1,0:T(8,128)(2,1)S(1)} %all_gather.27) | copy-start | bytes 98308
  270.5 23.9 %copy-start.40 = (f32[985]{0:T(1024)}, f32[985]{0:T(1024)S(1)}, u32[]{:S(2)}) copy-start(f32[985]{0:T(1024)S(1)} %broadcast_multiply_fusion.5) | copy-start | bytes 11824
  271.0 23.3 %copy-start.46 = (f32[985]{0:T(1024)}, f32[985]{0:T(1024)S(1)}, u32[]{:S(2)}) copy-start(f32[985]{0:T(1024)S(1)} %add_rsqrt_fusion.1) | copy-start | bytes 11824
  289.3 50.3 %copy-start.15 = (bf16[512,512]{1,0:T(8,128)(2,1)}, bf16[512,512]{1,0:T(8,128)(2,1)S(1)}, u32[]{:S(2)}) copy-start(bf16[512,512]{1,0:T(8,128)(2,1)S(1)} %all_gather.24) | copy-start | bytes 1572868
  289.4 85.0 %copy-start.42 = (s32[1970,1]{0,1:T(1,128)}, s32[1970,1]{0,1:T(1,128)S(1)}, u32[]{:S(2)}) copy-start(s32[1970,1]{0,1:T(1,128)S(1)} %compare_select_fusion) | copy-start | bytes 23644
  315.7 7.0 copy-start.5
  322.8 10.1 %copy-start.22 = (bf16[5,197,1,8,64]{1,4,3,0,2:T(8,128)(2,1)S(1)}, bf16[5,197,1,8,64]{1,4,3,0,2:T(8,128)(2,1)}, u32[]{:S(2)}) copy-start(bf16[5,197,1,8,64]{1,4,3,0,2:T(8,128)(2,1)} %copy.158) | copy-start | bytes 3025924
  329.5 3.2 copy-start.2
  329.5 3.3 copy-start.26
  341.7 21.3 %copy-start.38 = (f32[985]{0:T(1024)}, f32[985]{0:T(1024)S(1)}, u32[]{:S(2)}) copy-start(f32[985]{0:T(1024)S(1)} %add_rsqrt_fusion) | copy-start | bytes 11824
  342.1 29.2 %copy-start.10 = (bf16[985,512]{1,0:T(8,128)(2,1)}, bf16[985,512]{1,0:T(8,128)(2,1)S(1)}, u32[]{:S(2)}) copy-start(bf16[985,512]{1,0:T(8,128)(2,1)S(1)} %add_convert_fusion.1) | copy-start | bytes 3025924
  343.4 19.5 %copy-start.17 = (f32[985,2]{1,0:T(8,128)}, f32[985,2]{1,0:T(8,128)S(1)}, u32[]{:S(2)}) copy-start(f32[985,2]{1,0:T(8,128)S(1)} %copy.128) | copy-start | bytes 23644
  363.0 63.6 %all-to-all-start.4 = ((bf16[16,256,512]{2,1,0:T(8,128)(2,1)}), bf16[16,256,512]{2,1,0:T(8,128)(2,1)}, u32[]{:S(2)}, u32[]{:S(2)}) async-start(bf16[16,256,512]{2,1,0:T(8,128)(2,1)} %bitcast.124), calls=%async_computation.4 | async-start | bytes 8388608 | tf_op jit(solution)/shard_map/all_to_all | solution.py:101
  426.6 59.5 %all-to-all-start = ((bf16[16,256,512]{2,1,0:T(8,128)(2,1)}), bf16[16,256,512]{2,1,0:T(8,128)(2,1)}, u32[]{:S(2)}, u32[]{:S(2)}) async-start(bf16[16,256,512]{2,1,0:T(8,128)(2,1)} %bitcast.127), calls=%async_computation | async-start | bytes 8388608 | tf_op jit(solution)/shard_map/all_to_all | solution.py:101
  532.0 59.7 %all-to-all-start.3 = ((bf16[16,256,512]{2,1,0:T(8,128)(2,1)}), bf16[16,256,512]{2,1,0:T(8,128)(2,1)}, u32[]{:S(2)}, u32[]{:S(2)}) async-start(bf16[16,256,512]{2,1,0:T(8,128)(2,1)} %bitcast.129), calls=%async_computation.3 | async-start | bytes 8388608 | tf_op jit(solution)/shard_map/all_to_all | solution.py:108
  536.8 35.1 %copy-start.19 = (bf16[2,16,32,2048]{3,2,1,0:T(8,128)(2,1)S(1)}, bf16[2,16,32,2048]{3,2,1,0:T(8,128)(2,1)}, u32[]{:S(2)}) copy-start(bf16[2,16,32,2048]{3,2,1,0:T(8,128)(2,1)} %copy.134) | copy-start | bytes 12582916
  591.7 59.5 %all-to-all-start.5 = ((bf16[16,256,512]{2,1,0:T(8,128)(2,1)}), bf16[16,256,512]{2,1,0:T(8,128)(2,1)}, u32[]{:S(2)}, u32[]{:S(2)}) async-start(bf16[16,256,512]{2,1,0:T(8,128)(2,1)} %bitcast.128), calls=%async_computation.5 | async-start | bytes 8388608 | tf_op jit(solution)/shard_map/all_to_all | solution.py:108
  651.1 4.6 copy-start.13
  651.1 4.9 copy-start.43
  651.1 97.6 %all-to-all-start.7 = ((bf16[16,2,128,512]{3,2,1,0:T(8,128)(2,1)}), bf16[16,2,128,512]{3,2,1,0:T(8,128)(2,1)}, u32[]{:S(2)}, u32[]{:S(2)}) async-start(bf16[16,2,128,512]{3,2,1,0:T(8,128)(2,1)} %bitcast.126), calls=%async_computation.7 | async-start | bytes 8388608 | tf_op jit(solution)/shard_map/all_to_all | solution.py:89
  656.0 16.4 %copy-start.32 = (s32[2048]{0:T(1024)}, s32[2048]{0:T(1024)S(1)}, u32[]{:S(2)}) copy-start(s32[2048]{0:T(1024)S(1)} %pad_clamp_fusion) | copy-start | bytes 24580
  684.3 5.5 copy-start.18
  721.5 8.5 copy-start.34
  721.5 8.5 copy-start.21
  721.5 8.5 copy-start.29
  721.5 8.5 copy-start.36
  721.6 8.6 copy-start.1
  721.6 8.6 copy-start.24
  721.6 8.6 copy-start.31
  721.6 8.6 copy-start.39
  721.6 8.6 copy-start.45
  730.0 3.1 copy-start.14
  733.1 3.1 copy-start.16
  736.9 3.3 copy-start.27
  748.7 108.9 %all-to-all-start.6 = ((bf16[16,2,32,2048]{3,2,1,0:T(8,128)(2,1)}), bf16[16,2,32,2048]{3,2,1,0:T(8,128)(2,1)}, u32[]{:S(2)}, u32[]{:S(2)}) async-start(bf16[16,2,32,2048]{3,2,1,0:T(8,128)(2,1)} %bitcast.125), calls=%async_computation.6 | async-start | bytes 8388608 | tf_op jit(solution)/shard_map/all_to_all | solution.py:89
  754.2 103.3 %reduce-scatter.4.cloned.1.call-start = ((), (), s32[]{:S(2)}) async-start(), calls=%async_computation.12 | async-start | bytes 1671168 | tf_op jit(solution)/shard_map/reduce_scatter | solution.py:274
  754.3 6.7 copy-start.6
  761.0 1.3 copy-start.9
  780.1 9.0 copy-start.8
  780.1 9.0 copy-start.41
  780.1 9.0 copy-start.47
  780.1 9.0 copy-start.50
  780.1 9.0 copy-start.53
  789.2 8.3 copy-start.4
  794.3 121.6 %reduce-scatter.8.cloned.1.call-start = ((), (), s32[]{:S(2)}) async-start(), calls=%async_computation.15 | async-start | bytes 139264 | tf_op jit(solution)/shard_map/reduce_scatter | solution.py:286
  797.4 177.6 %reduce-scatter.6.cloned.1.call-start = ((), (), s32[]{:S(2)}) async-start(), calls=%async_computation.14 | async-start | bytes 557056 | tf_op jit(solution)/shard_map/reduce_scatter | solution.py:277
  800.3 198.5 %all-reduce.14.cloned.1.call-start = ((), (), s32[]{:S(2)}) async-start(), calls=%async_computation.13 | async-start | bytes 196608 | tf_op jit(solution)/shard_map/psum | solution.py:261
  (7 other events, 7.0 us)
Sparse Core Ops, SparseCore 0:
  22.4 77.5 all-gather.1
  794.5 63.0 reduce-scatter.3
  862.0 53.8 reduce-scatter.7
  919.8 55.1 reduce-scatter.5
  977.1 21.6 all-reduce.13

commit v2 on v0

v2 whole, which is shorter than its diff:
```python
from functools import partial

import jax
import jax.numpy as jnp
import numpy as np
from jax import lax
from jax.experimental import pallas as pl
from jax.experimental.pallas import tpu as pltpu
from jax.sharding import Mesh
from jax.sharding import PartitionSpec as P

D = 512
HEADS = 8
EXPERTS = 32
SEQ = 197
CAP = 128
ROWS = 208
HEAD = D // HEADS
LANES = 128
QKV = 3 * D
PACKED = QKV + D + LANES
epsilon = 1e-06
low = jnp.bfloat16
full = jnp.float32
BIG = 56 * 1024 * 1024


def dot(left, right):
    return jnp.dot(left, right, preferred_element_type=full)


def dot_rt(left, right):
    return lax.dot_general(left, right, (((1,), (1,)), ((), ())), preferred_element_type=full)


def dot_lt(left, right):
    return lax.dot_general(left, right, (((0,), (0,)), ((), ())), preferred_element_type=full)


def lanes_of(shape):
    return lax.broadcasted_iota(jnp.int32, shape, len(shape) - 1)


def normed_rows(values):
    center = values - jnp.mean(values, axis=-1, keepdims=True)
    factor = lax.rsqrt(jnp.mean(center * center, axis=-1, keepdims=True) + epsilon)
    return center * factor, factor


def norm_back(normed, factor, gain_vec, upstream):
    scaled = upstream * gain_vec
    return factor * (
        scaled
        - jnp.mean(scaled, axis=-1, keepdims=True)
        - normed * jnp.mean(scaled * normed, axis=-1, keepdims=True)
    )


def norm_vectors(weights_ref):
    rows = weights_ref[:, QKV + D :].astype(full).T
    return [rows[EXPERTS + i : EXPERTS + i + 1] for i in range(4)]


def halves(pair):
    first = lanes_of(pair.shape) < HEAD
    zero = jnp.zeros_like(pair)
    return jnp.where(first, pair, zero), jnp.where(first, zero, pair)


def head_probs(query, key_pair):
    scores = dot_rt(query, key_pair) * (HEAD**-0.5)
    scores = jnp.where(lanes_of(scores.shape) < SEQ, scores, -1e30)
    grown = jnp.exp(scores - jnp.max(scores, axis=-1, keepdims=True))
    return grown / jnp.sum(grown, axis=-1, keepdims=True)


def attend_kernel(x_ref, w_ref, qkv_ref, ctx_ref, r_ref, h_ref, probs_ref):
    gain_one, bias_one, gain_two, bias_two = norm_vectors(w_ref)
    x = x_ref[0].astype(full)
    normed, _ = normed_rows(x)
    attn_in = (normed * gain_one + bias_one).astype(low)
    qkv_ref[0] = dot(attn_in, w_ref[:, :QKV]).astype(low)
    for pair in range(HEADS // 2):
        at = pair * LANES
        query = halves(qkv_ref[0, :, at : at + LANES])
        key = qkv_ref[0, :, D + at : D + at + LANES]
        value = halves(qkv_ref[0, :, 2 * D + at : 2 * D + at + LANES])
        total = None
        for i in range(2):
            part = dot(head_probs(query[i], key).astype(low), value[i])
            total = part if total is None else total + part
        ctx_ref[0, :, at : at + LANES] = total.astype(low)
    r = x + dot(ctx_ref[0], w_ref[:, QKV : QKV + D])
    r_ref[0] = r
    normed, _ = normed_rows(r)
    h = (normed * gain_two + bias_two).astype(low)
    h_ref[0] = h
    logits = dot(h, w_ref[:, QKV + D :])
    logits = jnp.where(lanes_of(logits.shape) < EXPERTS, logits, -1e30)
    grown = jnp.exp(logits - jnp.max(logits, axis=-1, keepdims=True))
    probs_ref[0] = grown / jnp.sum(grown, axis=-1, keepdims=True)


def image_spec(width):
    return pl.BlockSpec((1, ROWS, width), lambda i: (i, 0, 0))


def whole_spec(shape):
    return pl.BlockSpec(shape, lambda *_: (0,) * len(shape))


def params(n):
    return pltpu.CompilerParams(
        dimension_semantics=("arbitrary",) * n, vmem_limit_bytes=BIG
    )


def attend(x, weights):
    images = x.shape[0]
    shapes = ((QKV, low), (D, low), (D, full), (D, low), (LANES, full))
    return pl.pallas_call(
        attend_kernel,
        grid=(images,),
        in_specs=[image_spec(D), whole_spec(weights.shape)],
        out_specs=[image_spec(width) for width, _ in shapes],
        out_shape=[jax.ShapeDtypeStruct((images, ROWS, w), t) for w, t in shapes],
        compiler_params=params(1),
        cost_estimate=pl.CostEstimate(
            flops=8 * 10**9, bytes_accessed=12 * 10**6, transcendentals=2 * 10**6
        ),
        name="attend",
    )(x, weights)


def attend_back_kernel(
    images, x_ref, w_ref, qkv_ref, ctx_ref, r_ref, h_ref, probs_ref, dprobs_ref, dh_ref, dy_ref,
    dx_ref, grads_ref, dqkv_ref, qkv_acc, proj_acc, router_acc, norm_acc,
):
    step = pl.program_id(0)

    @pl.when(step == 0)
    def _():
        qkv_acc[...] = jnp.zeros_like(qkv_acc)
        proj_acc[...] = jnp.zeros_like(proj_acc)
        router_acc[...] = jnp.zeros_like(router_acc)
        norm_acc[...] = jnp.zeros_like(norm_acc)

    gain_one, bias_one, gain_two, _ = norm_vectors(w_ref)
    probs, dprobs = probs_ref[0], dprobs_ref[0]
    dlogits = (probs * (dprobs - jnp.sum(probs * dprobs, axis=-1, keepdims=True))).astype(low)
    router_acc[...] += dot_lt(h_ref[0], dlogits)
    dh = dh_ref[0] + dot_rt(dlogits, w_ref[:, QKV + D :])
    normed, factor = normed_rows(r_ref[0])
    norm_acc[2:3] += jnp.sum(dh * normed, axis=0, keepdims=True)
    norm_acc[3:4] += jnp.sum(dh, axis=0, keepdims=True)
    dr = dy_ref[0].astype(full) + norm_back(normed, factor, gain_two, dh)
    dattended = dr.astype(low)
    proj_acc[...] += dot_lt(ctx_ref[0], dattended)
    dctx = dot_rt(dattended, w_ref[:, QKV : QKV + D]).astype(low)
    for pair in range(HEADS // 2):
        at = pair * LANES
        query = halves(qkv_ref[0, :, at : at + LANES])
        key = qkv_ref[0, :, D + at : D + at + LANES]
        keys = halves(key)
        value = qkv_ref[0, :, 2 * D + at : 2 * D + at + LANES]
        dhead = halves(dctx[:, at : at + LANES])
        dq = dk = dv = None
        for i in range(2):
            p = head_probs(query[i], key)
            dp = dot_rt(dhead[i], value)
            ds = (p * (dp - jnp.sum(p * dp, axis=-1, keepdims=True))).astype(low)
            parts = dot(ds, keys[i]), dot_lt(ds, query[i]), dot_lt(p.astype(low), dhead[i])
            dq, dk, dv = parts if dq is None else (dq + parts[0], dk + parts[1], dv + parts[2])
        dqkv_ref[:, at : at + LANES] = (dq * HEAD**-0.5).astype(low)
        dqkv_ref[:, D + at : D + at + LANES] = (dk * HEAD**-0.5).astype(low)
        dqkv_ref[:, 2 * D + at : 2 * D + at + LANES] = dv.astype(low)
    normed, factor = normed_rows(x_ref[0].astype(full))
    attn_in = (normed * gain_one + bias_one).astype(low)
    qkv_acc[...] += dot_lt(attn_in, dqkv_ref[...])
    da = dot_rt(dqkv_ref[...], w_ref[:, :QKV])
    norm_acc[0:1] += jnp.sum(da * normed, axis=0, keepdims=True)
    norm_acc[1:2] += jnp.sum(da, axis=0, keepdims=True)
    dx_ref[0] = dr + norm_back(normed, factor, gain_one, da)

    @pl.when(step == images - 1)
    def _():
        grads_ref[:, :QKV] = qkv_acc[...].astype(low)
        grads_ref[:, QKV : QKV + D] = proj_acc[...].astype(low)
        columns = norm_acc[...].T
        moved = pltpu.roll(columns, EXPERTS, 1)
        lane = lanes_of(moved.shape)
        tile = jnp.where(lane < EXPERTS, router_acc[...], moved)
        grads_ref[:, QKV + D :] = tile.astype(low)


def attend_back(x, weights, qkv, ctx, r, h, probs, dprobs, dh, dy):
    images = x.shape[0]
    widths = (D, None, QKV, D, D, D, LANES, LANES, D, D)
    return pl.pallas_call(
        partial(attend_back_kernel, images),
        grid=(images,),
        in_specs=[whole_spec(weights.shape) if w is None else image_spec(w) for w in widths],
        out_specs=[image_spec(D), whole_spec((D, PACKED))],
        out_shape=[
            jax.ShapeDtypeStruct((images, ROWS, D), full),
            jax.ShapeDtypeStruct((D, PACKED), low),
        ],
        scratch_shapes=[
            pltpu.VMEM((ROWS, QKV), low),
            pltpu.VMEM((D, QKV), full),
            pltpu.VMEM((D, D), full),
            pltpu.VMEM((D, LANES), full),
            pltpu.VMEM((LANES, D), full),
        ],
        compiler_params=params(1),
        cost_estimate=pl.CostEstimate(
            flops=20 * 10**9, bytes_accessed=16 * 10**6, transcendentals=2 * 10**6
        ),
        name="attend_back",
    )(x, weights, qkv, ctx, r, h, probs, dprobs, dh, dy)


def dispatch_kernel(own, keys_ref, rows_ref, out_ref):
    slots = lax.broadcasted_iota(jnp.int32, (CAP, keys_ref.shape[2]), 0).astype(full)
    picks = [(keys_ref[0, i : i + 1] == slots).astype(low) for i in range(own)]
    picks = jnp.concatenate(picks, axis=0)
    out_ref[0] = dot(picks, rows_ref[...]).astype(low)


def dispatch(keys, rows):
    peers, own, tokens = keys.shape
    return pl.pallas_call(
        partial(dispatch_kernel, own),
        grid=(peers,),
        in_specs=[pl.BlockSpec((1, own, tokens), lambda i: (i, 0, 0)), whole_spec(rows.shape)],
        out_specs=pl.BlockSpec((1, own * CAP, D), lambda i: (i, 0, 0)),
        out_shape=jax.ShapeDtypeStruct((peers, own * CAP, D), low),
        compiler_params=params(1),
        cost_estimate=pl.CostEstimate(
            flops=2 * EXPERTS * CAP * tokens * D, bytes_accessed=5 * 10**6, transcendentals=0
        ),
        name="dispatch",
    )(keys, rows)


def chooser(own, step):
    shape = (LANES, own * CAP)
    expert = lax.broadcasted_iota(jnp.int32, shape, 0)
    slot = lax.broadcasted_iota(jnp.int32, shape, 1)
    return (expert == step * own + slot // CAP).astype(low)


def combine_kernel(own, peers, keys_ref, probs_ref, dy_ref, r_ref, y_ref, out_ref, dprobs_ref, acc):
    step = pl.program_id(0)
    spread = chooser(own, step)
    y = y_ref[0]

    @pl.when(step == 0)
    def _():
        acc[...] = jnp.zeros_like(acc)
        dprobs_ref[...] = jnp.zeros_like(dprobs_ref)

    for at in range(0, acc.shape[0], ROWS):
        rows = slice(at, at + ROWS)
        slot = lanes_of((ROWS, own * CAP)) % CAP
        here = dot(keys_ref[rows], spread) == slot.astype(full)
        gate = dot(probs_ref[rows].astype(low), spread)
        acc[rows] += dot(jnp.where(here, gate, 0.0).astype(low), y)
        agreed = jnp.where(here, dot_rt(dy_ref[rows], y), 0.0)
        lane = lanes_of((ROWS, LANES))
        change = dprobs_ref[rows]
        for i in range(own):
            column = jnp.sum(agreed[:, i * CAP : (i + 1) * CAP], axis=-1, keepdims=True)
            change = jnp.where(lane == step * own + i, column, change)
        dprobs_ref[rows] = change

    @pl.when(step == peers - 1)
    def _():
        out_ref[...] = (r_ref[...] + acc[...]).astype(low)


def combine(keys, probs, dy, r, y):
    peers, width, _ = y.shape
    tokens = keys.shape[0]
    return pl.pallas_call(
        partial(combine_kernel, width // CAP, peers),
        grid=(peers,),
        in_specs=[whole_spec(a.shape) for a in (keys, probs, dy, r)]
        + [pl.BlockSpec((1, width, D), lambda i: (i, 0, 0))],
        out_specs=[whole_spec((tokens, D)), whole_spec((tokens, LANES))],
        out_shape=[
            jax.ShapeDtypeStruct((tokens, D), low),
            jax.ShapeDtypeStruct((tokens, LANES), full),
        ],
        scratch_shapes=[pltpu.VMEM((tokens, D), full)],
        compiler_params=params(1),
        cost_estimate=pl.CostEstimate(
            flops=12 * 10**9, bytes_accessed=10 * 10**6, transcendentals=0
        ),
        name="combine",
    )(keys, probs, dy, r, y)


def gather_kernel(own, keys_ref, rows_ref, out_ref):
    step = pl.program_id(0)
    spread = chooser(own, step)

    @pl.when(step == 0)
    def _():
        out_ref[...] = jnp.zeros_like(out_ref)

    for at in range(0, out_ref.shape[0], ROWS):
        rows = slice(at, at + ROWS)
        slot = lanes_of((ROWS, own * CAP)) % CAP
        here = dot(keys_ref[rows], spread) == slot.astype(full)
        out_ref[rows] += dot(here.astype(low), rows_ref[0])


def gather(keys, back):
    peers, width, _ = back.shape
    tokens = keys.shape[0]
    return pl.pallas_call(
        partial(gather_kernel, width // CAP),
        grid=(peers,),
        in_specs=[whole_spec(keys.shape), pl.BlockSpec((1, width, D), lambda i: (i, 0, 0))],
        out_specs=whole_spec((tokens, D)),
        out_shape=jax.ShapeDtypeStruct((tokens, D), full),
        compiler_params=params(1),
        cost_estimate=pl.CostEstimate(
            flops=6 * 10**9, bytes_accessed=7 * 10**6, transcendentals=0
        ),
        name="gather",
    )(keys, back)


GELU = 0.7978845608028654
CUBE = 0.044715


def gelu_pair(u):
    square = u * u
    bent = jnp.tanh(u * (GELU * CUBE * square + GELU))
    half = 0.5 * bent + 0.5
    value = u * half
    return value, half + value * (1.0 - bent) * (3.0 * GELU * CUBE * square + GELU)


def first_kernel(chunk, h_ref, dy_ref, w_ref, wr_ref, sel_ref, g_ref, slope_ref, dye_ref, dw_ref, dye_t):
    rows = h_ref.shape[0] * CAP
    sources = chunk // CAP
    tile = w_ref.shape[3]

    @pl.when(pl.program_id(1) == 0)
    def _():
        for at in range(0, rows, chunk):
            source = slice(at // CAP, at // CAP + sources)
            h = h_ref[source, 0].reshape(chunk, D)
            logits = dot(h, wr_ref[...])
            logits = jnp.where(lanes_of(logits.shape) < EXPERTS, logits, -1e30)
            grown = jnp.exp(logits - jnp.max(logits, axis=-1, keepdims=True))
            mine = jnp.sum(grown * sel_ref[0], axis=-1, keepdims=True)
            gate = mine / jnp.sum(grown, axis=-1, keepdims=True)
            dye = dy_ref[source, 0].reshape(chunk, D).astype(full) * gate
            dye_ref[source, 0] = dye.astype(low).reshape(sources, CAP, D)
            dye_t[:, at : at + chunk] = dye.T.astype(low)

    w = w_ref[:, 0].reshape(D, tile)
    for at in range(0, rows, chunk):
        source = slice(at // CAP, at // CAP + sources)
        u = dot(h_ref[source, 0].reshape(chunk, D), w)
        value, slope = gelu_pair(u)
        g_ref[0, at : at + chunk] = value.astype(low)
        slope_ref[0, at : at + chunk] = slope.astype(low)
    grad = dot(dye_t[...], g_ref[0]).T
    dw_ref[:, 0] = grad.astype(low).reshape(dw_ref.shape[0], dw_ref.shape[2], D)


def expert_first(h, dy, w_in, w_router, select, tile):
    sources, own, _, _ = h.shape
    owners, _, depth, hidden = w_in.shape
    rows = sources * CAP
    per = hidden // owners
    token_spec = pl.BlockSpec((sources, 1, CAP, D), lambda e, f: (0, e, 0, 0))
    hidden_spec = pl.BlockSpec((1, rows, tile), lambda e, f: (e, 0, f))
    return pl.pallas_call(
        partial(first_kernel, 2 * CAP),
        grid=(own, hidden // tile),
        in_specs=[
            token_spec,
            token_spec,
            pl.BlockSpec((owners, 1, depth, tile), lambda e, f: (0, e, 0, f)),
            whole_spec(w_router.shape),
            pl.BlockSpec((1, 1, LANES), lambda e, f: (e, 0, 0)),
        ],
        out_specs=[
            hidden_spec,
            hidden_spec,
            token_spec,
            pl.BlockSpec((tile // per, 1, per, D), lambda e, f: (f, e, 0, 0)),
        ],
        out_shape=[
            jax.ShapeDtypeStruct((own, rows, hidden), low),
            jax.ShapeDtypeStruct((own, rows, hidden), low),
            jax.ShapeDtypeStruct(h.shape, low),
            jax.ShapeDtypeStruct((owners, own, per, D), low),
        ],
        scratch_shapes=[pltpu.VMEM((D, rows), low)],
        compiler_params=params(2),
        cost_estimate=pl.CostEstimate(
            flops=4 * own * rows * D * hidden,
            bytes_accessed=50 * 10**6,
            transcendentals=own * rows * hidden,
        ),
        name="expert_first",
    )(h, dy, w_in, w_router, select)


def second_kernel(g_ref, w_ref, y_ref):
    hidden = g_ref.shape[2]
    y = dot(g_ref[0], w_ref[:, 0].reshape(hidden, D)).astype(low)
    y_ref[:, 0] = y.reshape(y_ref.shape[0], CAP, D)


def expert_second(g, w_out):
    own, rows, hidden = g.shape
    owners, _, per, _ = w_out.shape
    block = 4
    return pl.pallas_call(
        second_kernel,
        grid=(own, rows // (block * CAP)),
        in_specs=[
            pl.BlockSpec((1, block * CAP, hidden), lambda e, i: (e, i, 0)),
            pl.BlockSpec((owners, 1, per, D), lambda e, i: (0, e, 0, 0)),
        ],
        out_specs=pl.BlockSpec((block, 1, CAP, D), lambda e, i: (i, e, 0, 0)),
        out_shape=jax.ShapeDtypeStruct((rows // CAP, own, CAP, D), low),
        compiler_params=params(2),
        cost_estimate=pl.CostEstimate(
            flops=2 * own * rows * D * hidden, bytes_accessed=26 * 10**6, transcendentals=0
        ),
        name="expert_second",
    )(g, w_out)


def back_kernel(chunk, steps, h_ref, dye_ref, slope_ref, w_in_ref, w_out_ref, dbuf_ref, dw_ref, h_t, du_ref, acc):
    rows = h_ref.shape[0] * CAP
    sources = chunk // CAP
    tile = slope_ref.shape[2]
    step = pl.program_id(1)

    @pl.when(step == 0)
    def _():
        acc[...] = jnp.zeros_like(acc)
        for at in range(0, rows, chunk):
            source = slice(at // CAP, at // CAP + sources)
            h_t[:, at : at + chunk] = h_ref[source, 0].reshape(chunk, D).T

    w_in = w_in_ref[:, 0].reshape(D, tile)
    w_out = w_out_ref[:, 0].reshape(tile, D)
    for at in range(0, rows, chunk):
        source = slice(at // CAP, at // CAP + sources)
        dg = dot_rt(dye_ref[source, 0].reshape(chunk, D), w_out)
        du = (dg * slope_ref[0, at : at + chunk].astype(full)).astype(low)
        du_ref[at : at + chunk] = du
        acc[at : at + chunk] += dot_rt(du, w_in)
    grad = dot(h_t[...], du_ref[...]).astype(low)
    dw_ref[:, 0] = grad.reshape(dw_ref.shape[0], dw_ref.shape[2], tile)

    @pl.when(step == steps - 1)
    def _():
        dbuf_ref[:, 0] = acc[...].astype(low).reshape(rows // CAP, CAP, D)


def expert_back(h, dye, slope, w_in, w_out, tile):
    sources, own, _, _ = h.shape
    owners, _, depth, hidden = w_in.shape
    rows = sources * CAP
    per = hidden // owners
    token_spec = pl.BlockSpec((sources, 1, CAP, D), lambda e, f: (0, e, 0, 0))
    in_spec = pl.BlockSpec((owners, 1, depth, tile), lambda e, f: (0, e, 0, f))
    return pl.pallas_call(
        partial(back_kernel, 2 * CAP, hidden // tile),
        grid=(own, hidden // tile),
        in_specs=[
            token_spec,
            token_spec,
            pl.BlockSpec((1, rows, tile), lambda e, f: (e, 0, f)),
            in_spec,
            pl.BlockSpec((tile // per, 1, per, D), lambda e, f: (f, e, 0, 0)),
        ],
        out_specs=[token_spec, in_spec],
        out_shape=[
            jax.ShapeDtypeStruct(h.shape, low),
            jax.ShapeDtypeStruct(w_in.shape, low),
        ],
        scratch_shapes=[
            pltpu.VMEM((D, rows), low),
            pltpu.VMEM((rows, tile), low),
            pltpu.VMEM((rows, D), full),
        ],
        compiler_params=params(2),
        cost_estimate=pl.CostEstimate(
            flops=6 * own * rows * D * hidden, bytes_accessed=40 * 10**6, transcendentals=0
        ),
        name="expert_back",
    )(h, dye, slope, w_in, w_out)


ALL = ("replica", "part")


def body(
    tokens,
    choices,
    ln1_gain,
    ln1_bias,
    w_qkv,
    w_proj,
    ln2_gain,
    ln2_bias,
    w_router,
    w_expert_in,
    w_expert_out,
    cotangent,
):
    replicas, parts, groups = (lax.axis_size(name) for name in ("replica", "part", "expert"))
    owners = replicas * parts
    peers = parts * groups
    own = EXPERTS // peers
    images = tokens.shape[0] // SEQ
    count = images * ROWS
    tile = 512 * 16 // peers

    order = np.arange(EXPERTS).reshape(groups, parts, own).transpose(1, 0, 2).reshape(-1)
    small_rows = w_router.shape[0]
    placed_router = (
        w_router.reshape(small_rows, groups, parts, own).transpose(0, 2, 1, 3).reshape(small_rows, EXPERTS)
    )
    vectors = jnp.stack([ln1_gain, ln1_bias, ln2_gain, ln2_bias], axis=1)
    packed = jnp.concatenate(
        [w_qkv, w_proj, placed_router, vectors, jnp.zeros((small_rows, LANES - EXPERTS - 4), full)],
        axis=1,
    ).astype(low)
    weights = lax.all_gather(packed, ALL, axis=0, tiled=True)

    def spread(master):
        pieces = master.astype(low).reshape(parts, own, *master.shape[1:])
        pieces = jnp.concatenate([pieces] * replicas, axis=0)
        return lax.all_to_all(pieces, ALL, split_axis=0, concat_axis=0, tiled=True)

    def collect(grad):
        pieces = lax.all_to_all(grad, ALL, split_axis=0, concat_axis=0, tiled=True)
        pieces = pieces.reshape(replicas, parts * own, *grad.shape[2:])
        return jnp.sum(pieces.astype(full), axis=0)

    def exchange(rows):
        rows = rows.reshape(peers, own * CAP, D)
        rows = lax.all_to_all(rows, ("part", "expert"), split_axis=0, concat_axis=0, tiled=True)
        return rows.reshape(peers, own, CAP, D)

    def padded(rows, fill=0):
        rows = rows.reshape(images, SEQ, rows.shape[1])
        return jnp.pad(rows, ((0, 0), (0, ROWS - SEQ), (0, 0)), constant_values=fill)

    x = padded(tokens)
    dy = padded(cotangent)
    picks = padded(choices, -1).reshape(count, 2)
    named = (picks[:, :, None] == order[None, None, :]).any(axis=1)
    earlier = np.tril(np.ones((count, count)), -1).astype(low)
    slots = dot(earlier, named.astype(low))
    keys = jnp.where(named, slots, -1.0)
    key_rows = keys.T.reshape(peers, own, count)
    key_columns = jnp.pad(keys, ((0, 0), (0, LANES - EXPERTS)), constant_values=-1).astype(low)

    dy_rows = dy.reshape(count, D)
    dy_slots = exchange(dispatch(key_rows, dy_rows))
    first_weight = spread(w_expert_in)
    qkv, ctx, r, h, probs = attend(x, weights)
    h_slots = exchange(dispatch(key_rows, h.reshape(count, D)))
    second_weight = spread(w_expert_out)
    mine = (lax.axis_index("part") * groups + lax.axis_index("expert")) * own + jnp.arange(own)
    select = (mine[:, None, None] == jnp.arange(LANES)[None, None, :]).astype(full)
    g, slope, dye, dw_second = expert_first(
        h_slots, dy_slots, first_weight, weights[:, QKV + D :], select, tile
    )
    y = exchange(expert_second(g, second_weight))
    dbuf, dw_first = expert_back(h_slots, dye, slope, first_weight, second_weight, tile)
    dbuf = exchange(dbuf)
    expert_out_grad = collect(dw_second)
    expert_in_grad = collect(dw_first)
    output, dprobs = combine(
        key_columns,
        probs.reshape(count, LANES),
        dy_rows,
        r.reshape(count, D),
        y.reshape(peers, own * CAP, D),
    )
    dh = gather(key_columns, dbuf.reshape(peers, own * CAP, D))
    dx, grads = attend_back(
        x, weights, qkv, ctx, r, h, probs,
        dprobs.reshape(images, ROWS, LANES), dh.reshape(images, ROWS, D), dy,
    )
    grads = grads.reshape(owners, small_rows, PACKED)
    grads = lax.all_to_all(grads, ALL, split_axis=0, concat_axis=0, tiled=True)
    grads = jnp.sum(grads.astype(full), axis=0).astype(low)
    grads = lax.psum(grads, "expert").astype(full)
    router_grad = (
        grads[:, QKV + D : QKV + D + EXPERTS]
        .reshape(small_rows, parts, groups, own)
        .transpose(0, 2, 1, 3)
        .reshape(small_rows, EXPERTS)
    )
    norms = [grads[:, QKV + D + EXPERTS + i] for i in range(4)]

    def unpadded(rows):
        return rows.reshape(images, ROWS, D)[:, :SEQ].reshape(images * SEQ, D)

    return (
        unpadded(output),
        unpadded(dx),
        norms[0],
        norms[1],
        grads[:, :QKV],
        grads[:, QKV : QKV + D],
        norms[2],
        norms[3],
        router_grad,
        expert_in_grad,
        expert_out_grad,
    )


def solution(mesh):
    dp, groups = mesh.shape["dp"], mesh.shape["expert"]
    parts = min(EXPERTS // groups, dp // 2)
    mesh = Mesh(mesh.devices.reshape(dp // parts, parts, groups), ("replica", "part", "expert"))
    rows = P(("replica", "part", "expert"), None)
    vector, matrix = P(ALL), P(ALL, None)
    experts = P("expert", ALL, None)
    return jax.shard_map(
        body,
        mesh=mesh,
        in_specs=(
            rows, rows, vector, vector, matrix, matrix, vector, vector, matrix, experts, experts, rows,
        ),
        out_specs=(
            rows, rows, vector, vector, matrix, matrix, vector, vector, matrix, experts, experts,
        ),
        check_vma=False,
    )
```

time: 1570 us -> 774 us (0.49)
  waiting for transfers between devices: 954 us -> 347 us
  Pallas kernels: 0 us -> 213 us
  matrix products: 209 us -> 2.5 us
  local copies, waits for them, and re-layouts: 161 us -> 19.5 us
  other arithmetic: 94.2 us -> 24.2 us
  starting transfers between devices: 23.2 us -> 44.2 us
    reduce_scatter x5 -> x0, waiting for transfers between devices: 756 us -> none  [the longest x1 334 us: body(): lax.psum_scatter(grad_first.astype(jnp.bfloat16), 'dp', scatter_dimension...]
    pallas_call x0 -> x9, Pallas kernels: none -> 213 us  [the longest x1 40.1 us: expert_back(): pl.pallas_call(partial(back_kernel, 2 * CAP, hidden // tile), grid=(own,...]
    dot_general x21 -> x1, matrix products: 209 us -> 2.5 us  [dot(): return jnp.dot(left, right, preferred_element_type=full)]
    all_to_all x4 -> x7, waiting for transfers between devices: 107 us -> 264 us  [the longest x3 115 us: exchange(): lax.all_to_all(rows, ('part', 'expert'), split_axis=0, concat_axis=0, til...]
    all_to_all x0 -> x2, blocking collectives: none -> 107 us  [the longest x1 55 us: body(): grads = lax.all_to_all(grads, ALL, split_axis=0, concat_axis=0, tiled=True)]
    all_gather x2 -> x0, blocking collectives: 47.7 us -> none  [the longest x1 26.9 us: body(): lax.all_gather(w_router.astype(low_type), 'dp', axis=0, tiled=True)]
    unnamed x2 -> x0, blocking collectives: 45 us -> none
    convert_element_type x7 -> x0, local copies, waits for them, and re-layouts: 38.7 us -> none  [the longest x1 9 us: body(): grad_mixed = jnp.stack([grad_queries, grad_keys, grad_values], axis=2).re...]
  transfers between devices with their start and end apart: 13 -> 9, of which waited for: 10 -> 7; matrix products, arithmetic and copies ran while one was open for 18% -> 4% of each run, Pallas kernels for 0% -> 24%
where the time goes in v2:
time: 774 us; the launch traced here: 771 us
  waiting for transfers between devices  347 us (45%)
  Pallas kernels  213 us (28%)
  blocking collectives  107 us (14%)
  starting transfers between devices  44.2 us (6%)
  other arithmetic  24.2 us (3%)
  local copies, waits for them, and re-layouts  19.5 us (3%)
  between operations  14.3 us (2%)
    all_to_all x3, waiting for transfers between devices, exchange(): lax.all_to_all(rows, ('part', 'expert'), split_axis=0, concat_axis=0, til...  115 us
    all_to_all x2, waiting for transfers between devices, collect(): pieces = lax.all_to_all(grad, ALL, split_axis=0, concat_axis=0, tiled=True)  95.2 us
    all_gather x1, waiting for transfers between devices, body(): weights = lax.all_gather(packed, ALL, axis=0, tiled=True)  82.8 us
    all_to_all x1, blocking collectives, body(): grads = lax.all_to_all(grads, ALL, split_axis=0, concat_axis=0, tiled=True)  55 us
    all_to_all x2, waiting for transfers between devices, spread(): return lax.all_to_all(pieces, ALL, split_axis=0, concat_axis=0, tiled=True)  53.7 us
    all_to_all x1, blocking collectives, exchange(): lax.all_to_all(rows, ('part', 'expert'), split_axis=0, concat_axis=0, til...  51.7 us
    pallas_call x1, Pallas kernels, expert_back(): pl.pallas_call(partial(back_kernel, 2 * CAP, hidden // tile), grid=(own,...  40.1 us
    pallas_call x1, Pallas kernels, expert_first(): pl.pallas_call(partial(first_kernel, 2 * CAP), grid=(own, hidden // tile)...  36.5 us
  transfers between devices with their start and end apart: 9, of which 7 were waited for; matrix products, arithmetic and copies ran while one was open for 4% of the time, Pallas kernels for 24%

profile of v2, /device:TPU:13, one launch (start us, length us, event | category | flops | bytes accessed | tf_op | source)
XLA Modules:
  0.0 771.3 jit_solution(10575434330628645377)
XLA Ops:
  7.2 0.8 reshape.143
  8.0 0.1 eq.38
  8.1 1.5 reshape.148
  9.6 0.8 compare_reduce_fusion
  10.3 2.5 bitcast_select_fusion.1
  12.8 0.7 reshape.151.keys_ref
  13.6 1.1 pad.19.dy_ref
  14.7 12.1 %dispatch.3 = bf16[16,256,512]{2,1,0:T(8,128)(2,1)} custom-call(f32[16,2,1040]{2,1,0:T(2,128)} %reshape.151.keys_ref, bf16[1040,512]{1,0:T(8,128)(2,1)} %bitcast.55), custom_call_target="tpu_custom_call" | custom-call | flops 4362076160 | bytes 5000000 | tf_op jit(solution)/shard_map/dispatch/pallas_call | solution.py:232
  26.7 5.5 all-to-all-start.1
  32.2 2.5 convert_element_type.34
  34.7 2.4 pad_maximum_fusion
  37.1 50.4 %all-to-all-done.1 = bf16[16,256,512]{2,1,0:T(8,128)(2,1)} async-done(((bf16[16,256,512]{2,1,0:T(8,128)(2,1)}), bf16[16,256,512]{2,1,0:T(8,128)(2,1)}, u32[]{:S(2)}, u32[]{:S(2)}) %all-to-all-start.1) | async-done | bytes 4194336 | tf_op jit(solution)/shard_map/all_to_all | solution.py:558
  87.5 6.0 all-to-all-start.2
  93.6 0.1 copy.67
  93.7 0.1 copy.69
  93.8 0.1 copy.70
  93.9 0.1 copy.71
  94.0 0.1 copy.72
  94.1 0.1 copy.73
  94.2 0.8 concatenate.10
  95.0 0.3 reshape.144
  95.3 1.1 pad.18.x_ref
  96.4 82.8 %all-gather.2.cloned.1.call-done.w_ref = bf16[512,2176]{1,0:T(8,128)(2,1)} async-done(((bf16[32,2176]{1,0:T(8,128)(2,1)}), bf16[512,2176]{1,0:T(8,128)(2,1)}) %all-gather.2.cloned.1.call-update) | async-done | bytes 2228240 | tf_op jit(solution)/shard_map/all_gather | solution.py:544
  179.3 15.0 %attend.1 = (bf16[5,208,1536]{2,1,0:T(8,128)(2,1)}, bf16[5,208,512]{2,1,0:T(8,128)(2,1)}, f32[5,208,512]{2,1,0:T(8,128)}, bf16[5,208,512]{2,1,0:T(8,128)(2,1)}, f32[5,208,128]{2,1,0:T(8,128)}) custom-call(bf16[5,208,512]{2,1,0:T(8,128)(2,1)} %pad.18.x_ref, bf16[512,2176]{1,0:T(8,128)(2,1)} %all-gather.2.cloned.1.call-done.w_ref), custom_call_target="tpu_custom_call" | custom-call | flops 8000000000 | bytes 12000000 | tf_op jit(solution)/shard_map/attend/pallas_call | solution.py:121
  194.3 12.1 %dispatch.2 = bf16[16,256,512]{2,1,0:T(8,128)(2,1)} custom-call(f32[16,2,1040]{2,1,0:T(2,128)} %reshape.151.keys_ref, bf16[1040,512]{1,0:T(8,128)(2,1)} %bitcast.64), custom_call_target="tpu_custom_call" | custom-call | flops 4362076160 | bytes 5000000 | tf_op jit(solution)/shard_map/dispatch/pallas_call | solution.py:232
  206.3 7.5 all-to-all-start
  213.8 2.5 convert_element_type.36
  216.3 2.4 pad_maximum_fusion.1
  218.6 50.1 %all-to-all-done = bf16[16,256,512]{2,1,0:T(8,128)(2,1)} async-done(((bf16[16,256,512]{2,1,0:T(8,128)(2,1)}), bf16[16,256,512]{2,1,0:T(8,128)(2,1)}, u32[]{:S(2)}, u32[]{:S(2)}) %all-to-all-start) | async-done | bytes 4194336 | tf_op jit(solution)/shard_map/all_to_all | solution.py:558
  268.7 7.2 all-to-all-start.3
  275.9 0.6 compare_convert_fusion.sel_ref
  276.5 1.6 slice.40.wr_ref
  278.1 36.5 %expert_first.1 = (bf16[2,2048,2048]{2,1,0:T(8,128)(2,1)}, bf16[2,2048,2048]{2,1,0:T(8,128)(2,1)}, bf16[16,2,128,512]{3,2,1,0:T(8,128)(2,1)}, bf16[16,2,128,512]{3,2,1,0:T(8,128)(2,1)}) custom-call(bf16[16,2,128,512]{3,2,1,0:T(8,128)(2,1)} %bitcast.13.h_ref, bf16[16,2,128,512]{3,2,1,0:T(8,128)(2,1)} %bitcast.14.dy_ref, ...), custom_call_target="tpu_custom_call" | custom-call | flops 17179869184 | bytes 50000000 | tf_op jit(solution)/shard_map/expert_first/pallas_call | solution.py:385
  314.6 53.7 %all-to-all-done.3.w_ref.w_out_ref = bf16[16,2,128,512]{3,2,1,0:T(8,128)(2,1)} async-done(((bf16[16,2,128,512]{3,2,1,0:T(8,128)(2,1)}), bf16[16,2,128,512]{3,2,1,0:T(8,128)(2,1)}, u32[]{:S(2)}, u32[]{:S(2)}) %all-to-all-start.3) | async-done | bytes 4194336 | tf_op jit(solution)/shard_map/all_to_all | solution.py:549
  368.3 15.5 %expert_second.1 = bf16[16,2,128,512]{3,2,1,0:T(8,128)(2,1)} custom-call(bf16[2,2048,2048]{2,1,0:T(8,128)(2,1)} %get-tuple-element.29.g_ref, bf16[16,2,128,512]{3,2,1,0:T(8,128)(2,1)} %all-to-all-done.3.w_ref.w_out_ref), custom_call_target="tpu_custom_call" | custom-call | flops 8589934592 | bytes 26000000 | tf_op jit(solution)/shard_map/expert_second/pallas_call | solution.py:428
  383.9 4.4 all-to-all-start.4
  388.3 40.1 %expert_back.1 = (bf16[16,2,128,512]{3,2,1,0:T(8,128)(2,1)}, bf16[16,2,32,2048]{3,2,1,0:T(8,128)(2,1)}) custom-call(bf16[16,2,128,512]{3,2,1,0:T(8,128)(2,1)} %bitcast.13.h_ref, bf16[16,2,128,512]{3,2,1,0:T(8,128)(2,1)} %get-tuple-element.34.dye_ref, bf16[2,2048,2048]{2,1,0:T(8,128)(2,1)} %get-tuple-element.35.slope_ref, ...), custom_call_target="tpu_custom_call" | custom-call | flops 25769803776 | bytes 40000000 | tf_op jit(solution)/shard_map/expert_back/pallas_call | solution.py:481
  428.4 14.9 %all-to-all-done.4.y_ref = bf16[16,256,512]{2,1,0:T(8,128)(2,1)} async-done(((bf16[16,256,512]{2,1,0:T(8,128)(2,1)}), bf16[16,256,512]{2,1,0:T(8,128)(2,1)}, u32[]{:S(2)}, u32[]{:S(2)}) %all-to-all-start.4) | async-done | bytes 4194336 | tf_op jit(solution)/shard_map/all_to_all | solution.py:558
  443.2 51.7 %all_to_all.45.rows_ref = bf16[16,256,512]{2,1,0:T(8,128)(2,1)} all-to-all(bf16[16,256,512]{2,1,0:T(8,128)(2,1)} %bitcast.53), channel_id=1, replica_groups=mesh['replica'=2,'part'=8,'expert'=2] {'part','expert'}, dimensions={0} | all-to-all | bytes 8388608 | tf_op jit(solution)/shard_map/all_to_all | solution.py:558
  494.9 7.1 all-to-all-start.7
  502.0 0.3 copy.66
  502.3 0.2 copy.65
  502.5 0.1 fusion
  502.6 0.8 pad.17.keys_ref
  503.3 20.5 %gather.1 = f32[1040,512]{1,0:T(8,128)} custom-call(bf16[1040,128]{1,0:T(8,128)(2,1)} %pad.17.keys_ref, bf16[16,256,512]{2,1,0:T(8,128)(2,1)} %all_to_all.45.rows_ref), custom_call_target="tpu_custom_call" | custom-call | flops 6000000000 | bytes 7000000 | tf_op jit(solution)/shard_map/gather/pallas_call | solution.py:322
  523.9 30.8 %combine.1 = (bf16[1040,512]{1,0:T(8,128)(2,1)}, f32[1040,128]{1,0:T(8,128)}) custom-call(bf16[1040,128]{1,0:T(8,128)(2,1)} %pad.17.keys_ref, f32[1040,128]{1,0:T(8,128)} %bitcast.65, bf16[1040,512]{1,0:T(8,128)(2,1)} %bitcast.56, f32[1040,512]{1,0:T(8,128)} %bitcast.62, bf16[16,256,512]{2,1,0:T(8,128)(2,1)} %all-to-all-done.4.y_ref), custom_call_target="tpu_custom_call" | custom-call | flops 12000000000 | bytes 10000000 | tf_op jit(solution)/shard_map/combine/pallas_call | solution.py:285
  554.7 30.2 %attend_back.1 = (f32[5,208,512]{2,1,0:T(8,128)}, bf16[512,2176]{1,0:T(8,128)(2,1)}) custom-call(bf16[5,208,512]{2,1,0:T(8,128)(2,1)} %pad.18.x_ref, bf16[512,2176]{1,0:T(8,128)(2,1)} %all-gather.2.cloned.1.call-done.w_ref, bf16[5,208,1536]{2,1,0:T(8,128)(2,1)} %get-tuple-element.31.qkv_ref, bf16[5,208,512]{2,1,0:T(8,128)(2,1)} %get-tuple-element.32.ctx_ref, ...), custom_call_target="tpu_custom_call" | custom-call | flops 20000000000 | bytes 16000000 | tf_op jit(solution)/shard_map/attend_back/pallas_call | solution.py:199
  584.9 9.6 %all-to-all-done.7 = bf16[16,2,32,2048]{3,2,1,0:T(8,128)(2,1)} async-done(((bf16[16,2,32,2048]{3,2,1,0:T(8,128)(2,1)}), bf16[16,2,32,2048]{3,2,1,0:T(8,128)(2,1)}, u32[]{:S(2)}, u32[]{:S(2)}) %all-to-all-start.7) | async-done | bytes 4194336 | tf_op jit(solution)/shard_map/all_to_all | solution.py:552
  594.5 55.0 %all_to_all.46 = bf16[16,32,2176]{2,1,0:T(8,128)(2,1)S(1)} all-to-all(bf16[16,32,2176]{2,1,0:T(8,128)(2,1)} %bitcast.54), channel_id=1, replica_groups=mesh['replica'=2,'part'=8,'expert'=2] {'replica','part'}, dimensions={0} | all-to-all | bytes 4456448 | tf_op jit(solution)/shard_map/all_to_all | solution.py:604
  649.5 6.3 all-to-all-start.8
  655.7 0.3 all-reduce.6.cloned.1.call-start
  656.0 5.6 convert_reduce_fusion.1
  661.6 1.0 reduce_sum.30
  662.6 85.6 %all-to-all-done.8 = bf16[16,2,128,512]{3,2,1,0:T(8,128)(2,1)} async-done(((bf16[16,2,128,512]{3,2,1,0:T(8,128)(2,1)}), bf16[16,2,128,512]{3,2,1,0:T(8,128)(2,1)}, u32[]{:S(2)}, u32[]{:S(2)}) %all-to-all-start.8) | async-done | bytes 4194336 | tf_op jit(solution)/shard_map/all_to_all | solution.py:552
  748.2 5.5 convert_reduce_fusion
  753.8 1.2 reshape.159
  755.0 1.7 slice.32
  756.8 1.5 reshape.163
  758.3 0.9 convert_element_type.37
  759.2 0.7 slice_reduce_fusion
  760.0 0.7 slice.48
  760.8 0.7 copy.76
  761.5 1.6 slice.44
  763.0 1.4 slice.45
  (36 shorter events, 0.3 us)
Async XLA Ops:
  26.7 60.8 %all-to-all-start.1 = ((bf16[16,256,512]{2,1,0:T(8,128)(2,1)}), bf16[16,256,512]{2,1,0:T(8,128)(2,1)}, u32[]{:S(2)}, u32[]{:S(2)}) async-start(bf16[16,256,512]{2,1,0:T(8,128)(2,1)} %dispatch.3), calls=%async_computation.1 | async-start | bytes 8388608 | tf_op jit(solution)/shard_map/all_to_all | solution.py:558
  37.1 56.5 %copy-start.2 = (f32[32,1536]{1,0:T(8,128)S(1)}, f32[32,1536]{1,0:T(8,128)}, u32[]{:S(2)}) copy-start(f32[32,1536]{1,0:T(8,128)} %param.18) | copy-start | bytes 589828
  37.1 56.5 %copy-start.3 = (f32[32,512]{1,0:T(8,128)S(1)}, f32[32,512]{1,0:T(8,128)}, u32[]{:S(2)}) copy-start(f32[32,512]{1,0:T(8,128)} %param.19) | copy-start | bytes 196612
  37.1 56.5 %copy-start.4 = (f32[32,32]{1,0:T(8,128)S(1)}, f32[32,32]{1,0:T(8,128)}, u32[]{:S(2)}) copy-start(f32[32,32]{1,0:T(8,128)} %param.22) | copy-start | bytes 12292
  37.1 56.7 %copy-start.5 = (f32[32]{0:T(128)S(1)}, f32[32]{0:T(128)}, u32[]{:S(2)}) copy-start(f32[32]{0:T(128)} %param.16) | copy-start | bytes 388
  37.1 56.8 %copy-start.6 = (f32[32]{0:T(128)S(1)}, f32[32]{0:T(128)}, u32[]{:S(2)}) copy-start(f32[32]{0:T(128)} %param.17) | copy-start | bytes 388
  37.1 56.9 %copy-start.7 = (f32[32]{0:T(128)S(1)}, f32[32]{0:T(128)}, u32[]{:S(2)}) copy-start(f32[32]{0:T(128)} %param.20) | copy-start | bytes 388
  37.1 57.0 %copy-start.8 = (f32[32]{0:T(128)S(1)}, f32[32]{0:T(128)}, u32[]{:S(2)}) copy-start(f32[32]{0:T(128)} %param.21) | copy-start | bytes 388
  37.1 57.9 %copy-start = (bf16[985,512]{1,0:T(8,128)(2,1)S(1)}, bf16[985,512]{1,0:T(8,128)(2,1)}, u32[]{:S(2)}) copy-start(bf16[985,512]{1,0:T(8,128)(2,1)} %param.14) | copy-start | bytes 3025924
  87.5 118.8 %all-to-all-start.2 = ((bf16[16,2,32,2048]{3,2,1,0:T(8,128)(2,1)}), bf16[16,2,32,2048]{3,2,1,0:T(8,128)(2,1)}, u32[]{:S(2)}, u32[]{:S(2)}) async-start(bf16[16,2,32,2048]{3,2,1,0:T(8,128)(2,1)} %pad_maximum_fusion), calls=%async_computation.2 | async-start | bytes 8388608 | tf_op jit(solution)/shard_map/all_to_all | solution.py:549
  93.5 85.8 %all-gather.2.cloned.1.call-start = ((), (), s32[]{:S(2)}) async-start(), calls=%async_computation.9 | async-start | bytes 2367488 | tf_op jit(solution)/shard_map/all_gather | solution.py:544
  206.3 62.4 %all-to-all-start = ((bf16[16,256,512]{2,1,0:T(8,128)(2,1)}), bf16[16,256,512]{2,1,0:T(8,128)(2,1)}, u32[]{:S(2)}, u32[]{:S(2)}) async-start(bf16[16,256,512]{2,1,0:T(8,128)(2,1)} %dispatch.2), calls=%async_computation | async-start | bytes 8388608 | tf_op jit(solution)/shard_map/all_to_all | solution.py:558
  268.7 99.6 %all-to-all-start.3 = ((bf16[16,2,128,512]{3,2,1,0:T(8,128)(2,1)}), bf16[16,2,128,512]{3,2,1,0:T(8,128)(2,1)}, u32[]{:S(2)}, u32[]{:S(2)}) async-start(bf16[16,2,128,512]{3,2,1,0:T(8,128)(2,1)} %pad_maximum_fusion.1), calls=%async_computation.3 | async-start | bytes 8388608 | tf_op jit(solution)/shard_map/all_to_all | solution.py:549
  383.9 59.4 %all-to-all-start.4 = ((bf16[16,256,512]{2,1,0:T(8,128)(2,1)}), bf16[16,256,512]{2,1,0:T(8,128)(2,1)}, u32[]{:S(2)}, u32[]{:S(2)}) async-start(bf16[16,256,512]{2,1,0:T(8,128)(2,1)} %bitcast.52), calls=%async_computation.4 | async-start | bytes 8388608 | tf_op jit(solution)/shard_map/all_to_all | solution.py:558
  494.9 99.6 %all-to-all-start.7 = ((bf16[16,2,32,2048]{3,2,1,0:T(8,128)(2,1)}), bf16[16,2,32,2048]{3,2,1,0:T(8,128)(2,1)}, u32[]{:S(2)}, u32[]{:S(2)}) async-start(bf16[16,2,32,2048]{3,2,1,0:T(8,128)(2,1)} %get-tuple-element.39), calls=%async_computation.7 | async-start | bytes 8388608 | tf_op jit(solution)/shard_map/all_to_all | solution.py:552
  649.5 98.7 %all-to-all-start.8 = ((bf16[16,2,128,512]{3,2,1,0:T(8,128)(2,1)}), bf16[16,2,128,512]{3,2,1,0:T(8,128)(2,1)}, u32[]{:S(2)}, u32[]{:S(2)}) async-start(bf16[16,2,128,512]{3,2,1,0:T(8,128)(2,1)} %get-tuple-element.40), calls=%async_computation.8 | async-start | bytes 8388608 | tf_op jit(solution)/shard_map/all_to_all | solution.py:552
  655.7 102.6 %all-reduce.6.cloned.1.call-start = ((), (), s32[]{:S(2)}) async-start(), calls=%async_computation.10 | async-start | bytes 278528 | tf_op jit(solution)/shard_map/psum | solution.py:606
  748.2 5.5 copy-start.1
Sparse Core Ops, SparseCore 0:
  97.2 82.0 all-gather.1
  662.8 21.1 all-reduce.5

commit v3 on v2

v3 whole, which is shorter than its diff:
```python
from functools import partial

import jax
import jax.numpy as jnp
from jax import lax
from jax.experimental import pallas as pl
from jax.experimental.pallas import tpu as pltpu
from jax.sharding import Mesh
from jax.sharding import PartitionSpec as P

D = 512
HEADS = 8
EXPERTS = 32
SEQ = 197
CAP = 128
ROWS = 208
HEAD = D // HEADS
LANES = 128
QKV = 3 * D
PACKED = QKV + D + LANES
epsilon = 1e-06
low = jnp.bfloat16
full = jnp.float32
MESH = pl.DeviceIdType.MESH
BIG = 63 * 1024 * 1024


def dot(left, right):
    return jnp.dot(left, right, preferred_element_type=full)


def dot_rt(left, right):
    return lax.dot_general(left, right, (((1,), (1,)), ((), ())), preferred_element_type=full)


def dot_lt(left, right):
    return lax.dot_general(left, right, (((0,), (0,)), ((), ())), preferred_element_type=full)


def lanes_of(shape):
    return lax.broadcasted_iota(jnp.int32, shape, len(shape) - 1)


def normed_rows(values):
    center = values - jnp.mean(values, axis=-1, keepdims=True)
    factor = lax.rsqrt(jnp.mean(center * center, axis=-1, keepdims=True) + epsilon)
    return center * factor, factor


def norm_back(normed, factor, gain_vec, upstream):
    scaled = upstream * gain_vec
    return factor * (
        scaled
        - jnp.mean(scaled, axis=-1, keepdims=True)
        - normed * jnp.mean(scaled * normed, axis=-1, keepdims=True)
    )


def norm_vectors(weights_ref):
    rows = weights_ref[:, QKV + D :].astype(full).T
    return [rows[EXPERTS + i : EXPERTS + i + 1] for i in range(4)]


def halves(pair):
    first = lanes_of(pair.shape) < HEAD
    zero = jnp.zeros_like(pair)
    return jnp.where(first, pair, zero), jnp.where(first, zero, pair)


def head_probs(query, key_pair):
    scores = dot_rt(query, key_pair) * (HEAD**-0.5)
    scores = jnp.where(lanes_of(scores.shape) < SEQ, scores, -1e30)
    grown = jnp.exp(scores - jnp.max(scores, axis=-1, keepdims=True))
    return grown / jnp.sum(grown, axis=-1, keepdims=True)


def attend_kernel(x_ref, w_ref, order_ref, qkv_ref, ctx_ref, r_ref, h_ref, probs_ref):
    gain_one, bias_one, gain_two, bias_two = norm_vectors(w_ref)
    x = x_ref[0].astype(full)
    normed, _ = normed_rows(x)
    attn_in = (normed * gain_one + bias_one).astype(low)
    qkv_ref[0] = dot(attn_in, w_ref[:, :QKV]).astype(low)
    for pair in range(HEADS // 2):
        at = pair * LANES
        query = halves(qkv_ref[0, :, at : at + LANES])
        key = qkv_ref[0, :, D + at : D + at + LANES]
        value = halves(qkv_ref[0, :, 2 * D + at : 2 * D + at + LANES])
        total = None
        for i in range(2):
            part = dot(head_probs(query[i], key).astype(low), value[i])
            total = part if total is None else total + part
        ctx_ref[0, :, at : at + LANES] = total.astype(low)
    r = x + dot(ctx_ref[0], w_ref[:, QKV : QKV + D])
    r_ref[0] = r
    normed, _ = normed_rows(r)
    h = (normed * gain_two + bias_two).astype(low)
    h_ref[0] = h
    logits = dot(h, dot(w_ref[:, QKV + D :], order_ref[...]).astype(low))
    logits = jnp.where(lanes_of(logits.shape) < EXPERTS, logits, -1e30)
    grown = jnp.exp(logits - jnp.max(logits, axis=-1, keepdims=True))
    probs_ref[0] = grown / jnp.sum(grown, axis=-1, keepdims=True)


def image_spec(width):
    return pl.BlockSpec((1, ROWS, width), lambda i: (i, 0, 0))


def whole_spec(shape):
    return pl.BlockSpec(shape, lambda *_: (0,) * len(shape))


def params(n):
    return pltpu.CompilerParams(
        dimension_semantics=("arbitrary",) * n, vmem_limit_bytes=BIG
    )


def attend(x, weights, order):
    images = x.shape[0]
    shapes = ((QKV, low), (D, low), (D, full), (D, low), (LANES, full))
    return pl.pallas_call(
        attend_kernel,
        grid=(images,),
        in_specs=[image_spec(D), whole_spec(weights.shape), whole_spec(order.shape)],
        out_specs=[image_spec(width) for width, _ in shapes],
        out_shape=[jax.ShapeDtypeStruct((images, ROWS, w), t) for w, t in shapes],
        compiler_params=params(1),
        cost_estimate=pl.CostEstimate(
            flops=8 * 10**9, bytes_accessed=12 * 10**6, transcendentals=2 * 10**6
        ),
        name="attend",
    )(x, weights, order)


def attend_back_kernel(
    images, x_ref, w_ref, order_ref, qkv_ref, ctx_ref, r_ref, h_ref, probs_ref, dprobs_ref, dh_ref, dy_ref,
    dx_ref, grads_ref, dqkv_ref, qkv_acc, proj_acc, router_acc, norm_acc,
):
    step = pl.program_id(0)

    @pl.when(step == 0)
    def _():
        qkv_acc[...] = jnp.zeros_like(qkv_acc)
        proj_acc[...] = jnp.zeros_like(proj_acc)
        router_acc[...] = jnp.zeros_like(router_acc)
        norm_acc[...] = jnp.zeros_like(norm_acc)

    gain_one, bias_one, gain_two, _ = norm_vectors(w_ref)
    probs, dprobs = probs_ref[0], dprobs_ref[0]
    dlogits = (probs * (dprobs - jnp.sum(probs * dprobs, axis=-1, keepdims=True))).astype(low)
    router_acc[...] += dot_lt(h_ref[0], dlogits)
    router = dot(w_ref[:, QKV + D :], order_ref[...]).astype(low)
    dh = dh_ref[0] + dot_rt(dlogits, router)
    normed, factor = normed_rows(r_ref[0])
    norm_acc[2:3] += jnp.sum(dh * normed, axis=0, keepdims=True)
    norm_acc[3:4] += jnp.sum(dh, axis=0, keepdims=True)
    dr = dy_ref[0].astype(full) + norm_back(normed, factor, gain_two, dh)
    dattended = dr.astype(low)
    proj_acc[...] += dot_lt(ctx_ref[0], dattended)
    dctx = dot_rt(dattended, w_ref[:, QKV : QKV + D]).astype(low)
    for pair in range(HEADS // 2):
        at = pair * LANES
        query = halves(qkv_ref[0, :, at : at + LANES])
        key = qkv_ref[0, :, D + at : D + at + LANES]
        keys = halves(key)
        value = qkv_ref[0, :, 2 * D + at : 2 * D + at + LANES]
        dhead = halves(dctx[:, at : at + LANES])
        dq = dk = dv = None
        for i in range(2):
            p = head_probs(query[i], key)
            dp = dot_rt(dhead[i], value)
            ds = (p * (dp - jnp.sum(p * dp, axis=-1, keepdims=True))).astype(low)
            parts = dot(ds, keys[i]), dot_lt(ds, query[i]), dot_lt(p.astype(low), dhead[i])
            dq, dk, dv = parts if dq is None else (dq + parts[0], dk + parts[1], dv + parts[2])
        dqkv_ref[:, at : at + LANES] = (dq * HEAD**-0.5).astype(low)
        dqkv_ref[:, D + at : D + at + LANES] = (dk * HEAD**-0.5).astype(low)
        dqkv_ref[:, 2 * D + at : 2 * D + at + LANES] = dv.astype(low)
    normed, factor = normed_rows(x_ref[0].astype(full))
    attn_in = (normed * gain_one + bias_one).astype(low)
    qkv_acc[...] += dot_lt(attn_in, dqkv_ref[...])
    da = dot_rt(dqkv_ref[...], w_ref[:, :QKV])
    norm_acc[0:1] += jnp.sum(da * normed, axis=0, keepdims=True)
    norm_acc[1:2] += jnp.sum(da, axis=0, keepdims=True)
    dx_ref[0] = dr + norm_back(normed, factor, gain_one, da)

    @pl.when(step == images - 1)
    def _():
        grads_ref[:, :QKV] = qkv_acc[...].astype(low)
        grads_ref[:, QKV : QKV + D] = proj_acc[...].astype(low)
        columns = norm_acc[...].T
        moved = pltpu.roll(columns, EXPERTS, 1)
        lane = lanes_of(moved.shape)
        tile = jnp.where(lane < EXPERTS, router_acc[...], moved)
        grads_ref[:, QKV + D :] = dot_rt(tile.astype(low), order_ref[...]).astype(low)


def attend_back(x, weights, order, qkv, ctx, r, h, probs, dprobs, dh, dy):
    images = x.shape[0]
    widths = (D, None, None, QKV, D, D, D, LANES, LANES, D, D)
    arrays = (x, weights, order, qkv, ctx, r, h, probs, dprobs, dh, dy)
    return pl.pallas_call(
        partial(attend_back_kernel, images),
        grid=(images,),
        in_specs=[
            whole_spec(a.shape) if w is None else image_spec(w) for a, w in zip(arrays, widths)
        ],
        out_specs=[image_spec(D), whole_spec((D, PACKED))],
        out_shape=[
            jax.ShapeDtypeStruct((images, ROWS, D), full),
            jax.ShapeDtypeStruct((D, PACKED), low),
        ],
        scratch_shapes=[
            pltpu.VMEM((ROWS, QKV), low),
            pltpu.VMEM((D, QKV), full),
            pltpu.VMEM((D, D), full),
            pltpu.VMEM((D, LANES), full),
            pltpu.VMEM((LANES, D), full),
        ],
        compiler_params=params(1),
        cost_estimate=pl.CostEstimate(
            flops=20 * 10**9, bytes_accessed=16 * 10**6, transcendentals=2 * 10**6
        ),
        name="attend_back",
    )(*arrays)


def position(groups):
    return lax.axis_index("part") * groups + lax.axis_index("expert")


def peer_of(groups, k):
    peer = position(groups) ^ k
    return lax.axis_index("replica"), peer // groups, peer % groups


def greet(peers, groups):
    barrier = pltpu.get_barrier_semaphore()
    for k in range(1, peers):
        pl.semaphore_signal(barrier, inc=1, device_id=peer_of(groups, k), device_id_type=MESH)
    pl.semaphore_wait(barrier, peers - 1)


def swap(source, target, sends, receives, groups, k):
    return pltpu.make_async_remote_copy(
        src_ref=source.at[k],
        dst_ref=target.at[k],
        send_sem=sends.at[k],
        recv_sem=receives.at[k],
        device_id=peer_of(groups, k),
        device_id_type=MESH,
    )


def dispatch_kernel(groups, keys_ref, rows_ref, out_ref, blocks, sends, receives, local):
    peers, own, tokens = keys_ref.shape
    slots = lax.broadcasted_iota(jnp.int32, (CAP, tokens), 0).astype(full)
    greet(peers, groups)

    def build(k):
        picks = [(keys_ref[k, i : i + 1] == slots).astype(low) for i in range(own)]
        picks = jnp.concatenate(picks, axis=0) if own > 1 else picks[0]
        blocks[k] = dot(picks, rows_ref[...]).astype(low).reshape(own, CAP, D)

    copies = [swap(blocks, out_ref, sends, receives, groups, k) for k in range(1, peers)]
    for k in range(1, peers):
        build(k)
        copies[k - 1].start()
    build(0)
    mine = pltpu.make_async_copy(blocks.at[0], out_ref.at[0], local)
    mine.start()
    for copy in copies:
        copy.wait()
    mine.wait()


def dispatch(keys, rows, groups, number):
    peers, own, tokens = keys.shape
    shape = (peers, own, CAP, D)
    return pl.pallas_call(
        partial(dispatch_kernel, groups),
        in_specs=[pl.BlockSpec(memory_space=pltpu.VMEM)] * 2,
        out_specs=pl.BlockSpec(memory_space=pl.ANY),
        out_shape=jax.ShapeDtypeStruct(shape, low),
        scratch_shapes=[
            pltpu.VMEM(shape, low),
            pltpu.SemaphoreType.DMA((peers,)),
            pltpu.SemaphoreType.DMA((peers,)),
            pltpu.SemaphoreType.DMA,
        ],
        compiler_params=pltpu.CompilerParams(
            vmem_limit_bytes=BIG, collective_id=number, has_side_effects=True
        ),
        cost_estimate=pl.CostEstimate(
            flops=60 * 10**9, bytes_accessed=5 * 10**6, transcendentals=0
        ),
        name=f"dispatch_{number}",
    )(keys, rows)


def exchange_kernel(groups, blocks_ref, out_ref, sends, receives, local):
    peers = blocks_ref.shape[0]
    greet(peers, groups)
    copies = [swap(blocks_ref, out_ref, sends, receives, groups, k) for k in range(1, peers)]
    for copy in copies:
        copy.start()
    mine = pltpu.make_async_copy(blocks_ref.at[0], out_ref.at[0], local)
    mine.start()
    for copy in copies:
        copy.wait()
    mine.wait()


def exchange(blocks, groups, number):
    peers = blocks.shape[0]
    return pl.pallas_call(
        partial(exchange_kernel, groups),
        in_specs=[pl.BlockSpec(memory_space=pl.ANY)],
        out_specs=pl.BlockSpec(memory_space=pl.ANY),
        out_shape=jax.ShapeDtypeStruct(blocks.shape, low),
        scratch_shapes=[
            pltpu.SemaphoreType.DMA((peers,)),
            pltpu.SemaphoreType.DMA((peers,)),
            pltpu.SemaphoreType.DMA,
        ],
        compiler_params=pltpu.CompilerParams(collective_id=number, has_side_effects=True),
        cost_estimate=pl.CostEstimate(
            flops=60 * 10**9, bytes_accessed=10 * 10**6, transcendentals=0
        ),
        name=f"exchange_{number}",
    )(blocks)


def chooser(own, k):
    shape = (LANES, own * CAP)
    expert = lax.broadcasted_iota(jnp.int32, shape, 0)
    slot = lax.broadcasted_iota(jnp.int32, shape, 1)
    return (expert == k * own + slot // CAP).astype(low)


def combine_kernel(keys_ref, probs_ref, r_ref, y_ref, out_ref):
    peers, own, _, _ = y_ref.shape

    @pl.loop(0, r_ref.shape[0] // ROWS)
    def _(i):
        rows = pl.ds(pl.multiple_of(i * ROWS, ROWS), ROWS)
        slot = (lanes_of((ROWS, own * CAP)) % CAP).astype(full)
        probs = probs_ref[rows].astype(low)
        total = r_ref[rows]
        for k in range(peers):
            spread = chooser(own, k)
            here = dot(keys_ref[rows], spread) == slot
            gate = jnp.where(here, dot(probs, spread), 0.0)
            total = total + dot(gate.astype(low), y_ref[k].reshape(own * CAP, D))
        out_ref[rows] = total.astype(low)


def combine(keys, probs, r, y):
    tokens = keys.shape[0]
    return pl.pallas_call(
        combine_kernel,
        out_shape=jax.ShapeDtypeStruct((tokens, D), low),
        compiler_params=pltpu.CompilerParams(vmem_limit_bytes=BIG),
        cost_estimate=pl.CostEstimate(
            flops=6 * 10**9, bytes_accessed=10 * 10**6, transcendentals=0
        ),
        name="combine",
    )(keys, probs, r, y)


def gather_kernel(keys_ref, back_ref, dh_ref, dprobs_ref):
    peers, own, _, _ = back_ref.shape
    width = own * CAP

    @pl.loop(0, dh_ref.shape[0] // ROWS)
    def _(i):
        rows = pl.ds(pl.multiple_of(i * ROWS, ROWS), ROWS)
        slot = (lanes_of((ROWS, width)) % CAP).astype(full)
        lane = lanes_of((ROWS, LANES))
        total = jnp.zeros((ROWS, D), full)
        dprobs = jnp.zeros((ROWS, LANES), full)
        for k in range(peers):
            here = dot(keys_ref[rows], chooser(own, k)) == slot
            total = total + dot(here.astype(low), back_ref[k, :, :CAP].reshape(width, D))
            dgate = back_ref[k, :, CAP : CAP + 1].astype(full)
            dgate = dgate[:, :, :CAP] + dgate[:, :, CAP : 2 * CAP]
            agreed = [
                jnp.where(here[:, e * CAP : (e + 1) * CAP], dgate[e], 0.0) for e in range(own)
            ]
            for e in range(own):
                column = jnp.sum(agreed[e], axis=-1, keepdims=True)
                dprobs = jnp.where(lane == k * own + e, column, dprobs)
        dh_ref[rows] = total
        dprobs_ref[rows] = dprobs


def gather(keys, back):
    tokens = keys.shape[0]
    return pl.pallas_call(
        gather_kernel,
        out_shape=[
            jax.ShapeDtypeStruct((tokens, D), full),
            jax.ShapeDtypeStruct((tokens, LANES), full),
        ],
        compiler_params=pltpu.CompilerParams(vmem_limit_bytes=BIG),
        cost_estimate=pl.CostEstimate(
            flops=6 * 10**9, bytes_accessed=7 * 10**6, transcendentals=0
        ),
        name="gather",
    )(keys, back)


GELU = 0.7978845608028654
CUBE = 0.044715


def gelu_pair(u):
    square = u * u
    bent = jnp.tanh(u * (GELU * CUBE * square + GELU))
    half = 0.5 * bent + 0.5
    value = u * half
    return value, half + value * (1.0 - bent) * (3.0 * GELU * CUBE * square + GELU)


def first_kernel(h_ref, dy_ref, w_ref, wr_ref, sel_ref, g_ref, slope_ref, dw_ref, gates, dye_t):
    sources = h_ref.shape[0]
    tile = w_ref.shape[3]

    @pl.when(pl.program_id(1) == 0)
    def _():
        for k in range(sources):
            rows = slice(k * CAP, (k + 1) * CAP)
            logits = dot(h_ref[k, 0], wr_ref[...])
            logits = jnp.where(lanes_of(logits.shape) < EXPERTS, logits, -1e30)
            grown = jnp.exp(logits - jnp.max(logits, axis=-1, keepdims=True))
            mine = jnp.sum(grown * sel_ref[0], axis=-1, keepdims=True)
            gate = mine / jnp.sum(grown, axis=-1, keepdims=True)
            gates[rows] = jnp.broadcast_to(gate, (CAP, LANES))
            dye_t[:, rows] = (dy_ref[k, 0].astype(full) * gate).T.astype(low)

    w = w_ref[:, 0].reshape(D, tile)
    for k in range(0, sources, 2):
        rows = slice(k * CAP, (k + 2) * CAP)
        value, slope = gelu_pair(dot(h_ref[k : k + 2, 0].reshape(2 * CAP, D), w))
        g_ref[0, rows] = value.astype(low)
        slope_ref[0, rows] = (slope * gates[rows, :1]).astype(low)
    grad = dot(dye_t[...], g_ref[0]).T
    dw_ref[:, 0] = grad.astype(low).reshape(dw_ref.shape[0], dw_ref.shape[2], D)


def slot_spec(sources):
    return pl.BlockSpec((sources, 1, CAP, D), lambda e, f: (0, e, 0, 0))


def expert_first(h, dy, w_in, w_router, select, tile):
    sources = h.shape[0]
    owners, own, depth, hidden = w_in.shape
    rows = sources * CAP
    per = hidden // owners
    hidden_spec = pl.BlockSpec((1, rows, tile), lambda e, f: (e, 0, f))
    return pl.pallas_call(
        first_kernel,
        grid=(own, hidden // tile),
        in_specs=[
            slot_spec(sources),
            slot_spec(sources),
            pl.BlockSpec((owners, 1, depth, tile), lambda e, f: (0, e, 0, f)),
            whole_spec(w_router.shape),
            pl.BlockSpec((1, 1, LANES), lambda e, f: (e, 0, 0)),
        ],
        out_specs=[
            hidden_spec,
            hidden_spec,
            pl.BlockSpec((tile // per, 1, per, D), lambda e, f: (f, e, 0, 0)),
        ],
        out_shape=[
            jax.ShapeDtypeStruct((own, rows, hidden), low),
            jax.ShapeDtypeStruct((own, rows, hidden), low),
            jax.ShapeDtypeStruct((owners, own, per, D), low),
        ],
        scratch_shapes=[pltpu.VMEM((rows, LANES), full), pltpu.VMEM((D, rows), low)],
        compiler_params=params(2),
        cost_estimate=pl.CostEstimate(
            flops=4 * own * rows * D * hidden,
            bytes_accessed=50 * 10**6,
            transcendentals=own * rows * hidden,
        ),
        name="expert_first",
    )(h, dy, w_in, w_router, select)


def rest_kernel(
    groups, own, steps, dy_ref, h_ref, g_ref, slope_ref, w_in_ref, w_out_ref,
    back_ref, dw_ref, y_ref, du, acc, dgates, dgate_rows, h_t, staged, sends, receives, local,
):
    sources = dy_ref.shape[0]
    tile = slope_ref.shape[2]
    at = pl.program_id(0)
    phase, expert, step = at // (own * steps), at // steps % own, at % steps
    w_in = w_in_ref[:, 0].reshape(D, tile)
    w_out = w_out_ref[:, 0].reshape(tile, D)
    chunk = 2 * CAP

    def copy(k, e):
        return pltpu.make_async_remote_copy(
            src_ref=staged.at[k, e],
            dst_ref=back_ref.at[k, e],
            send_sem=sends.at[k, e],
            recv_sem=receives.at[k, e],
            device_id=peer_of(groups, k),
            device_id_type=MESH,
        )

    def mine(e):
        return pltpu.make_async_copy(staged.at[0, e], back_ref.at[0, e], local.at[e])

    @pl.when(at == 0)
    def _():
        greet(sources, groups)

    @pl.when((phase != 1) & (step == 0))
    def _():
        acc[...] = jnp.zeros_like(acc)

    @pl.when(phase == 0)
    def _():
        @pl.when(step == 0)
        def _():
            dgates[...] = jnp.zeros_like(dgates)

        for k in range(0, sources, 2):
            rows = slice(k * CAP, (k + 2) * CAP)
            dg = dot_rt(dy_ref[k : k + 2, 0].reshape(chunk, D), w_out)
            change = (dg * slope_ref[0, rows].astype(full)).astype(low)
            du[expert * steps + step, rows] = change
            acc[rows] += dot_rt(change, w_in)
            agreed = dg * g_ref[0, rows].astype(full)
            dgates[rows] += sum(agreed[:, i : i + LANES] for i in range(0, tile, LANES))

        @pl.when(step == steps - 1)
        def _():
            sums = dgates[...]
            high = sums.astype(low)
            rest = (sums - high.astype(full)).astype(low)
            ones = jnp.ones((16, LANES), low)
            dgate_rows[...] = dot_rt(ones, high) + dot_rt(ones, rest)
            for k in range(sources):
                rows = slice(k * CAP, (k + 1) * CAP)
                staged[k, expert, :CAP] = acc[rows].astype(low)
                row = dgate_rows[:, rows]
                high = row.astype(low)
                staged[k, expert, CAP:, :CAP] = high
                staged[k, expert, CAP:, CAP : 2 * CAP] = (row - high.astype(full)).astype(low)
                staged[k, expert, CAP:, 2 * CAP :] = jnp.zeros((16, D - 2 * CAP), low)

        for e in range(own):
            @pl.when((step == steps - 1) & (expert == e))
            def _():
                for k in range(1, sources):
                    copy(k, e).start()
                mine(e).start()

    @pl.when(phase == 1)
    def _():
        @pl.when(step == 0)
        def _():
            for k in range(sources):
                h_t[:, k * CAP : (k + 1) * CAP] = h_ref[k, 0].T

        grad = dot(h_t[...], du[expert * steps + step]).astype(low)
        dw_ref[:, 0] = grad.reshape(dw_ref.shape[0], dw_ref.shape[2], tile)

    @pl.when(phase == 2)
    def _():
        for k in range(0, sources, 2):
            rows = slice(k * CAP, (k + 2) * CAP)
            acc[rows] += dot(g_ref[0, rows], w_out)

        @pl.when(step == steps - 1)
        def _():
            y_ref[:, 0] = acc[...].astype(low).reshape(sources, CAP, D)

    @pl.when(at == 3 * own * steps - 1)
    def _():
        for e in range(own):
            for k in range(1, sources):
                copy(k, e).wait()
            mine(e).wait()


def expert_rest(dy, h, g, slope, w_in, w_out, tile, groups, number):
    sources, own, _, _ = dy.shape
    owners, _, depth, hidden = w_in.shape
    rows = sources * CAP
    per = hidden // owners
    steps = hidden // tile
    last = own * steps - 1

    def during(phases):
        def find(at):
            if 0 in phases and 2 in phases:
                inside = jnp.where(at // (last + 1) == 1, last, at % (last + 1))
            else:
                inside = jnp.clip(at - phases[0] * (last + 1), 0, last)
            return inside // steps, inside % steps

        return find

    def spec(shape, phases, index, buffers=2):
        return pl.BlockSpec(
            shape, lambda at: index(*during(phases)(at)), pipeline_mode=pl.Buffered(buffers)
        )

    token, hidden_at = (sources, 1, CAP, D), (1, rows, tile)
    whole_expert = lambda e, f: (0, e, 0, 0)
    in_tile = lambda e, f: (0, e, 0, f)
    return pl.pallas_call(
        partial(rest_kernel, groups, own, steps),
        grid=(3 * own * steps,),
        in_specs=[
            spec(token, (0,), whole_expert, 1),
            spec(token, (1,), whole_expert, 1),
            spec(hidden_at, (0, 2), lambda e, f: (e, 0, f)),
            spec(hidden_at, (0,), lambda e, f: (e, 0, f)),
            spec((owners, 1, depth, tile), (0,), in_tile),
            spec((tile // per, 1, per, D), (0, 2), lambda e, f: (f, e, 0, 0)),
        ],
        out_specs=[
            pl.BlockSpec(memory_space=pl.ANY),
            spec((owners, 1, depth, tile), (1,), in_tile),
            spec(token, (2,), whole_expert),
        ],
        out_shape=[
            jax.ShapeDtypeStruct((sources, own, CAP + 16, D), low),
            jax.ShapeDtypeStruct(w_in.shape, low),
            jax.ShapeDtypeStruct(dy.shape, low),
        ],
        scratch_shapes=[
            pltpu.VMEM((own * steps, rows, tile), low),
            pltpu.VMEM((rows, D), full),
            pltpu.VMEM((rows, LANES), full),
            pltpu.VMEM((16, rows), full),
            pltpu.VMEM((D, rows), low),
            pltpu.VMEM((sources, own, CAP + 16, D), low),
            pltpu.SemaphoreType.DMA((sources, own)),
            pltpu.SemaphoreType.DMA((sources, own)),
            pltpu.SemaphoreType.DMA((own,)),
        ],
        compiler_params=pltpu.CompilerParams(
            dimension_semantics=("arbitrary",),
            vmem_limit_bytes=BIG,
            collective_id=number,
            has_side_effects=True,
        ),
        cost_estimate=pl.CostEstimate(
            flops=8 * own * rows * D * hidden, bytes_accessed=60 * 10**6, transcendentals=0
        ),
        name="expert_rest",
    )(dy, h, g, slope, w_in, w_out)


ALL = ("replica", "part")


def body(
    tokens,
    choices,
    ln1_gain,
    ln1_bias,
    w_qkv,
    w_proj,
    ln2_gain,
    ln2_bias,
    w_router,
    w_expert_in,
    w_expert_out,
    cotangent,
):
    replicas, parts, groups = (lax.axis_size(name) for name in ("replica", "part", "expert"))
    owners = replicas * parts
    peers = parts * groups
    own = EXPERTS // peers
    images = tokens.shape[0] // SEQ
    count = images * ROWS
    tile = 512 * 16 // peers

    small_rows = w_router.shape[0]
    placed_router = (
        w_router.reshape(small_rows, groups, parts, own).transpose(0, 2, 1, 3).reshape(small_rows, EXPERTS)
    )
    vectors = jnp.stack([ln1_gain, ln1_bias, ln2_gain, ln2_bias], axis=1)
    packed = jnp.concatenate(
        [w_qkv, w_proj, placed_router, vectors, jnp.zeros((small_rows, LANES - EXPERTS - 4), full)],
        axis=1,
    ).astype(low)
    weights = lax.all_gather(packed, ALL, axis=0, tiled=True)

    def spread(master):
        pieces = master.astype(low).reshape(parts, own, *master.shape[1:])
        pieces = jnp.concatenate([pieces] * replicas, axis=0)
        return lax.all_to_all(pieces, ALL, split_axis=0, concat_axis=0, tiled=True)

    def collect(grad):
        pieces = lax.all_to_all(grad, ALL, split_axis=0, concat_axis=0, tiled=True)
        pieces = pieces.reshape(replicas, parts * own, *grad.shape[2:])
        return jnp.sum(pieces.astype(full), axis=0)

    me = position(groups)

    def padded(rows, fill=0):
        rows = rows.reshape(images, SEQ, rows.shape[1])
        return jnp.pad(rows, ((0, 0), (0, ROWS - SEQ), (0, 0)), constant_values=fill)

    x = padded(tokens)
    dy = padded(cotangent)
    picks = padded(choices, -1).reshape(count, 2)
    column = jnp.arange(EXPERTS)
    place = (me ^ (column // own)) * own + column % own
    expert = (place // own % groups) * (parts * own) + place // (groups * own) * own + place % own
    lane = jnp.arange(LANES)
    order = jnp.where(lane < EXPERTS, jnp.pad(place, (0, LANES - EXPERTS)), lane)
    order = (lane[:, None] == order[None, :]).astype(low)
    named = (picks[:, :, None] == expert[None, None, :]).any(axis=1)
    row = jnp.arange(count)
    slots = dot((row[None, :] < row[:, None]).astype(low), named.astype(low))
    keys = jnp.where(named, slots, -1.0)
    key_rows = keys.T.reshape(peers, own, count)
    key_columns = jnp.pad(keys, ((0, 0), (0, LANES - EXPERTS)), constant_values=-1).astype(low)

    first_weight = spread(w_expert_in)
    dy_slots = dispatch(key_rows, dy.reshape(count, D), groups, 0)
    qkv, ctx, r, h, probs = attend(x, weights, order)
    w_expert_out, h = lax.optimization_barrier((w_expert_out, h))
    second_weight = spread(w_expert_out)
    h_slots = dispatch(key_rows, h.reshape(count, D), groups, 1)
    select = ((me * own + jnp.arange(own))[:, None, None] == lane[None, None, :]).astype(full)
    g, slope, dw_second = expert_first(
        h_slots, dy_slots, first_weight, weights[:, QKV + D :], select, tile
    )
    back, dw_first, y = expert_rest(
        dy_slots, h_slots, g, slope, first_weight, second_weight, tile, groups, 2
    )
    y = exchange(y, groups, 3)
    expert_out_grad = collect(dw_second)
    expert_in_grad = collect(dw_first)
    dh, dprobs = gather(key_columns, back)
    dx, grads = attend_back(
        x, weights, order, qkv, ctx, r, h, probs,
        dprobs.reshape(images, ROWS, LANES), dh.reshape(images, ROWS, D), dy,
    )
    output = combine(key_columns, probs.reshape(count, LANES), r.reshape(count, D), y)
    grads = lax.psum_scatter(grads, ALL, scatter_dimension=0, tiled=True)
    grads = lax.psum(grads, "expert").astype(full)
    router_grad = (
        grads[:, QKV + D : QKV + D + EXPERTS]
        .reshape(small_rows, parts, groups, own)
        .transpose(0, 2, 1, 3)
        .reshape(small_rows, EXPERTS)
    )
    norms = [grads[:, QKV + D + EXPERTS + i] for i in range(4)]

    def unpadded(rows):
        return rows.reshape(images, ROWS, D)[:, :SEQ].reshape(images * SEQ, D)

    return (
        unpadded(output),
        unpadded(dx),
        norms[0],
        norms[1],
        grads[:, :QKV],
        grads[:, QKV : QKV + D],
        norms[2],
        norms[3],
        router_grad,
        expert_in_grad,
        expert_out_grad,
    )


def solution(mesh):
    dp, groups = mesh.shape["dp"], mesh.shape["expert"]
    parts = min(EXPERTS // groups, dp // 2)
    mesh = Mesh(mesh.devices.reshape(dp // parts, parts, groups), ("replica", "part", "expert"))
    rows = P(("replica", "part", "expert"), None)
    vector, matrix = P(ALL), P(ALL, None)
    experts = P("expert", ALL, None)
    return jax.shard_map(
        body,
        mesh=mesh,
        in_specs=(
            rows, rows, vector, vector, matrix, matrix, vector, vector, matrix, experts, experts, rows,
        ),
        out_specs=(
            rows, rows, vector, vector, matrix, matrix, vector, vector, matrix, experts, experts,
        ),
        check_vma=False,
    )
```

time: 774 us -> 715 us (0.924)
  Pallas kernels: 213 us -> 539 us
  waiting for transfers between devices: 347 us -> 78.2 us
  blocking collectives: 107 us -> 0 us
  starting transfers between devices: 44.2 us -> 31.7 us
    pallas_call x7, Pallas kernels: 168 us -> 493 us  [the longest x2 182 us: dispatch(): pl.pallas_call(partial(dispatch_kernel, groups), in_specs=[pl.BlockSpec(m...]
    all_to_all x3 -> x0, waiting for transfers between devices: 115 us -> none  [exchange(): lax.all_to_all(rows, ('part', 'expert'), split_axis=0, concat_axis=0, til...]
    all_to_all x2 -> x0, blocking collectives: 107 us -> none  [the longest x1 55 us: body(): grads = lax.all_to_all(grads, ALL, split_axis=0, concat_axis=0, tiled=True)]
    all_to_all x2, waiting for transfers between devices: 95.2 us -> 0.01 us  [collect(): pieces = lax.all_to_all(grad, ALL, split_axis=0, concat_axis=0, tiled=True)]
    all_to_all x2, waiting for transfers between devices: 53.7 us -> 0.34 us  [spread(): return lax.all_to_all(pieces, ALL, split_axis=0, concat_axis=0, tiled=True)]
    all_to_all x3 -> x0, starting transfers between devices: 17.3 us -> none  [exchange(): lax.all_to_all(rows, ('part', 'expert'), split_axis=0, concat_axis=0, til...]
  transfers between devices with their start and end apart: 9 -> 7, of which waited for: 7 -> 2; matrix products, arithmetic and copies ran while one was open for 4% -> 5% of each run, Pallas kernels for 24% -> 76%
where the time goes in v3:
time: 715 us; the launch traced here: 705 us
  Pallas kernels  539 us (75%)
  waiting for transfers between devices  78.2 us (11%)
  starting transfers between devices  31.7 us (4%)
  other arithmetic  23.1 us (3%)
  local copies, waits for them, and re-layouts  17.7 us (2%)
  between operations  14.3 us (2%)
    pallas_call x2, Pallas kernels, dispatch(): pl.pallas_call(partial(dispatch_kernel, groups), in_specs=[pl.BlockSpec(m...  182 us
    pallas_call x1, Pallas kernels, expert_rest(): pl.pallas_call(partial(rest_kernel, groups, own, steps), grid=(3 * own *...  130 us
    pallas_call x1, Pallas kernels, exchange(): pl.pallas_call(partial(exchange_kernel, groups), in_specs=[pl.BlockSpec(m...  101 us
    all_gather x1, waiting for transfers between devices, body(): weights = lax.all_gather(packed, ALL, axis=0, tiled=True)  77.8 us
    pallas_call x1, Pallas kernels, expert_first(): pl.pallas_call(first_kernel, grid=(own, hidden // tile), in_specs=[slot_s...  39.8 us
    pallas_call x1, Pallas kernels, attend_back(): pl.pallas_call(partial(attend_back_kernel, images), grid=(images,), in_sp...  31.1 us
    pallas_call x1, Pallas kernels, combine(): pl.pallas_call(combine_kernel, out_shape=jax.ShapeDtypeStruct((tokens, D)...  20.1 us
    pallas_call x1, Pallas kernels, gather(): pl.pallas_call(gather_kernel, out_shape=[jax.ShapeDtypeStruct((tokens, D)...  19.7 us
  transfers between devices with their start and end apart: 7, of which 2 were waited for; matrix products, arithmetic and copies ran while one was open for 5% of the time, Pallas kernels for 76%

profile of v3, /device:TPU:13, one launch (start us, length us, event | category | flops | bytes accessed | tf_op | source)
XLA Modules:
  0.0 705.3 jit_solution(11078279565876302748)
XLA Ops:
  7.2 2.5 convert_element_type.37
  9.7 2.4 pad_maximum_fusion
  12.1 0.0 copy-start.6
  12.1 0.0 copy-start.5
  12.1 0.0 copy-start.4
  12.1 6.7 all-to-all-start
  18.8 0.0 all-gather.2.cloned.1.call-start
  18.9 0.1 copy.54
  19.0 0.1 copy.53
  19.1 0.1 copy.52
  19.2 0.1 copy.51
  19.3 0.1 copy.48
  19.4 0.1 copy.50
  19.6 0.8 concatenate.10
  20.3 0.0 all-gather.2.cloned.1.call-update
  20.4 0.1 reshape.203
  20.5 0.1 eq.53
  20.6 0.1 compare_reduce_fusion
  20.7 0.3 copy.46
  21.0 1.5 fusion.10
  22.5 0.2 copy.55
  22.7 0.8 reshape.209.keys_ref
  23.4 0.3 reshape.204
  23.7 1.1 pad.22.x_ref
  24.8 0.3 reshape.210
  25.1 1.1 pad.24.dy_ref
  26.2 0.6 fusion.2.order_ref
  26.8 77.8 %all-gather.2.cloned.1.call-done.w_ref = bf16[512,2176]{1,0:T(8,128)(2,1)} async-done(((bf16[32,2176]{1,0:T(8,128)(2,1)}), bf16[512,2176]{1,0:T(8,128)(2,1)}) %all-gather.2.cloned.1.call-update) | async-done | bytes 2228240 | tf_op jit(solution)/shard_map/all_gather | solution.py:695
  104.6 14.9 %attend.1 = (bf16[5,208,1536]{2,1,0:T(8,128)(2,1)}, bf16[5,208,512]{2,1,0:T(8,128)(2,1)}, f32[5,208,512]{2,1,0:T(8,128)}, bf16[5,208,512]{2,1,0:T(8,128)(2,1)}, f32[5,208,128]{2,1,0:T(8,128)}) custom-call(bf16[5,208,512]{2,1,0:T(8,128)(2,1)} %pad.22.x_ref, bf16[512,2176]{1,0:T(8,128)(2,1)} %all-gather.2.cloned.1.call-done.w_ref, ...), custom_call_target="tpu_custom_call" | custom-call | flops 8000000000 | bytes 12000000 | tf_op jit(solution)/shard_map/attend/pallas_call | solution.py:121
  119.5 2.5 convert_element_type.39
  122.0 2.4 pad_maximum_fusion.1
  124.4 0.3 all-to-all-done.w_ref.w_in_ref
  124.7 8.5 %all-to-all-start.1 = ((bf16[16,2,128,512]{3,2,1,0:T(8,128)(2,1)}), bf16[16,2,128,512]{3,2,1,0:T(8,128)(2,1)}, u32[]{:S(2)}, u32[]{:S(2)}) async-start(bf16[16,2,128,512]{3,2,1,0:T(8,128)(2,1)} %pad_maximum_fusion.1), calls=%async_computation.1 | async-start | bytes 8388608 | tf_op jit(solution)/shard_map/all_to_all | solution.py:700
  133.2 118.9 %dispatch_0.1.dy_ref = bf16[16,2,128,512]{3,2,1,0:T(8,128)(2,1)} custom-call(f32[16,2,1040]{2,1,0:T(2,128)} %reshape.209.keys_ref, bf16[1040,512]{1,0:T(8,128)(2,1)} %bitcast.41), custom_call_target="tpu_custom_call" | custom-call | flops 60000002048 | bytes 5000000 | tf_op jit(solution)/shard_map/dispatch_0/pallas_call | solution.py:279
  252.2 0.6 compare_convert_fusion.sel_ref
  252.8 1.6 slice.40.wr_ref
  254.4 63.1 %dispatch_1.1.h_ref = bf16[16,2,128,512]{3,2,1,0:T(8,128)(2,1)} custom-call(f32[16,2,1040]{2,1,0:T(2,128)} %reshape.209.keys_ref, bf16[1040,512]{1,0:T(8,128)(2,1)} %bitcast.50), custom_call_target="tpu_custom_call" | custom-call | flops 60000002048 | bytes 5000000 | tf_op jit(solution)/shard_map/dispatch_1/pallas_call | solution.py:279
  317.5 39.8 %expert_first.1 = (bf16[2,2048,2048]{2,1,0:T(8,128)(2,1)}, bf16[2,2048,2048]{2,1,0:T(8,128)(2,1)}, bf16[16,2,128,512]{3,2,1,0:T(8,128)(2,1)}) custom-call(bf16[16,2,128,512]{3,2,1,0:T(8,128)(2,1)} %dispatch_1.1.h_ref, bf16[16,2,128,512]{3,2,1,0:T(8,128)(2,1)} %dispatch_0.1.dy_ref, bf16[16,2,32,2048]{3,2,1,0:T(8,128)(2,1)} %all-to-all-done.w_ref.w_in_ref, ...), custom_call_target="tpu_custom_call" | custom-call | flops 17179869184 | bytes 50000000 | tf_op jit(solution)/shard_map/expert_first/pallas_call | solution.py:460
  357.3 6.8 all-to-all-start.3
  364.1 0.8 pad.21.keys_ref
  364.9 129.8 %expert_rest.1 = (bf16[16,2,144,512]{3,2,1,0:T(8,128)(2,1)}, bf16[16,2,32,2048]{3,2,1,0:T(8,128)(2,1)}, bf16[16,2,128,512]{3,2,1,0:T(8,128)(2,1)}) custom-call(bf16[16,2,128,512]{3,2,1,0:T(8,128)(2,1)} %dispatch_0.1.dy_ref, bf16[16,2,128,512]{3,2,1,0:T(8,128)(2,1)} %dispatch_1.1.h_ref, bf16[2,2048,2048]{2,1,0:T(8,128)(2,1)} %get-tuple-element.32.g_ref, ...), custom_call_target="tpu_custom_call" | custom-call | flops 34359738368 | bytes 60000000 | tf_op jit(solution)/shard_map/expert_rest/pallas_call | solution.py:616
  494.7 19.7 %gather.1 = (f32[1040,512]{1,0:T(8,128)}, f32[1040,128]{1,0:T(8,128)}) custom-call(bf16[1040,128]{1,0:T(8,128)(2,1)} %pad.21.keys_ref, bf16[16,2,144,512]{3,2,1,0:T(8,128)(2,1)} %get-tuple-element.38.back_ref), custom_call_target="tpu_custom_call" | custom-call | flops 6000000000 | bytes 7000000 | tf_op jit(solution)/shard_map/gather/pallas_call | solution.py:398
  514.4 9.6 %all-to-all-start.2 = ((bf16[16,2,32,2048]{3,2,1,0:T(8,128)(2,1)}), bf16[16,2,32,2048]{3,2,1,0:T(8,128)(2,1)}, u32[]{:S(2)}, u32[]{:S(2)}) async-start(bf16[16,2,32,2048]{3,2,1,0:T(8,128)(2,1)} %get-tuple-element.43), calls=%async_computation.3 | async-start | bytes 8388608 | tf_op jit(solution)/shard_map/all_to_all | solution.py:703
  524.0 0.0 reduce-scatter.2.cloned.1.call-start
  524.1 31.1 %attend_back.1 = (f32[5,208,512]{2,1,0:T(8,128)}, bf16[512,2176]{1,0:T(8,128)(2,1)}) custom-call(bf16[5,208,512]{2,1,0:T(8,128)(2,1)} %pad.22.x_ref, bf16[512,2176]{1,0:T(8,128)(2,1)} %all-gather.2.cloned.1.call-done.w_ref, bf16[128,128]{1,0:T(8,128)(2,1)} %fusion.2.order_ref, bf16[5,208,1536]{2,1,0:T(8,128)(2,1)} %get-tuple-element.36.qkv_ref, ...), custom_call_target="tpu_custom_call" | custom-call | flops 20000000000 | bytes 16000000 | tf_op jit(solution)/shard_map/attend_back/pallas_call | solution.py:201
  555.1 0.0 reduce-scatter.2.cloned.1.call-update
  555.2 0.0 all-reduce.7.cloned.1.call-start
  555.2 101.2 %exchange_3.1.y_ref = bf16[16,2,128,512]{3,2,1,0:T(8,128)(2,1)} custom-call(bf16[16,2,128,512]{3,2,1,0:T(8,128)(2,1)} %get-tuple-element.35.blocks_ref), custom_call_target="tpu_custom_call" | custom-call | flops 60000002048 | bytes 10000000 | tf_op jit(solution)/shard_map/exchange_3/pallas_call | solution.py:315
  656.4 0.0 reduce-scatter.2.cloned.1.call-done
  656.4 0.0 all-reduce.7.cloned.1.call-update
  656.5 20.1 %combine.1 = bf16[1040,512]{1,0:T(8,128)(2,1)} custom-call(bf16[1040,128]{1,0:T(8,128)(2,1)} %pad.21.keys_ref, f32[1040,128]{1,0:T(8,128)} %bitcast.51, f32[1040,512]{1,0:T(8,128)} %bitcast.48, bf16[16,2,128,512]{3,2,1,0:T(8,128)(2,1)} %exchange_3.1.y_ref), custom_call_target="tpu_custom_call" | custom-call | flops 6000000000 | bytes 10000000 | tf_op jit(solution)/shard_map/combine/pallas_call | solution.py:359
  676.6 1.8 slice.32
  678.5 1.5 reshape.219
  680.0 0.1 slice.41
  680.1 1.2 reshape.216
  681.3 0.7 slice.48
  682.0 0.1 copy.56
  682.1 0.7 copy.58
  682.8 1.4 slice.45
  684.2 1.6 slice.44
  685.8 0.9 convert_element_type.40
  686.7 0.7 slice_reduce_fusion
  687.4 5.5 convert_reduce_fusion
  692.9 5.6 convert_reduce_fusion.1
  (38 shorter events, 0.2 us)
Async XLA Ops:
  12.1 6.8 copy-start.8
  12.1 6.9 copy-start.9
  12.1 7.0 copy-start.10
  12.1 7.2 %copy-start.11 = (f32[32]{0:T(128)S(1)}, f32[32]{0:T(128)}, u32[]{:S(2)}) copy-start(f32[32]{0:T(128)} %param.14) | copy-start | bytes 388
  12.1 7.3 %copy-start.6 = (f32[32,32]{1,0:T(8,128)S(1)}, f32[32,32]{1,0:T(8,128)}, u32[]{:S(2)}) copy-start(f32[32,32]{1,0:T(8,128)} %param.20) | copy-start | bytes 12292
  12.1 7.4 %copy-start.5 = (f32[32,512]{1,0:T(8,128)S(1)}, f32[32,512]{1,0:T(8,128)}, u32[]{:S(2)}) copy-start(f32[32,512]{1,0:T(8,128)} %param.17) | copy-start | bytes 196612
  12.1 7.5 %copy-start.4 = (f32[32,1536]{1,0:T(8,128)S(1)}, f32[32,1536]{1,0:T(8,128)}, u32[]{:S(2)}) copy-start(f32[32,1536]{1,0:T(8,128)} %param.16) | copy-start | bytes 589828
  12.1 8.3 %copy-start.7 = (s32[985,2]{0,1:T(2,128)S(1)}, s32[985,2]{0,1:T(2,128)}, u32[]{:S(2)}) copy-start(s32[985,2]{0,1:T(2,128)} %param.13) | copy-start | bytes 23644
  12.1 112.6 %all-to-all-start = ((bf16[16,2,32,2048]{3,2,1,0:T(8,128)(2,1)}), bf16[16,2,32,2048]{3,2,1,0:T(8,128)(2,1)}, u32[]{:S(2)}, u32[]{:S(2)}) async-start(bf16[16,2,32,2048]{3,2,1,0:T(8,128)(2,1)} %pad_maximum_fusion), calls=%async_computation | async-start | bytes 8388608 | tf_op jit(solution)/shard_map/all_to_all | solution.py:700
  18.8 4.6 copy-start
  18.8 85.8 %all-gather.2.cloned.1.call-start = ((), (), s32[]{:S(2)}) async-start(), calls=%async_computation.5 | async-start | bytes 2367488 | tf_op jit(solution)/shard_map/all_gather | solution.py:695
  20.3 4.5 copy-start.1
  124.7 232.6 %all-to-all-start.1 = ((bf16[16,2,128,512]{3,2,1,0:T(8,128)(2,1)}), bf16[16,2,128,512]{3,2,1,0:T(8,128)(2,1)}, u32[]{:S(2)}, u32[]{:S(2)}) async-start(bf16[16,2,128,512]{3,2,1,0:T(8,128)(2,1)} %pad_maximum_fusion.1), calls=%async_computation.1 | async-start | bytes 8388608 | tf_op jit(solution)/shard_map/all_to_all | solution.py:700
  357.3 6.8 copy-start.3
  357.3 157.1 %all-to-all-start.3 = ((bf16[16,2,128,512]{3,2,1,0:T(8,128)(2,1)}), bf16[16,2,128,512]{3,2,1,0:T(8,128)(2,1)}, u32[]{:S(2)}, u32[]{:S(2)}) async-start(bf16[16,2,128,512]{3,2,1,0:T(8,128)(2,1)} %get-tuple-element.44), calls=%async_computation.4 | async-start | bytes 8388608 | tf_op jit(solution)/shard_map/all_to_all | solution.py:703
  514.4 178.5 %all-to-all-start.2 = ((bf16[16,2,32,2048]{3,2,1,0:T(8,128)(2,1)}), bf16[16,2,32,2048]{3,2,1,0:T(8,128)(2,1)}, u32[]{:S(2)}, u32[]{:S(2)}) async-start(bf16[16,2,32,2048]{3,2,1,0:T(8,128)(2,1)} %get-tuple-element.43), calls=%async_computation.3 | async-start | bytes 8388608 | tf_op jit(solution)/shard_map/all_to_all | solution.py:703
  524.0 132.4 %reduce-scatter.2.cloned.1.call-start = ((), (), s32[]{:S(2)}) async-start(), calls=%async_computation.6 | async-start | bytes 2367488 | tf_op jit(solution)/shard_map/reduce_scatter | solution.py:751
  555.2 126.2 %all-reduce.7.cloned.1.call-start = ((), (), s32[]{:S(2)}) async-start(), calls=%async_computation.7 | async-start | bytes 278528 | tf_op jit(solution)/shard_map/psum | solution.py:752
  676.6 3.4 copy-start.2
Sparse Core Ops, SparseCore 0:
  22.5 82.0 all-gather.1
  555.3 86.0 reduce-scatter.1
  656.6 24.3 all-reduce.6

commit v4 on v3

--- a/solution.py
+++ b/solution.py
@@ -17,6 +17,7 @@
 HEAD = D // HEADS
 LANES = 128
 QKV = 3 * D
+SENT = D + LANES
 PACKED = QKV + D + LANES
 epsilon = 1e-06
 low = jnp.bfloat16
@@ -74,7 +75,7 @@
     return grown / jnp.sum(grown, axis=-1, keepdims=True)
 
 
-def attend_kernel(x_ref, w_ref, order_ref, qkv_ref, ctx_ref, r_ref, h_ref, probs_ref):
+def attend_kernel(x_ref, w_ref, order_ref, qkv_ref, ctx_ref, r_ref, sent_ref, probs_ref):
     gain_one, bias_one, gain_two, bias_two = norm_vectors(w_ref)
     x = x_ref[0].astype(full)
     normed, _ = normed_rows(x)
@@ -94,11 +95,13 @@
     r_ref[0] = r
     normed, _ = normed_rows(r)
     h = (normed * gain_two + bias_two).astype(low)
-    h_ref[0] = h
+    sent_ref[0, :, :D] = h
     logits = dot(h, dot(w_ref[:, QKV + D :], order_ref[...]).astype(low))
     logits = jnp.where(lanes_of(logits.shape) < EXPERTS, logits, -1e30)
     grown = jnp.exp(logits - jnp.max(logits, axis=-1, keepdims=True))
-    probs_ref[0] = grown / jnp.sum(grown, axis=-1, keepdims=True)
+    probs = grown / jnp.sum(grown, axis=-1, keepdims=True)
+    probs_ref[0] = probs
+    sent_ref[0, :, D:] = pltpu.roll(probs, LANES - EXPERTS // 2, 1).astype(low)
 
 
 def image_spec(width):
@@ -117,7 +120,7 @@
 
 def attend(x, weights, order):
     images = x.shape[0]
-    shapes = ((QKV, low), (D, low), (D, full), (D, low), (LANES, full))
+    shapes = ((QKV, low), (D, low), (D, full), (SENT, low), (LANES, full))
     return pl.pallas_call(
         attend_kernel,
         grid=(images,),
@@ -224,69 +227,133 @@
     )(*arrays)
 
 
-def position(groups):
-    return lax.axis_index("part") * groups + lax.axis_index("expert")
-
-
-def peer_of(groups, k):
-    peer = position(groups) ^ k
-    return lax.axis_index("replica"), peer // groups, peer % groups
-
-
-def greet(peers, groups):
+def device(offset):
+    names = ("replica", "part", "expert")
+    return tuple(lax.axis_index(name) ^ o for name, o in zip(names, offset))
+
+
+def near(groups, j):
+    return (0, j // groups, j % groups)
+
+
+def greet(offsets):
     barrier = pltpu.get_barrier_semaphore()
-    for k in range(1, peers):
-        pl.semaphore_signal(barrier, inc=1, device_id=peer_of(groups, k), device_id_type=MESH)
-    pl.semaphore_wait(barrier, peers - 1)
-
-
-def swap(source, target, sends, receives, groups, k):
+    for offset in offsets:
+        pl.semaphore_signal(barrier, inc=1, device_id=device(offset), device_id_type=MESH)
+    pl.semaphore_wait(barrier, len(offsets))
+
+
+def remote(source, target, send, receive, offset):
     return pltpu.make_async_remote_copy(
-        src_ref=source.at[k],
-        dst_ref=target.at[k],
-        send_sem=sends.at[k],
-        recv_sem=receives.at[k],
-        device_id=peer_of(groups, k),
+        src_ref=source,
+        dst_ref=target,
+        send_sem=send,
+        recv_sem=receive,
+        device_id=device(offset),
         device_id_type=MESH,
     )
 
 
-def dispatch_kernel(groups, keys_ref, rows_ref, out_ref, blocks, sends, receives, local):
-    peers, own, tokens = keys_ref.shape
+def owners_like(replicas, parts):
+    return [(r, p, 0) for r in range(replicas) for p in range(0, parts, 2) if (r, p) != (0, 0)]
+
+
+def owner(parts, offset=(0, 0, 0)):
+    return (lax.axis_index("replica") ^ offset[0]) * parts + (lax.axis_index("part") ^ offset[1])
+
+
+CORE = (0, 1, 0)
+
+
+def dispatch_kernel(sizes, keys_ref, rows_ref, *refs):
+    replicas, parts, groups = sizes
+    opening = replicas > 0
+    if opening:
+        shard_ref, out_ref, weights_ref, *refs = refs
+    else:
+        out_ref, other_ref, *refs = refs
+    blocks, other, hop, sends, receives, local, *refs = refs
+    _, count, own, tokens = keys_ref.shape
+    mirror = (0, parts // 2, 0)
+    owners = owners_like(replicas, parts)
+    greet(sorted({near(groups, j) for j in range(1, count)} | {mirror, *owners}))
     slots = lax.broadcasted_iota(jnp.int32, (CAP, tokens), 0).astype(full)
-    greet(peers, groups)
-
-    def build(k):
-        picks = [(keys_ref[k, i : i + 1] == slots).astype(low) for i in range(own)]
-        picks = jnp.concatenate(picks, axis=0) if own > 1 else picks[0]
-        blocks[k] = dot(picks, rows_ref[...]).astype(low).reshape(own, CAP, D)
-
-    copies = [swap(blocks, out_ref, sends, receives, groups, k) for k in range(1, peers)]
-    for k in range(1, peers):
-        build(k)
-        copies[k - 1].start()
-    build(0)
-    mine = pltpu.make_async_copy(blocks.at[0], out_ref.at[0], local)
-    mine.start()
-    for copy in copies:
+    copies = [remote(rows_ref, other, hop.at[0], hop.at[1], mirror)]
+    copies[0].start()
+    if opening:
+        early, late, here = refs
+        mine = owner(parts)
+        gathers = [
+            remote(shard_ref, weights_ref.at[mine], early.at[0, i], early.at[1, i], o)
+            for i, o in enumerate(owners)
+        ]
+        passes = [remote(shard_ref, weights_ref.at[mine], late.at[0, 0], late.at[1, 0], CORE)]
+        for i, o in enumerate(owners):
+            slot = weights_ref.at[owner(parts, o)]
+            passes.append(remote(slot, slot, late.at[0, i + 1], late.at[1, i + 1], CORE))
+        for copy in gathers:
+            copy.start()
+        passes[0].start()
+        kept = pltpu.make_async_copy(shard_ref, weights_ref.at[mine], here)
+        kept.start()
+
+    def build(s, source_ref):
+        for j in [*range(1, count), 0]:
+            picks = [(keys_ref[s, j, i : i + 1] == slots).astype(low) for i in range(own)]
+            picks = jnp.concatenate(picks, axis=0) if own > 1 else picks[0]
+            rows = dot(picks, source_ref[:, :D]).astype(low)
+            blocks[j, s] = rows.reshape(own, CAP, D)
+            if j:
+                copy = remote(
+                    blocks.at[j, s], out_ref.at[j, s], sends.at[j, s], receives.at[j, s],
+                    near(groups, j),
+                )
+            else:
+                copy = pltpu.make_async_copy(blocks.at[0, s], out_ref.at[0, s], local.at[s])
+            copy.start()
+            copies.append(copy)
+
+    build(0, rows_ref)
+    if opening:
+        for i, copy in enumerate(gathers):
+            copy.wait_recv()
+            passes[i + 1].start()
+    copies[0].wait_recv()
+    build(1, other)
+    if not opening:
+        keep = pltpu.make_async_copy(other, other_ref, local.at[2])
+        keep.start()
+        keep.wait()
+    copies[0].wait_send()
+    for copy in copies[1:]:
         copy.wait()
-    mine.wait()
-
-
-def dispatch(keys, rows, groups, number):
-    peers, own, tokens = keys.shape
-    shape = (peers, own, CAP, D)
+    if opening:
+        for copy in gathers:
+            copy.wait_send()
+        for copy in passes:
+            copy.wait()
+        kept.wait()
+
+
+def dispatch(keys, rows, sizes, number, shard=None):
+    replicas, parts, groups = sizes
+    _, count, own, tokens = keys.shape
+    shape = (count, 2, own, CAP, D)
+    owners = replicas * parts
+    opening = shard is not None
+    second = (owners, *shard.shape) if opening else rows.shape
+    semaphores = [(2,), (count, 2), (count, 2), (3,)]
+    if opening:
+        semaphores += [(2, owners // 2 - 1), (2, owners // 2), ()]
+    inner = pl.BlockSpec(memory_space=pltpu.VMEM)
+    outer = pl.BlockSpec(memory_space=pl.ANY)
     return pl.pallas_call(
-        partial(dispatch_kernel, groups),
-        in_specs=[pl.BlockSpec(memory_space=pltpu.VMEM)] * 2,
-        out_specs=pl.BlockSpec(memory_space=pl.ANY),
-        out_shape=jax.ShapeDtypeStruct(shape, low),
-        scratch_shapes=[
-            pltpu.VMEM(shape, low),
-            pltpu.SemaphoreType.DMA((peers,)),
-            pltpu.SemaphoreType.DMA((peers,)),
-            pltpu.SemaphoreType.DMA,
-        ],
+        partial(dispatch_kernel, sizes if opening else (0, parts, groups)),
+        in_specs=[inner, inner] + [inner] * opening,
+        out_specs=[outer, outer],
+        out_shape=[jax.ShapeDtypeStruct(shape, low), jax.ShapeDtypeStruct(second, low)],
+        scratch_shapes=[pltpu.VMEM(shape, low), pltpu.VMEM(rows.shape, low)]
+        + [pltpu.SemaphoreType.DMA(n) for n in semaphores],
         compiler_params=pltpu.CompilerParams(
             vmem_limit_bytes=BIG, collective_id=number, has_side_effects=True
         ),
@@ -294,119 +361,245 @@
             flops=60 * 10**9, bytes_accessed=5 * 10**6, transcendentals=0
         ),
         name=f"dispatch_{number}",
-    )(keys, rows)
-
-
-def exchange_kernel(groups, blocks_ref, out_ref, sends, receives, local):
-    peers = blocks_ref.shape[0]
-    greet(peers, groups)
-    copies = [swap(blocks_ref, out_ref, sends, receives, groups, k) for k in range(1, peers)]
-    for copy in copies:
-        copy.start()
-    mine = pltpu.make_async_copy(blocks_ref.at[0], out_ref.at[0], local)
-    mine.start()
-    for copy in copies:
-        copy.wait()
-    mine.wait()
-
-
-def exchange(blocks, groups, number):
-    peers = blocks.shape[0]
-    return pl.pallas_call(
-        partial(exchange_kernel, groups),
-        in_specs=[pl.BlockSpec(memory_space=pl.ANY)],
-        out_specs=pl.BlockSpec(memory_space=pl.ANY),
-        out_shape=jax.ShapeDtypeStruct(blocks.shape, low),
-        scratch_shapes=[
-            pltpu.SemaphoreType.DMA((peers,)),
-            pltpu.SemaphoreType.DMA((peers,)),
-            pltpu.SemaphoreType.DMA,
-        ],
-        compiler_params=pltpu.CompilerParams(collective_id=number, has_side_effects=True),
-        cost_estimate=pl.CostEstimate(
-            flops=60 * 10**9, bytes_accessed=10 * 10**6, transcendentals=0
-        ),
-        name=f"exchange_{number}",
-    )(blocks)
-
-
-def chooser(own, k):
+    )(keys, rows, *([shard] if opening else []))
+
+
+def chooser(own, j):
     shape = (LANES, own * CAP)
     expert = lax.broadcasted_iota(jnp.int32, shape, 0)
     slot = lax.broadcasted_iota(jnp.int32, shape, 1)
-    return (expert == k * own + slot // CAP).astype(low)
-
-
-def combine_kernel(keys_ref, probs_ref, r_ref, y_ref, out_ref):
-    peers, own, _, _ = y_ref.shape
-
-    @pl.loop(0, r_ref.shape[0] // ROWS)
-    def _(i):
-        rows = pl.ds(pl.multiple_of(i * ROWS, ROWS), ROWS)
-        slot = (lanes_of((ROWS, own * CAP)) % CAP).astype(full)
-        probs = probs_ref[rows].astype(low)
-        total = r_ref[rows]
-        for k in range(peers):
-            spread = chooser(own, k)
-            here = dot(keys_ref[rows], spread) == slot
-            gate = jnp.where(here, dot(probs, spread), 0.0)
-            total = total + dot(gate.astype(low), y_ref[k].reshape(own * CAP, D))
-        out_ref[rows] = total.astype(low)
-
-
-def combine(keys, probs, r, y):
-    tokens = keys.shape[0]
-    return pl.pallas_call(
-        combine_kernel,
-        out_shape=jax.ShapeDtypeStruct((tokens, D), low),
-        compiler_params=pltpu.CompilerParams(vmem_limit_bytes=BIG),
-        cost_estimate=pl.CostEstimate(
-            flops=6 * 10**9, bytes_accessed=10 * 10**6, transcendentals=0
-        ),
-        name="combine",
-    )(keys, probs, r, y)
-
-
-def gather_kernel(keys_ref, back_ref, dh_ref, dprobs_ref):
-    peers, own, _, _ = back_ref.shape
+    return (expert == j * own + slot // CAP).astype(low)
+
+
+def gather_kernel(sizes, keys_ref, back_ref, dh_ref, dprobs_ref, sent, got, sends, receives):
+    _, parts, groups = sizes
+    count, _, own, _, _ = back_ref.shape
+    tokens = dh_ref.shape[0]
     width = own * CAP
-
-    @pl.loop(0, dh_ref.shape[0] // ROWS)
-    def _(i):
-        rows = pl.ds(pl.multiple_of(i * ROWS, ROWS), ROWS)
+    half = count * own
+    mirror = (0, parts // 2, 0)
+    greet([mirror])
+
+    def rows_of(i):
+        return pl.ds(pl.multiple_of(i * ROWS, ROWS), ROWS)
+
+    def hop(i):
+        rows = rows_of(i)
+        return remote(sent.at[rows], got.at[rows], sends.at[i], receives.at[i], mirror)
+
+    def summed(s, rows):
         slot = (lanes_of((ROWS, width)) % CAP).astype(full)
         lane = lanes_of((ROWS, LANES))
+        keys = keys_ref[s, rows]
         total = jnp.zeros((ROWS, D), full)
         dprobs = jnp.zeros((ROWS, LANES), full)
-        for k in range(peers):
-            here = dot(keys_ref[rows], chooser(own, k)) == slot
-            total = total + dot(here.astype(low), back_ref[k, :, :CAP].reshape(width, D))
-            dgate = back_ref[k, :, CAP : CAP + 1].astype(full)
+        for j in range(count):
+            here = dot(keys, chooser(own, j)) == slot
+            total = total + dot(here.astype(low), back_ref[j, s, :, :CAP].reshape(width, D))
+            dgate = back_ref[j, s, :, CAP : CAP + 1].astype(full)
             dgate = dgate[:, :, :CAP] + dgate[:, :, CAP : 2 * CAP]
-            agreed = [
-                jnp.where(here[:, e * CAP : (e + 1) * CAP], dgate[e], 0.0) for e in range(own)
-            ]
             for e in range(own):
-                column = jnp.sum(agreed[e], axis=-1, keepdims=True)
-                dprobs = jnp.where(lane == k * own + e, column, dprobs)
-        dh_ref[rows] = total
-        dprobs_ref[rows] = dprobs
-
-
-def gather(keys, back):
-    tokens = keys.shape[0]
+                agreed = jnp.where(here[:, e * CAP : (e + 1) * CAP], dgate[e], 0.0)
+                column = jnp.sum(agreed, axis=-1, keepdims=True)
+                dprobs = jnp.where(lane == j * own + e, column, dprobs)
+        return total, dprobs
+
+    @pl.loop(0, tokens // ROWS)
+    def _(i):
+        rows = rows_of(i)
+        total, dprobs = summed(1, rows)
+        sent[rows, :D] = total.astype(low)
+        high = dprobs.astype(low)
+        rest = pltpu.roll(dprobs - high.astype(full), half, 1)
+        sent[rows, D:] = (high.astype(full) + rest).astype(low)
+        hop(i).start()
+
+    @pl.loop(0, tokens // ROWS)
+    def _(i):
+        rows = rows_of(i)
+        dh_ref[rows], dprobs_ref[rows] = summed(0, rows)
+
+    @pl.loop(0, tokens // ROWS)
+    def _(i):
+        rows = rows_of(i)
+        hop(i).wait()
+        dh_ref[rows] += got[rows, :D].astype(full)
+        pair = got[rows, D:].astype(full)
+        lane = lanes_of(pair.shape)
+        theirs = pair + pltpu.roll(pair, half, 1)
+        mine = (lane >= half) & (lane < 2 * half)
+        dprobs_ref[rows] += jnp.where(mine, theirs, 0.0)
+
+
+def gather(keys, back, sizes, number):
+    tokens = keys.shape[1]
+    steps = tokens // ROWS
+    inner = pl.BlockSpec(memory_space=pltpu.VMEM)
     return pl.pallas_call(
-        gather_kernel,
+        partial(gather_kernel, sizes),
+        in_specs=[inner, inner],
+        out_specs=[inner, inner],
         out_shape=[
             jax.ShapeDtypeStruct((tokens, D), full),
             jax.ShapeDtypeStruct((tokens, LANES), full),
         ],
-        compiler_params=pltpu.CompilerParams(vmem_limit_bytes=BIG),
+        scratch_shapes=[
+            pltpu.VMEM((tokens, SENT), low),
+            pltpu.VMEM((tokens, SENT), low),
+            pltpu.SemaphoreType.DMA((steps,)),
+            pltpu.SemaphoreType.DMA((steps,)),
+        ],
+        compiler_params=pltpu.CompilerParams(
+            vmem_limit_bytes=BIG, collective_id=number, has_side_effects=True
+        ),
         cost_estimate=pl.CostEstimate(
-            flops=6 * 10**9, bytes_accessed=7 * 10**6, transcendentals=0
+            flops=30 * 10**9, bytes_accessed=7 * 10**6, transcendentals=0
         ),
         name="gather",
     )(keys, back)
+
+
+def close_kernel(
+    sizes, keys_ref, probs_ref, r_ref, theirs_ref, y_ref, grads_ref, out_ref, total_ref,
+    ys, acc, sent, got, kept, first, second, third,
+    y_sends, y_receives, y_local, hops, core_sems, kept_sems, owner_sems, expert_sems,
+):
+    replicas, parts, groups = sizes
+    count, _, own, _, _ = y_ref.shape
+    tokens = r_ref.shape[0]
+    width = own * CAP
+    mirror = (0, parts // 2, 0)
+    owners = owners_like(replicas, parts)
+    across = [(0, 0, g) for g in range(1, groups)]
+    greet(sorted({near(groups, j) for j in range(1, count)} | {mirror, CORE, *owners, *across}))
+    core = lax.axis_index("part") % 2
+    pairs = replicas * parts // 2
+
+    def swap(j, s):
+        if j == 0:
+            return pltpu.make_async_copy(y_ref.at[0, s], ys.at[0, s], y_local.at[s])
+        return remote(
+            y_ref.at[j, s], ys.at[j, s], y_sends.at[j, s], y_receives.at[j, s], near(groups, j)
+        )
+
+    swaps = [[swap(j, s) for j in range(count)] for s in range(2)]
+    to_core = [
+        remote(grads_ref.at[2 * i + 1 - core], first.at[i], core_sems.at[0, i], core_sems.at[1, i], CORE)
+        for i in range(pairs)
+    ]
+    own_rows = [
+        pltpu.make_async_copy(grads_ref.at[2 * i + core], kept.at[i], kept_sems.at[i])
+        for i in range(pairs)
+    ]
+    for copy in to_core + own_rows + swaps[1] + swaps[0]:
+        copy.start()
+    for i in range(pairs):
+        own_rows[i].wait()
+        to_core[i].wait()
+        kept[i] = (kept[i].astype(full) + first[i].astype(full)).astype(low)
+    to_owner = [
+        remote(kept.at[owner(parts, o) // 2], second.at[i], owner_sems.at[0, i], owner_sems.at[1, i], o)
+        for i, o in enumerate(owners)
+    ]
+    for copy in to_owner:
+        copy.start()
+
+    def rows_of(i):
+        return pl.ds(pl.multiple_of(i * ROWS, ROWS), ROWS)
+
+    def weighted(s, rows, probs):
+        slot = (lanes_of((ROWS, width)) % CAP).astype(full)
+        keys = keys_ref[s, rows]
+        total = jnp.zeros((ROWS, D), full)
+        for j in range(count):
+            spread = chooser(own, j)
+            gate = jnp.where(dot(keys, spread) == slot, dot(probs, spread), 0.0)
+            total = total + dot(gate.astype(low), ys[j, s].reshape(width, D))
+        return total
+
+    def hop(i):
+        rows = rows_of(i)
+        return remote(sent.at[rows], got.at[rows], hops.at[0, i], hops.at[1, i], mirror)
+
+    for copy in swaps[1]:
+        copy.wait()
+
+    @pl.loop(0, tokens // ROWS)
+    def _(i):
+        rows = rows_of(i)
+        sent[rows] = weighted(1, rows, theirs_ref[rows, D:]).astype(low)
+        hop(i).start()
+
+    total = kept[owner(parts) // 2].astype(full)
+    for i, copy in enumerate(to_owner):
+        copy.wait()
+        total = total + second[i].astype(full)
+    me = lax.axis_index("expert")
+    third[me] = total.astype(low)
+    to_others = [
+        remote(third.at[me], third.at[me], expert_sems.at[0, i], expert_sems.at[1, i], o)
+        for i, o in enumerate(across)
+    ]
+    for copy in to_others:
+        copy.start()
+    for copy in swaps[0]:
+        copy.wait()
+
+    @pl.loop(0, tokens // ROWS)
+    def _(i):
+        rows = rows_of(i)
+        acc[rows] = r_ref[rows] + weighted(0, rows, probs_ref[rows].astype(low))
+
+    for copy in to_others:
+        copy.wait()
+    total = third[0].astype(full)
+    for g in range(1, groups):
+        total = total + third[g].astype(full)
+    total_ref[...] = total
+
+    @pl.loop(0, tokens // ROWS)
+    def _(i):
+        rows = rows_of(i)
+        hop(i).wait()
+        out_ref[rows] = (acc[rows] + got[rows].astype(full)).astype(low)
+
+
+def close(keys, probs, r, theirs, y, grads, sizes, number):
+    replicas, parts, groups = sizes
+    tokens = r.shape[0]
+    steps = tokens // ROWS
+    count = y.shape[0]
+    pairs = replicas * parts // 2
+    shard = grads.shape[1:]
+    inner = pl.BlockSpec(memory_space=pltpu.VMEM)
+    outer = pl.BlockSpec(memory_space=pl.ANY)
+    semaphores = [
+        (count, 2), (count, 2), (2,), (2, steps), (2, pairs), (pairs,), (2, pairs - 1), (2, groups - 1),
+    ]
+    return pl.pallas_call(
+        partial(close_kernel, sizes),
+        in_specs=[inner] * 4 + [outer] * 2,
+        out_specs=[inner, inner],
+        out_shape=[jax.ShapeDtypeStruct((tokens, D), low), jax.ShapeDtypeStruct(shard, full)],
+        scratch_shapes=[
+            pltpu.VMEM(y.shape, low),
+            pltpu.VMEM((tokens, D), full),
+            pltpu.VMEM((tokens, D), low),
+            pltpu.VMEM((tokens, D), low),
+            pltpu.VMEM((pairs, *shard), low),
+            pltpu.VMEM((pairs, *shard), low),
+            pltpu.VMEM((pairs - 1, *shard), low),
+            pltpu.VMEM((groups, *shard), low),
+        ]
+        + [pltpu.SemaphoreType.DMA(n) for n in semaphores],
+        compiler_params=pltpu.CompilerParams(
+            vmem_limit_bytes=BIG, collective_id=number, has_side_effects=True
+        ),
+        cost_estimate=pl.CostEstimate(
+            flops=60 * 10**9, bytes_accessed=10 * 10**6, transcendentals=0
+        ),
+        name="close",
+    )(keys, probs, r, theirs, y, grads)
 
 
 GELU = 0.7978845608028654
@@ -506,16 +699,16 @@
             dst_ref=back_ref.at[k, e],
             send_sem=sends.at[k, e],
             recv_sem=receives.at[k, e],
-            device_id=peer_of(groups, k),
+            device_id=device(near(groups, k // 2)),
             device_id_type=MESH,
         )
 
-    def mine(e):
-        return pltpu.make_async_copy(staged.at[0, e], back_ref.at[0, e], local.at[e])
+    def mine(k, e):
+        return pltpu.make_async_copy(staged.at[k, e], back_ref.at[k, e], local.at[k, e])
 
     @pl.when(at == 0)
     def _():
-        greet(sources, groups)
+        greet([near(groups, j) for j in range(1, sources // 2)])
 
     @pl.when((phase != 1) & (step == 0))
     def _():
@@ -555,9 +748,10 @@
         for e in range(own):
             @pl.when((step == steps - 1) & (expert == e))
             def _():
-                for k in range(1, sources):
+                for k in range(2, sources):
                     copy(k, e).start()
-                mine(e).start()
+                mine(0, e).start()
+                mine(1, e).start()
 
     @pl.when(phase == 1)
     def _():
@@ -582,9 +776,10 @@
     @pl.when(at == 3 * own * steps - 1)
     def _():
         for e in range(own):
-            for k in range(1, sources):
+            for k in range(2, sources):
                 copy(k, e).wait()
-            mine(e).wait()
+            mine(0, e).wait()
+            mine(1, e).wait()
 
 
 def expert_rest(dy, h, g, slope, w_in, w_out, tile, groups, number):
@@ -643,7 +838,7 @@
             pltpu.VMEM((sources, own, CAP + 16, D), low),
             pltpu.SemaphoreType.DMA((sources, own)),
             pltpu.SemaphoreType.DMA((sources, own)),
-            pltpu.SemaphoreType.DMA((own,)),
+            pltpu.SemaphoreType.DMA((2, own)),
         ],
         compiler_params=pltpu.CompilerParams(
             dimension_semantics=("arbitrary",),
@@ -692,8 +887,6 @@
         [w_qkv, w_proj, placed_router, vectors, jnp.zeros((small_rows, LANES - EXPERTS - 4), full)],
         axis=1,
     ).astype(low)
-    weights = lax.all_gather(packed, ALL, axis=0, tiled=True)
-
     def spread(master):
         pieces = master.astype(low).reshape(parts, own, *master.shape[1:])
         pieces = jnp.concatenate([pieces] * replicas, axis=0)
@@ -704,7 +897,8 @@
         pieces = pieces.reshape(replicas, parts * own, *grad.shape[2:])
         return jnp.sum(pieces.astype(full), axis=0)
 
-    me = position(groups)
+    me = lax.axis_index("part") * groups + lax.axis_index("expert")
+    sizes = (replicas, parts, groups)
 
     def padded(rows, fill=0):
         rows = rows.reshape(images, SEQ, rows.shape[1])
@@ -712,26 +906,37 @@
 
     x = padded(tokens)
     dy = padded(cotangent)
-    picks = padded(choices, -1).reshape(count, 2)
+    half = parts // 2
+    flips = [(i, i ^ half) for i in range(parts)]
+    picks = jnp.stack([choices, lax.ppermute(choices, "part", flips)]).reshape(2 * images, SEQ, 2)
+    picks = jnp.pad(picks, ((0, 0), (0, ROWS - SEQ), (0, 0)), constant_values=-1)
+    picks = picks.reshape(2, count, 2)
     column = jnp.arange(EXPERTS)
     place = (me ^ (column // own)) * own + column % own
     expert = (place // own % groups) * (parts * own) + place // (groups * own) * own + place % own
     lane = jnp.arange(LANES)
     order = jnp.where(lane < EXPERTS, jnp.pad(place, (0, LANES - EXPERTS)), lane)
     order = (lane[:, None] == order[None, :]).astype(low)
-    named = (picks[:, :, None] == expert[None, None, :]).any(axis=1)
+    expert = expert[: EXPERTS // 2]
+    named = (picks[:, :, :, None] == expert).any(axis=2)
     row = jnp.arange(count)
-    slots = dot((row[None, :] < row[:, None]).astype(low), named.astype(low))
+    earlier = (row[None, :] < row[:, None]).astype(low)
+    slots = jnp.einsum("tu,sue->ste", earlier, named.astype(low), preferred_element_type=full)
     keys = jnp.where(named, slots, -1.0)
-    key_rows = keys.T.reshape(peers, own, count)
-    key_columns = jnp.pad(keys, ((0, 0), (0, LANES - EXPERTS)), constant_values=-1).astype(low)
+    key_rows = keys.transpose(0, 2, 1).reshape(2, peers // 2, own, count)
+    key_columns = jnp.pad(
+        keys, ((0, 0), (0, 0), (0, LANES - EXPERTS // 2)), constant_values=-1
+    ).astype(low)
 
     first_weight = spread(w_expert_in)
-    dy_slots = dispatch(key_rows, dy.reshape(count, D), groups, 0)
-    qkv, ctx, r, h, probs = attend(x, weights, order)
-    w_expert_out, h = lax.optimization_barrier((w_expert_out, h))
+    dy_slots, weights = dispatch(key_rows, dy.reshape(count, D), sizes, 0, packed)
+    weights = weights.reshape(D, PACKED)
+    qkv, ctx, r, sent, probs = attend(x, weights, order)
+    w_expert_out, sent = lax.optimization_barrier((w_expert_out, sent))
     second_weight = spread(w_expert_out)
-    h_slots = dispatch(key_rows, h.reshape(count, D), groups, 1)
+    h_slots, theirs = dispatch(key_rows, sent.reshape(count, SENT), sizes, 1)
+    dy_slots = dy_slots.reshape(peers, own, CAP, D)
+    h_slots = h_slots.reshape(peers, own, CAP, D)
     select = ((me * own + jnp.arange(own))[:, None, None] == lane[None, None, :]).astype(full)
     g, slope, dw_second = expert_first(
         h_slots, dy_slots, first_weight, weights[:, QKV + D :], select, tile
@@ -739,17 +944,19 @@
     back, dw_first, y = expert_rest(
         dy_slots, h_slots, g, slope, first_weight, second_weight, tile, groups, 2
     )
-    y = exchange(y, groups, 3)
+    back = back.reshape(peers // 2, 2, own, CAP + 16, D)
+    y = y.reshape(peers // 2, 2, own, CAP, D)
     expert_out_grad = collect(dw_second)
     expert_in_grad = collect(dw_first)
-    dh, dprobs = gather(key_columns, back)
+    dh, dprobs = gather(key_columns, back, sizes, 3)
     dx, grads = attend_back(
-        x, weights, order, qkv, ctx, r, h, probs,
+        x, weights, order, qkv, ctx, r, sent, probs,
         dprobs.reshape(images, ROWS, LANES), dh.reshape(images, ROWS, D), dy,
     )
-    output = combine(key_columns, probs.reshape(count, LANES), r.reshape(count, D), y)
-    grads = lax.psum_scatter(grads, ALL, scatter_dimension=0, tiled=True)
-    grads = lax.psum(grads, "expert").astype(full)
+    output, grads = close(
+        key_columns, probs.reshape(count, LANES), r.reshape(count, D), theirs, y,
+        grads.reshape(owners, small_rows, PACKED), sizes, 4,
+    )
     router_grad = (
         grads[:, QKV + D : QKV + D + EXPERTS]
         .reshape(small_rows, parts, groups, own)

time: 715 us -> 672 us (0.940)
  waiting for transfers between devices: 78.2 us -> 0.01 us
  Pallas kernels: 539 us -> 585 us
  between operations: 14.3 us -> 1.49 us
    all_gather x1 -> x0, waiting for transfers between devices: 77.8 us -> none  [body(): weights = lax.all_gather(packed, ALL, axis=0, tiled=True)]
    pallas_call x5 -> x4, Pallas kernels: 323 us -> 398 us  [the longest x2 264 us: dispatch(): pl.pallas_call(partial(dispatch_kernel, sizes if opening else (0, parts,...]
    pallas_call x1, Pallas kernels: 130 us -> 101 us  [expert_rest(): pl.pallas_call(partial(rest_kernel, groups, own, steps), grid=(3 * own *...]
  transfers between devices with their start and end apart: 7 -> 5, of which waited for: 2 -> 0; matrix products, arithmetic and copies ran while one was open for 5% -> 6% of each run, Pallas kernels for 76% -> 89%
where the time goes in v4:
time: 672 us; the launch traced here: 659 us
  Pallas kernels  585 us (87%)
  starting transfers between devices  29.5 us (4%)
  other arithmetic  22.3 us (3%)
  local copies, waits for them, and re-layouts  19.2 us (3%)
    pallas_call x2, Pallas kernels, dispatch(): pl.pallas_call(partial(dispatch_kernel, sizes if opening else (0, parts,...  264 us
    pallas_call x1, Pallas kernels, expert_rest(): pl.pallas_call(partial(rest_kernel, groups, own, steps), grid=(3 * own *...  101 us
    pallas_call x1, Pallas kernels, close(): pl.pallas_call(partial(close_kernel, sizes), in_specs=[inner] * 4 + [oute...  98.7 us
    pallas_call x1, Pallas kernels, expert_first(): pl.pallas_call(first_kernel, grid=(own, hidden // tile), in_specs=[slot_s...  39.7 us
    pallas_call x1, Pallas kernels, gather(): pl.pallas_call(partial(gather_kernel, sizes), in_specs=[inner, inner], ou...  35.6 us
    pallas_call x1, Pallas kernels, attend_back(): pl.pallas_call(partial(attend_back_kernel, images), grid=(images,), in_sp...  30.8 us
    pallas_call x1, Pallas kernels, attend(): pl.pallas_call(attend_kernel, grid=(images,), in_specs=[image_spec(D), wh...  15.3 us
    all_to_all x2, starting transfers between devices, collect(): pieces = lax.all_to_all(grad, ALL, split_axis=0, concat_axis=0, tiled=True)  14.9 us
  transfers between devices with their start and end apart: 5, of which 0 were waited for; matrix products, arithmetic and copies ran while one was open for 6% of the time, Pallas kernels for 89%

profile of v4, /device:TPU:13, one launch (start us, length us, event | category | flops | bytes accessed | tf_op | source)
XLA Modules:
  0.0 659.0 jit_solution(5520143175643087852)
XLA Ops:
  0.6 0.2 collective-permute-start
  0.9 2.5 convert_element_type.34
  3.4 2.4 pad_maximum_fusion
  5.8 0.0 copy-start
  5.8 0.0 copy-start.3
  5.8 0.0 copy-start.7
  5.8 0.0 copy-start.8
  5.8 0.0 copy-start.1
  5.8 7.1 %all-to-all-start = ((bf16[16,2,32,2048]{3,2,1,0:T(8,128)(2,1)}), bf16[16,2,32,2048]{3,2,1,0:T(8,128)(2,1)}, u32[]{:S(2)}, u32[]{:S(2)}) async-start(bf16[16,2,32,2048]{3,2,1,0:T(8,128)(2,1)} %pad_maximum_fusion), calls=%async_computation | async-start | bytes 8388608 | tf_op jit(solution)/shard_map/all_to_all | solution.py:893
  13.0 0.6 fusion.4.order_ref
  13.7 0.0 copy-start.9
  13.7 0.3 reshape.151
  14.0 0.1 copy.75
  14.1 0.1 copy.77
  14.2 0.1 copy.78
  14.3 0.1 copy.79
  14.4 0.1 copy.80
  14.5 0.1 copy.81
  14.6 0.3 reshape.149
  14.9 1.1 pad.23.dy_ref
  16.0 1.1 pad.22.x_ref
  17.1 0.8 concatenate.10.refs_0_
  17.9 0.0 collective-permute-done
  17.9 0.1 reshape.148
  18.0 0.1 eq.53
  18.1 0.1 compare_reduce_fusion
  18.2 0.0 copy-start.4
  18.2 1.2 bitcast_select_fusion.1
  19.4 0.1 copy.74
  19.4 0.7 copy.82.keys_ref
  20.2 137.3 %dispatch_0.1 = (bf16[8,2,2,128,512]{4,3,2,1,0:T(8,128)(2,1)}, bf16[16,32,2176]{2,1,0:T(8,128)(2,1)}) custom-call(f32[2,8,2,1040]{3,2,1,0:T(2,128)} %copy.82.keys_ref, bf16[1040,512]{1,0:T(8,128)(2,1)} %bitcast.61, bf16[32,2176]{1,0:T(8,128)(2,1)} %concatenate.10.refs_0_), custom_call_target="tpu_custom_call" | custom-call | flops 60000002048 | bytes 5000000 | tf_op jit(solution)/shard_map/dispatch_0/pallas_call | solution.py:350
  157.5 15.3 %attend.1 = (bf16[5,208,1536]{2,1,0:T(8,128)(2,1)}, bf16[5,208,512]{2,1,0:T(8,128)(2,1)}, f32[5,208,512]{2,1,0:T(8,128)}, bf16[5,208,640]{2,1,0:T(8,128)(2,1)}, f32[5,208,128]{2,1,0:T(8,128)}) custom-call(bf16[5,208,512]{2,1,0:T(8,128)(2,1)} %pad.22.x_ref, bf16[512,2176]{1,0:T(8,128)(2,1)} %bitcast.70, bf16[128,128]{1,0:T(8,128)(2,1)} %fusion.4.order_ref), custom_call_target="tpu_custom_call" | custom-call | flops 8000000000 | bytes 12000000 | tf_op jit(solution)/shard_map/attend/pallas_call | solution.py:124
  172.9 2.5 convert_element_type.36
  175.4 2.4 pad_maximum_fusion.1
  177.7 0.0 all-to-all-done.w_ref.w_in_ref
  177.7 7.3 %all-to-all-start.1 = ((bf16[16,2,128,512]{3,2,1,0:T(8,128)(2,1)}), bf16[16,2,128,512]{3,2,1,0:T(8,128)(2,1)}, u32[]{:S(2)}, u32[]{:S(2)}) async-start(bf16[16,2,128,512]{3,2,1,0:T(8,128)(2,1)} %pad_maximum_fusion.1), calls=%async_computation.1 | async-start | bytes 8388608 | tf_op jit(solution)/shard_map/all_to_all | solution.py:893
  185.0 0.6 compare_convert_fusion.sel_ref
  185.7 1.6 slice.44.wr_ref
  187.2 126.5 %dispatch_1.1 = (bf16[8,2,2,128,512]{4,3,2,1,0:T(8,128)(2,1)}, bf16[1040,640]{1,0:T(8,128)(2,1)}) custom-call(f32[2,8,2,1040]{3,2,1,0:T(2,128)} %copy.82.keys_ref, bf16[1040,640]{1,0:T(8,128)(2,1)} %bitcast.83), custom_call_target="tpu_custom_call" | custom-call | flops 60000002048 | bytes 5000000 | tf_op jit(solution)/shard_map/dispatch_1/pallas_call | solution.py:350
  313.7 39.7 %expert_first.1 = (bf16[2,2048,2048]{2,1,0:T(8,128)(2,1)}, bf16[2,2048,2048]{2,1,0:T(8,128)(2,1)}, bf16[16,2,128,512]{3,2,1,0:T(8,128)(2,1)}) custom-call(bf16[16,2,128,512]{3,2,1,0:T(8,128)(2,1)} %bitcast.78, bf16[16,2,128,512]{3,2,1,0:T(8,128)(2,1)} %bitcast.75, bf16[16,2,32,2048]{3,2,1,0:T(8,128)(2,1)} %all-to-all-done.w_ref.w_in_ref, ...), custom_call_target="tpu_custom_call" | custom-call | flops 17179869184 | bytes 50000000 | tf_op jit(solution)/shard_map/expert_first/pallas_call | solution.py:653
  353.3 0.0 copy-start.5
  353.4 6.3 all-to-all-start.3
  359.7 0.5 copy.73
  360.2 0.3 copy.72
  360.5 0.2 fusion.3
  360.6 0.9 pad.21.keys_ref
  361.5 101.3 %expert_rest.1 = (bf16[16,2,144,512]{3,2,1,0:T(8,128)(2,1)}, bf16[16,2,32,2048]{3,2,1,0:T(8,128)(2,1)}, bf16[16,2,128,512]{3,2,1,0:T(8,128)(2,1)}) custom-call(bf16[16,2,128,512]{3,2,1,0:T(8,128)(2,1)} %bitcast.76, bf16[16,2,128,512]{3,2,1,0:T(8,128)(2,1)} %bitcast.79, bf16[2,2048,2048]{2,1,0:T(8,128)(2,1)} %get-tuple-element.42.g_ref, ...), custom_call_target="tpu_custom_call" | custom-call | flops 34359738368 | bytes 60000000 | tf_op jit(solution)/shard_map/expert_rest/pallas_call | solution.py:811
  462.9 35.6 %gather.1 = (f32[1040,512]{1,0:T(8,128)}, f32[1040,128]{1,0:T(8,128)}) custom-call(bf16[2,1040,128]{2,1,0:T(8,128)(2,1)} %pad.21.keys_ref, bf16[8,2,2,144,512]{4,3,2,1,0:T(8,128)(2,1)} %bitcast.74), custom_call_target="tpu_custom_call" | custom-call | flops 30000001024 | bytes 7000000 | tf_op jit(solution)/shard_map/gather/pallas_call | solution.py:438
  498.5 8.6 %all-to-all-start.2 = ((bf16[16,2,32,2048]{3,2,1,0:T(8,128)(2,1)}), bf16[16,2,32,2048]{3,2,1,0:T(8,128)(2,1)}, u32[]{:S(2)}, u32[]{:S(2)}) async-start(bf16[16,2,32,2048]{3,2,1,0:T(8,128)(2,1)} %get-tuple-element.55), calls=%async_computation.2 | async-start | bytes 8388608 | tf_op jit(solution)/shard_map/all_to_all | solution.py:896
  507.1 30.8 %attend_back.1 = (f32[5,208,512]{2,1,0:T(8,128)}, bf16[512,2176]{1,0:T(8,128)(2,1)}) custom-call(bf16[5,208,512]{2,1,0:T(8,128)(2,1)} %pad.22.x_ref, bf16[512,2176]{1,0:T(8,128)(2,1)} %bitcast.72, bf16[128,128]{1,0:T(8,128)(2,1)} %fusion.4.order_ref, bf16[5,208,1536]{2,1,0:T(8,128)(2,1)} %get-tuple-element.46.qkv_ref, ...), custom_call_target="tpu_custom_call" | custom-call | flops 20000000000 | bytes 16000000 | tf_op jit(solution)/shard_map/attend_back/pallas_call | solution.py:204
  537.9 98.7 %close.1 = (bf16[1040,512]{1,0:T(8,128)(2,1)}, f32[32,2176]{1,0:T(8,128)}) custom-call(bf16[2,1040,128]{2,1,0:T(8,128)(2,1)} %pad.21.keys_ref, f32[1040,128]{1,0:T(8,128)} %bitcast.84, f32[1040,512]{1,0:T(8,128)} %bitcast.81, bf16[1040,640]{1,0:T(8,128)(2,1)} %get-tuple-element.39.theirs_ref, bf16[8,2,2,128,512]{4,3,2,1,0:T(8,128)(2,1)} %bitcast.77, ...), custom_call_target="tpu_custom_call" | custom-call | flops 60000002048 | bytes 10000000 | tf_op jit(solution)/shard_map/close/pallas_call | solution.py:579
  636.6 1.6 slice.39
  638.2 0.8 slice.43
  639.1 1.5 slice.40
  640.5 1.7 slice.36
  642.3 1.5 reshape.170
  643.8 0.1 slice.45
  643.9 1.2 reshape.169
  645.1 0.1 copy.84
  645.2 0.7 copy.86
  645.9 1.6 slice_reduce_fusion
  647.5 5.5 convert_reduce_fusion
  652.9 0.0 all-to-all-done.2
  653.0 5.6 convert_reduce_fusion.1
  (38 shorter events, 0.2 us)
Async XLA Ops:
  0.6 17.2 %collective-permute-start = (s32[985,2]{0,1:T(2,128)}, s32[985,2]{0,1:T(2,128)S(1)}, u32[]{:S(2)}, u32[]{:S(2)}) collective-permute-start(s32[985,2]{0,1:T(2,128)} %param.13), channel_id=1, source_target_pairs={{0,8},{2,10},{4,12},{6,14},{8,0},{10,2},{12,4},{14,6},{1,9},{3,11}... | collective-permute-start | bytes 23648 | tf_op jit(solution)/shard_map/ppermute | solution.py:911
  5.8 7.2 %copy-start.10 = (f32[32]{0:T(128)S(1)}, f32[32]{0:T(128)}, u32[]{:S(2)}) copy-start(f32[32]{0:T(128)} %param.14) | copy-start | bytes 388
  5.8 7.2 %copy-start.11 = (f32[32]{0:T(128)S(1)}, f32[32]{0:T(128)}, u32[]{:S(2)}) copy-start(f32[32]{0:T(128)} %param.15) | copy-start | bytes 388
  5.8 7.2 %copy-start.12 = (f32[32]{0:T(128)S(1)}, f32[32]{0:T(128)}, u32[]{:S(2)}) copy-start(f32[32]{0:T(128)} %param.18) | copy-start | bytes 388
  5.8 7.9 %copy-start.13 = (f32[32]{0:T(128)S(1)}, f32[32]{0:T(128)}, u32[]{:S(2)}) copy-start(f32[32]{0:T(128)} %param.19) | copy-start | bytes 388
  5.8 7.9 %copy-start = (bf16[985,512]{1,0:T(8,128)(2,1)S(1)}, bf16[985,512]{1,0:T(8,128)(2,1)}, u32[]{:S(2)}) copy-start(bf16[985,512]{1,0:T(8,128)(2,1)} %param.23) | copy-start | bytes 3025924
  5.8 8.2 %copy-start.3 = (f32[32,1536]{1,0:T(8,128)S(1)}, f32[32,1536]{1,0:T(8,128)}, u32[]{:S(2)}) copy-start(f32[32,1536]{1,0:T(8,128)} %param.16) | copy-start | bytes 589828
  5.8 8.2 %copy-start.7 = (f32[32,512]{1,0:T(8,128)S(1)}, f32[32,512]{1,0:T(8,128)}, u32[]{:S(2)}) copy-start(f32[32,512]{1,0:T(8,128)} %param.17) | copy-start | bytes 196612
  5.8 8.2 %copy-start.8 = (f32[32,32]{1,0:T(8,128)S(1)}, f32[32,32]{1,0:T(8,128)}, u32[]{:S(2)}) copy-start(f32[32,32]{1,0:T(8,128)} %param.20) | copy-start | bytes 12292
  5.8 8.8 %copy-start.1 = (bf16[985,512]{1,0:T(8,128)(2,1)S(1)}, bf16[985,512]{1,0:T(8,128)(2,1)}, u32[]{:S(2)}) copy-start(bf16[985,512]{1,0:T(8,128)(2,1)} %param.12) | copy-start | bytes 3025924
  5.8 171.9 %all-to-all-start = ((bf16[16,2,32,2048]{3,2,1,0:T(8,128)(2,1)}), bf16[16,2,32,2048]{3,2,1,0:T(8,128)(2,1)}, u32[]{:S(2)}, u32[]{:S(2)}) async-start(bf16[16,2,32,2048]{3,2,1,0:T(8,128)(2,1)} %pad_maximum_fusion), calls=%async_computation | async-start | bytes 8388608 | tf_op jit(solution)/shard_map/all_to_all | solution.py:893
  13.7 4.2 copy-start.9
  18.2 2.0 copy-start.4
  177.7 175.6 %all-to-all-start.1 = ((bf16[16,2,128,512]{3,2,1,0:T(8,128)(2,1)}), bf16[16,2,128,512]{3,2,1,0:T(8,128)(2,1)}, u32[]{:S(2)}, u32[]{:S(2)}) async-start(bf16[16,2,128,512]{3,2,1,0:T(8,128)(2,1)} %pad_maximum_fusion.1), calls=%async_computation.1 | async-start | bytes 8388608 | tf_op jit(solution)/shard_map/all_to_all | solution.py:893
  353.3 6.3 copy-start.5
  353.4 6.8 %copy-start.6 = (bf16[2,16,1040]{2,1,0:T(8,128)(2,1)S(1)}, bf16[2,16,1040]{2,1,0:T(8,128)(2,1)}, u32[]{:S(2)}) copy-start(bf16[2,16,1040]{2,1,0:T(8,128)(2,1)} %get-tuple-element.95) | copy-start | bytes 199684
  353.4 145.1 %all-to-all-start.3 = ((bf16[16,2,128,512]{3,2,1,0:T(8,128)(2,1)}), bf16[16,2,128,512]{3,2,1,0:T(8,128)(2,1)}, u32[]{:S(2)}, u32[]{:S(2)}) async-start(bf16[16,2,128,512]{3,2,1,0:T(8,128)(2,1)} %get-tuple-element.56), calls=%async_computation.3 | async-start | bytes 8388608 | tf_op jit(solution)/shard_map/all_to_all | solution.py:896
  498.5 154.5 %all-to-all-start.2 = ((bf16[16,2,32,2048]{3,2,1,0:T(8,128)(2,1)}), bf16[16,2,32,2048]{3,2,1,0:T(8,128)(2,1)}, u32[]{:S(2)}, u32[]{:S(2)}) async-start(bf16[16,2,32,2048]{3,2,1,0:T(8,128)(2,1)} %get-tuple-element.55), calls=%async_computation.2 | async-start | bytes 8388608 | tf_op jit(solution)/shard_map/all_to_all | solution.py:896
  638.2 5.6 copy-start.2

commit v5 on v4

v5 whole, which is shorter than its diff:
```python
from functools import partial

import jax
import jax.numpy as jnp
from jax import lax
from jax.experimental import pallas as pl
from jax.experimental.pallas import tpu as pltpu
from jax.sharding import Mesh
from jax.sharding import PartitionSpec as P

D = 512
HEADS = 8
EXPERTS = 32
SEQ = 197
CAP = 128
ROWS = 208
HEAD = D // HEADS
LANES = 128
QKV = 3 * D
SENT = D + LANES
PACKED = QKV + D + LANES
epsilon = 1e-06
low = jnp.bfloat16
full = jnp.float32
MESH = pl.DeviceIdType.MESH
BIG = 63 * 1024 * 1024


def dot(left, right):
    return jnp.dot(left, right, preferred_element_type=full)


def dot_rt(left, right):
    return lax.dot_general(left, right, (((1,), (1,)), ((), ())), preferred_element_type=full)


def dot_lt(left, right):
    return lax.dot_general(left, right, (((0,), (0,)), ((), ())), preferred_element_type=full)


def lanes_of(shape):
    return lax.broadcasted_iota(jnp.int32, shape, len(shape) - 1)


def normed_rows(values):
    center = values - jnp.mean(values, axis=-1, keepdims=True)
    factor = lax.rsqrt(jnp.mean(center * center, axis=-1, keepdims=True) + epsilon)
    return center * factor, factor


def norm_back(normed, factor, gain_vec, upstream):
    scaled = upstream * gain_vec
    return factor * (
        scaled
        - jnp.mean(scaled, axis=-1, keepdims=True)
        - normed * jnp.mean(scaled * normed, axis=-1, keepdims=True)
    )


def norm_vectors(weights_ref):
    rows = weights_ref[:, QKV + D :].astype(full).T
    return [rows[EXPERTS + i : EXPERTS + i + 1] for i in range(4)]


def halves(pair):
    first = lanes_of(pair.shape) < HEAD
    zero = jnp.zeros_like(pair)
    return jnp.where(first, pair, zero), jnp.where(first, zero, pair)


def head_probs(query, key_pair):
    scores = dot_rt(query, key_pair) * (HEAD**-0.5)
    scores = jnp.where(lanes_of(scores.shape) < SEQ, scores, -1e30)
    grown = jnp.exp(scores - jnp.max(scores, axis=-1, keepdims=True))
    return grown / jnp.sum(grown, axis=-1, keepdims=True)


def attend_kernel(
    sizes, x_ref, w_ref, order_ref, master_ref, _, qkv_ref, ctx_ref, r_ref, sent_ref, probs_ref, first_ref, flow
):
    def moved():
        return outward(sizes, wide_part, master_ref, first_ref, flow, GROUPS - 1, 0)

    @pl.when(pl.program_id(0) == 0)
    def _():
        greet(all_owners(*sizes[:2]))
        start(moved())

    gain_one, bias_one, gain_two, bias_two = norm_vectors(w_ref)
    x = x_ref[0].astype(full)
    normed, _ = normed_rows(x)
    attn_in = (normed * gain_one + bias_one).astype(low)
    qkv_ref[0] = dot(attn_in, w_ref[:, :QKV]).astype(low)
    for pair in range(HEADS // 2):
        at = pair * LANES
        query = halves(qkv_ref[0, :, at : at + LANES])
        key = qkv_ref[0, :, D + at : D + at + LANES]
        value = halves(qkv_ref[0, :, 2 * D + at : 2 * D + at + LANES])
        total = None
        for i in range(2):
            part = dot(head_probs(query[i], key).astype(low), value[i])
            total = part if total is None else total + part
        ctx_ref[0, :, at : at + LANES] = total.astype(low)
    r = x + dot(ctx_ref[0], w_ref[:, QKV : QKV + D])
    r_ref[0] = r
    normed, _ = normed_rows(r)
    h = (normed * gain_two + bias_two).astype(low)
    sent_ref[0, :, :D] = h
    logits = dot(h, dot(w_ref[:, QKV + D :], order_ref[...]).astype(low))
    logits = jnp.where(lanes_of(logits.shape) < EXPERTS, logits, -1e30)
    grown = jnp.exp(logits - jnp.max(logits, axis=-1, keepdims=True))
    probs = grown / jnp.sum(grown, axis=-1, keepdims=True)
    probs_ref[0] = probs
    sent_ref[0, :, D:] = pltpu.roll(probs, LANES - EXPERTS // 2, 1).astype(low)

    @pl.when(pl.program_id(0) == pl.num_programs(0) - 1)
    def _():
        wait(moved())


def image_spec(width):
    return pl.BlockSpec((1, ROWS, width), lambda i: (i, 0, 0))


def whole_spec(shape):
    return pl.BlockSpec(shape, lambda *_: (0,) * len(shape))


def params(n):
    return pltpu.CompilerParams(
        dimension_semantics=("arbitrary",) * n, vmem_limit_bytes=BIG
    )


def remote_params(n, number):
    return pltpu.CompilerParams(
        dimension_semantics=("arbitrary",) * n,
        vmem_limit_bytes=BIG,
        collective_id=number,
        has_side_effects=True,
    )


def attend(x, weights, order, master, first, sizes, number):
    images = x.shape[0]
    shapes = ((QKV, low), (D, low), (D, full), (SENT, low), (LANES, full))
    outer = pl.BlockSpec(memory_space=pl.ANY)
    return pl.pallas_call(
        partial(attend_kernel, sizes),
        grid=(images,),
        in_specs=[image_spec(D), whole_spec(weights.shape), whole_spec(order.shape), outer, outer],
        out_specs=[image_spec(width) for width, _ in shapes] + [outer],
        out_shape=[jax.ShapeDtypeStruct((images, ROWS, w), t) for w, t in shapes]
        + [jax.ShapeDtypeStruct(first.shape, low)],
        input_output_aliases={4: 5},
        scratch_shapes=[flow_semaphores(sizes, 1)],
        compiler_params=remote_params(1, number),
        cost_estimate=pl.CostEstimate(
            flops=8 * 10**9, bytes_accessed=12 * 10**6, transcendentals=2 * 10**6
        ),
        name="attend",
    )(x, weights, order, master, first)


def device(offset):
    names = ("replica", "part", "expert")
    return tuple(lax.axis_index(name) ^ o for name, o in zip(names, offset))


def near(groups, j):
    return (0, j // groups, j % groups)


def greet(offsets):
    barrier = pltpu.get_barrier_semaphore()
    for offset in offsets:
        pl.semaphore_signal(barrier, inc=1, device_id=device(offset), device_id_type=MESH)
    pl.semaphore_wait(barrier, len(offsets))


def remote(source, target, send, receive, offset):
    return pltpu.make_async_remote_copy(
        src_ref=source,
        dst_ref=target,
        send_sem=send,
        recv_sem=receive,
        device_id=device(offset),
        device_id_type=MESH,
    )


def owners_like(replicas, parts):
    return [(r, p, 0) for r in range(replicas) for p in range(0, parts, 2) if (r, p) != (0, 0)]


def owner(parts, offset=(0, 0, 0)):
    return (lax.axis_index("replica") ^ offset[0]) * parts + (lax.axis_index("part") ^ offset[1])


CORE = (0, 1, 0)
GROUPS = 4


def all_owners(replicas, parts):
    return [(r, p, 0) for r in range(replicas) for p in range(parts) if (r, p) != (0, 0)]


def wide_part(ref, at, g):
    width = ref.shape[-1] // GROUPS
    return ref.at[at, ..., pl.ds(g * width, width)]


def narrow_part(ref, at, g):
    width = ref.shape[-1] // (2 * GROUPS)
    return ref.at[at, ..., pl.ds(g * width, width)]


def tall_part(ref, at, g):
    depth = ref.shape[-2] // GROUPS
    return ref.at[at, ..., pl.ds(g * depth, depth), :]


def outward(sizes, part_of, source, target, semaphores, g, slot):
    _, parts, _ = sizes
    own = target.shape[1]
    here = owner(parts)

    def block(p):
        return part_of(source, pl.ds((lax.axis_index("part") ^ p) * own, own), g)

    copies = [
        remote(block(o[1]), part_of(target, here, g), semaphores.at[0, slot, i], semaphores.at[1, slot, i], o)
        for i, o in enumerate(all_owners(*sizes[:2]))
    ]
    last = semaphores.at[0, slot, len(copies)]
    return copies + [pltpu.make_async_copy(block(0), part_of(target, here, g), last)]


def across(sizes, part_of, source, target, semaphores, g, slot):
    replicas, parts, _ = sizes

    def rows(r):
        return pl.ds((lax.axis_index("replica") ^ r) * parts, parts)

    return [
        remote(
            part_of(source, rows(r), g), part_of(target, r - 1, g),
            semaphores.at[0, slot, r], semaphores.at[1, slot, r], (r, 0, 0),
        )
        for r in range(1, replicas)
    ]


def homeward(sizes, part_of, source, target, semaphores, g, slot):
    _, parts, _ = sizes
    here = lax.axis_index("part")
    copies = [
        remote(
            part_of(source, here ^ p, g), part_of(target, here, g),
            semaphores.at[0, slot, p], semaphores.at[1, slot, p], (0, p, 0),
        )
        for p in range(1, parts)
    ]
    last = semaphores.at[0, slot, 0]
    return copies + [pltpu.make_async_copy(part_of(source, here, g), part_of(target, here, g), last)]


def partners(sizes):
    replicas, parts, _ = sizes
    return {(0, p, 0) for p in range(1, parts)} | {(r, 0, 0) for r in range(1, replicas)}


def mine_of(sizes, dw_ref):
    return dw_ref.at[pl.ds(lax.axis_index("replica") * sizes[1], sizes[1])]


def pieces_of(sizes, dw):
    return jax.ShapeDtypeStruct((sizes[0] - 1, sizes[1], *dw.shape[1:]), low)


def start(copies):
    for copy in copies:
        copy.start()


def wait(copies):
    for copy in copies:
        copy.wait()


def flow_semaphores(sizes, slots):
    return pltpu.SemaphoreType.DMA((2, slots, sizes[0] * sizes[1]))


def swap_slots(groups, keys_ref, blocks, out_ref, sends, receives, local):
    _, count, own, tokens = keys_ref.shape
    slots = lax.broadcasted_iota(jnp.int32, (CAP, tokens), 0).astype(full)

    def build(s, source_ref):
        copies = []
        for j in [*range(1, count), 0]:
            picks = [(keys_ref[s, j, i : i + 1] == slots).astype(low) for i in range(own)]
            picks = jnp.concatenate(picks, axis=0) if own > 1 else picks[0]
            rows = dot(picks, source_ref[:, :D]).astype(low)
            blocks[j, s] = rows.reshape(own, CAP, D)
            if j:
                copy = remote(
                    blocks.at[j, s], out_ref.at[j, s], sends.at[j, s], receives.at[j, s],
                    near(groups, j),
                )
            else:
                copy = pltpu.make_async_copy(blocks.at[0, s], out_ref.at[0, s], local.at[s])
            copy.start()
            copies.append(copy)
        return copies

    return build


def open_kernel(
    sizes, keys_ref, rows_ref, shard_ref, master_ref, out_ref, weights_ref, first_ref,
    blocks, other, hop, sends, receives, local, flow, early, late, here,
):
    replicas, parts, groups = sizes
    count = keys_ref.shape[1]
    mirror = (0, parts // 2, 0)
    owners = owners_like(replicas, parts)
    greet(
        sorted({near(groups, j) for j in range(1, count)} | {mirror, *all_owners(replicas, parts)})
    )
    hops = remote(rows_ref, other, hop.at[0], hop.at[1], mirror)
    hops.start()
    mine = weights_ref.at[owner(parts)]
    gathers = [
        remote(shard_ref, mine, early.at[0, i], early.at[1, i], o) for i, o in enumerate(owners)
    ]
    passes = [remote(shard_ref, mine, late.at[0, 0], late.at[1, 0], CORE)]
    for i, o in enumerate(owners):
        slot = weights_ref.at[owner(parts, o)]
        passes.append(remote(slot, slot, late.at[0, i + 1], late.at[1, i + 1], CORE))
    start(gathers)
    passes[0].start()
    kept = pltpu.make_async_copy(shard_ref, mine, here)
    kept.start()
    parts_of = [
        outward(sizes, wide_part, master_ref, first_ref, flow, g, g) for g in range(GROUPS - 1)
    ]
    start(parts_of[0])
    build = swap_slots(groups, keys_ref, blocks, out_ref, sends, receives, local)
    copies = build(0, rows_ref)
    start(parts_of[1])
    for i, copy in enumerate(gathers):
        copy.wait_recv()
        passes[i + 1].start()
    hops.wait_recv()
    copies += build(1, other)
    start(parts_of[2])
    hops.wait_send()
    wait(copies)
    for copy in gathers:
        copy.wait_send()
    wait(passes)
    kept.wait()
    for group in parts_of:
        wait(group)


def dispatch_kernel(
    sizes, keys_ref, rows_ref, master_ref, out_ref, other_ref, second_ref,
    blocks, other, hop, sends, receives, local, flow,
):
    replicas, parts, groups = sizes
    count = keys_ref.shape[1]
    mirror = (0, parts // 2, 0)
    greet(
        sorted({near(groups, j) for j in range(1, count)} | {mirror, *all_owners(replicas, parts)})
    )
    hops = remote(rows_ref, other, hop.at[0], hop.at[1], mirror)
    hops.start()
    build = swap_slots(groups, keys_ref, blocks, out_ref, sends, receives, local)
    copies = build(0, rows_ref)
    more = [outward(sizes, tall_part, master_ref, second_ref, flow, g, g) for g in range(3)]
    start(more[0])
    start(more[1])
    hops.wait()
    copies += build(1, other)
    start(more[2])
    keep = pltpu.make_async_copy(other, other_ref, local.at[2])
    keep.start()
    keep.wait()
    wait(copies)
    for group in more:
        wait(group)


def dispatch(keys, rows, sizes, number, master, shard=None):
    replicas, parts, groups = sizes
    _, count, own, tokens = keys.shape
    shape = (count, 2, own, CAP, D)
    owners = replicas * parts
    opening = number == 0
    inner = pl.BlockSpec(memory_space=pltpu.VMEM)
    outer = pl.BlockSpec(memory_space=pl.ANY)
    whole = jax.ShapeDtypeStruct((owners, own, *master.shape[1:]), low)
    outs = [jax.ShapeDtypeStruct(shape, low)]
    semaphores = [(2,), (count, 2), (count, 2), (3,)]
    scratch = [pltpu.VMEM(shape, low), pltpu.VMEM(rows.shape, low)]
    scratch += [pltpu.SemaphoreType.DMA(n) for n in semaphores] + [flow_semaphores(sizes, 3)]
    if opening:
        arrays = (keys, rows, shard, master)
        outs += [jax.ShapeDtypeStruct((owners, *shard.shape), low), whole]
        more = [(2, owners // 2 - 1), (2, owners // 2), ()]
        scratch += [pltpu.SemaphoreType.DMA(n) for n in more]
    else:
        arrays = (keys, rows, master)
        outs += [jax.ShapeDtypeStruct(rows.shape, low), whole]
    return pl.pallas_call(
        partial(open_kernel if opening else dispatch_kernel, sizes),
        in_specs=[inner, inner] + [outer] * (len(arrays) - 2),
        out_specs=[outer] * len(outs),
        out_shape=outs,
        scratch_shapes=scratch,
        compiler_params=pltpu.CompilerParams(
            vmem_limit_bytes=BIG, collective_id=number, has_side_effects=True
        ),
        cost_estimate=pl.CostEstimate(
            flops=60 * 10**9, bytes_accessed=5 * 10**6, transcendentals=0
        ),
        name="open" if opening else "dispatch",
    )(*arrays)


def chooser(own, j):
    shape = (LANES, own * CAP)
    expert = lax.broadcasted_iota(jnp.int32, shape, 0)
    slot = lax.broadcasted_iota(jnp.int32, shape, 1)
    return (expert == j * own + slot // CAP).astype(low)


def attend_back(i, weights, held, acc, dqkv, dx_ref):
    w_ref, order_ref = weights
    x_ref, qkv_ref, ctx_ref, r_ref, h_ref, probs_ref, dy_ref, dh_ref, dprobs_ref = held
    qkv_acc, proj_acc, router_acc, norm_acc = acc
    rows = pl.ds(pl.multiple_of(i * ROWS, ROWS), ROWS)
    gain_one, bias_one, gain_two, _ = norm_vectors(w_ref)
    probs, dprobs = probs_ref[i], dprobs_ref[rows]
    dlogits = (probs * (dprobs - jnp.sum(probs * dprobs, axis=-1, keepdims=True))).astype(low)
    router_acc[...] += dot_lt(h_ref[i], dlogits)
    router = dot(w_ref[:, QKV + D :], order_ref[...]).astype(low)
    dh = dh_ref[rows] + dot_rt(dlogits, router)
    normed, factor = normed_rows(r_ref[i])
    norm_acc[2:3] += jnp.sum(dh * normed, axis=0, keepdims=True)
    norm_acc[3:4] += jnp.sum(dh, axis=0, keepdims=True)
    dr = dy_ref[i].astype(full) + norm_back(normed, factor, gain_two, dh)
    dattended = dr.astype(low)
    proj_acc[...] += dot_lt(ctx_ref[i], dattended)
    dctx = dot_rt(dattended, w_ref[:, QKV : QKV + D]).astype(low)
    for pair in range(HEADS // 2):
        at = pair * LANES
        query = halves(qkv_ref[i, :, at : at + LANES])
        key = qkv_ref[i, :, D + at : D + at + LANES]
        keys = halves(key)
        value = qkv_ref[i, :, 2 * D + at : 2 * D + at + LANES]
        dhead = halves(dctx[:, at : at + LANES])
        dq = dk = dv = None
        for e in range(2):
            p = head_probs(query[e], key)
            dp = dot_rt(dhead[e], value)
            ds = (p * (dp - jnp.sum(p * dp, axis=-1, keepdims=True))).astype(low)
            terms = dot(ds, keys[e]), dot_lt(ds, query[e]), dot_lt(p.astype(low), dhead[e])
            dq, dk, dv = terms if dq is None else (dq + terms[0], dk + terms[1], dv + terms[2])
        dqkv[:, at : at + LANES] = (dq * HEAD**-0.5).astype(low)
        dqkv[:, D + at : D + at + LANES] = (dk * HEAD**-0.5).astype(low)
        dqkv[:, 2 * D + at : 2 * D + at + LANES] = dv.astype(low)
    normed, factor = normed_rows(x_ref[i].astype(full))
    attn_in = (normed * gain_one + bias_one).astype(low)
    qkv_acc[...] += dot_lt(attn_in, dqkv[...])
    da = dot_rt(dqkv[...], w_ref[:, :QKV])
    norm_acc[0:1] += jnp.sum(da * normed, axis=0, keepdims=True)
    norm_acc[1:2] += jnp.sum(da, axis=0, keepdims=True)
    dx_ref[i] = dr + norm_back(normed, factor, gain_one, da)


def close_kernel(
    sizes, keys_ref, back_ref, w_ref, order_ref, x_ref, qkv_ref, ctx_ref, r_ref, sent_ref, probs_ref, dy_ref,
    theirs_ref, y_ref, dw_one_ref, dw_two_ref, got_two_ref,
    dx_ref, out_ref, total_ref, one_ref, two_ref,
    xs, qkvs, ctxs, rs, hs, ps, dys, their_probs, ys, dh, dprobs, sent, got, sent_two, got_two,
    mine_one, others_one, mine_two, others_two,
    dqkv, qkv_acc, proj_acc, router_acc, norm_acc, grads, kept, first, second, third,
    loads, y_sends, y_receives, hops, hops_two, flow, home_one, home_two,
    core_sems, owner_sems, expert_sems,
):
    replicas, parts, groups = sizes
    count, _, own, _, _ = y_ref.shape
    images = x_ref.shape[0]
    width = own * CAP
    half = count * own
    mirror = (0, parts // 2, 0)
    owners = owners_like(replicas, parts)
    sideways = [(0, 0, g) for g in range(1, groups)]
    peers = {near(groups, j) for j in range(1, count)} | {mirror, *sideways, *owners}
    greet(sorted(peers | partners(sizes)))

    pairs_of = [
        (r_ref, rs), (theirs_ref.at[:, D:], their_probs), (x_ref, xs), (qkv_ref, qkvs), (ctx_ref, ctxs),
        (sent_ref.at[:, :, :D], hs), (probs_ref, ps), (dy_ref, dys),
        (mine_of(sizes, dw_two_ref), mine_two), (got_two_ref, others_two),
        (mine_of(sizes, dw_one_ref), mine_one), (y_ref.at[0], ys.at[0]),
    ]
    loading = [
        pltpu.make_async_copy(source, target, loads.at[i])
        for i, (source, target) in enumerate(pairs_of)
    ]
    swaps = [
        [
            remote(y_ref.at[j, s], ys.at[j, s], y_sends.at[j, s], y_receives.at[j, s], near(groups, j))
            for j in range(1, count)
        ]
        for s in range(2)
    ]
    eighths = [
        across(sizes, narrow_part, dw_one_ref, others_one, flow, g, g) for g in range(2 * GROUPS)
    ]
    start(swaps[1])
    start(swaps[0])
    start(eighths[0])
    start(eighths[1])
    start(loading)

    def rows_of(i):
        return pl.ds(pl.multiple_of(i * ROWS, ROWS), ROWS)

    def hop(i):
        rows = rows_of(i)
        return remote(sent.at[rows], got.at[rows], hops.at[0, i], hops.at[1, i], mirror)

    def hop_two(i):
        rows = rows_of(i)
        return remote(sent_two.at[rows], got_two.at[rows], hops_two.at[0, i], hops_two.at[1, i], mirror)

    def gathered(s, rows):
        slot = (lanes_of((ROWS, width)) % CAP).astype(full)
        lane = lanes_of((ROWS, LANES))
        keys = keys_ref[s, rows]
        total = jnp.zeros((ROWS, D), full)
        change = jnp.zeros((ROWS, LANES), full)
        for j in range(count):
            here = dot(keys, chooser(own, j)) == slot
            total = total + dot(here.astype(low), back_ref[j, s, :, :CAP].reshape(width, D))
            dgate = back_ref[j, s, :, CAP : CAP + 1].astype(full)
            dgate = dgate[:, :, :CAP] + dgate[:, :, CAP : 2 * CAP]
            for e in range(own):
                agreed = jnp.where(here[:, e * CAP : (e + 1) * CAP], dgate[e], 0.0)
                column = jnp.sum(agreed, axis=-1, keepdims=True)
                change = jnp.where(lane == j * own + e, column, change)
        return total, change

    def weighted(s, rows, probs):
        slot = (lanes_of((ROWS, width)) % CAP).astype(full)
        keys = keys_ref[s, rows]
        total = jnp.zeros((ROWS, D), full)
        for j in range(count):
            spread = chooser(own, j)
            gate = jnp.where(dot(keys, spread) == slot, dot(probs, spread), 0.0)
            total = total + dot(gate.astype(low), ys[j, s].reshape(width, D))
        return total

    @pl.loop(0, images)
    def _(i):
        rows = rows_of(i)
        total, change = gathered(1, rows)
        sent[rows, :D] = total.astype(low)
        high = change.astype(low)
        rest = pltpu.roll(change - high.astype(full), half, 1)
        sent[rows, D:] = (high.astype(full) + rest).astype(low)
        hop(i).start()

    start(eighths[2])

    @pl.loop(0, images)
    def _(i):
        rows = rows_of(i)
        dh[rows], dprobs[rows] = gathered(0, rows)

    wait(loading)
    wait(swaps[1])

    @pl.loop(0, images)
    def _(i):
        rows = rows_of(i)
        sent_two[rows] = weighted(1, rows, their_probs[rows]).astype(low)
        hop_two(i).start()

    start(eighths[3])

    @pl.loop(0, images)
    def _(i):
        rows = rows_of(i)
        hop(i).wait()
        dh[rows] += got[rows, :D].astype(full)
        pair = got[rows, D:].astype(full)
        lane = lanes_of(pair.shape)
        whole = pair + pltpu.roll(pair, half, 1)
        dprobs[rows] += jnp.where((lane >= half) & (lane < 2 * half), whole, 0.0)

    for g in range(GROUPS, 2 * GROUPS):
        start(eighths[g])

    def add(mine, others, columns):
        @pl.loop(0, parts)
        def _(p):
            total = mine[p, :, :, columns].astype(full)
            for r in range(replicas - 1):
                total = total + others[r, p, :, :, columns].astype(full)
            mine[p, :, :, columns] = total.astype(low)

    add(mine_two, others_two, slice(None))
    homes = homeward(sizes, lambda ref, at, g: ref.at[at], mine_two, two_ref, home_two, 0, 0)
    start(homes)
    for ref in (qkv_acc, proj_acc, router_acc, norm_acc):
        ref[...] = jnp.zeros_like(ref)

    @pl.loop(0, images)
    def _(i):
        attend_back(
            i, (w_ref, order_ref), (xs, qkvs, ctxs, rs, hs, ps, dys, dh, dprobs),
            (qkv_acc, proj_acc, router_acc, norm_acc), dqkv, dx_ref,
        )

    columns = norm_acc[...].T
    shifted = pltpu.roll(columns, EXPERTS, 1)
    tile = jnp.where(lanes_of(shifted.shape) < EXPERTS, router_acc[...], shifted)
    router_acc[...] = dot_rt(tile.astype(low), order_ref[...])
    depth = grads.shape[1]
    core = lax.axis_index("part") % 2
    blocks = replicas * parts // 2

    @pl.loop(0, 2 * blocks)
    def _(o):
        rows = pl.ds(pl.multiple_of(o * depth, depth), depth)
        grads[o, :, :QKV] = qkv_acc[rows].astype(low)
        grads[o, :, QKV : QKV + D] = proj_acc[rows].astype(low)
        grads[o, :, QKV + D :] = router_acc[rows].astype(low)

    to_core = [
        remote(grads.at[2 * i + 1 - core], first.at[i], core_sems.at[0, i], core_sems.at[1, i], CORE)
        for i in range(blocks)
    ]
    start(to_core)
    for i in range(blocks):
        to_core[i].wait()
        kept[i] = (grads[2 * i + core].astype(full) + first[i].astype(full)).astype(low)
    to_owner = [
        remote(kept.at[owner(parts, o) // 2], second.at[i], owner_sems.at[0, i], owner_sems.at[1, i], o)
        for i, o in enumerate(owners)
    ]
    start(to_owner)

    each = mine_one.shape[-1] // GROUPS
    for g in range(GROUPS):
        wait(eighths[2 * g])
        wait(eighths[2 * g + 1])
        add(mine_one, others_one, slice(g * each, (g + 1) * each))
        copies = homeward(sizes, wide_part, mine_one, one_ref, home_one, g, g)
        start(copies)
        homes += copies
    wait(swaps[0])

    @pl.loop(0, images)
    def _(i):
        rows = rows_of(i)
        total = rs[i] + weighted(0, rows, ps[i].astype(low))
        hop_two(i).wait()
        out_ref[rows] = (total + got_two[rows].astype(full)).astype(low)

    total = kept[owner(parts) // 2].astype(full)
    for i, copy in enumerate(to_owner):
        copy.wait()
        total = total + second[i].astype(full)
    me = lax.axis_index("expert")
    third[me] = total.astype(low)
    to_others = [
        remote(third.at[me], third.at[me], expert_sems.at[0, i], expert_sems.at[1, i], o)
        for i, o in enumerate(sideways)
    ]
    start(to_others)
    wait(to_others)
    total = third[0].astype(full)
    for g in range(1, groups):
        total = total + third[g].astype(full)
    total_ref[...] = total
    wait(homes)


def close(keys, back, weights, order, x, qkv, ctx, r, sent, probs, dy, theirs, y, dw_one, dw_two, got_two, sizes, number):
    replicas, parts, groups = sizes
    images = x.shape[0]
    tokens = images * ROWS
    count = y.shape[0]
    owners = replicas * parts
    shard = (weights.shape[0] // owners, PACKED)
    one = (parts, *dw_one.shape[1:])
    two = (parts, *dw_two.shape[1:])
    inner = pl.BlockSpec(memory_space=pltpu.VMEM)
    outer = pl.BlockSpec(memory_space=pl.ANY)
    buffers = [
        (x.shape, low), (qkv.shape, low), (ctx.shape, low), (r.shape, full), (x.shape, low),
        (probs.shape, full), (dy.shape, low), ((tokens, LANES), low), (y.shape, low),
        ((tokens, D), full), ((tokens, LANES), full),
        ((tokens, SENT), low), ((tokens, SENT), low), ((tokens, D), low), ((tokens, D), low),
        (one, low), ((replicas - 1, *one), low), (two, low), ((replicas - 1, *two), low),
        ((ROWS, QKV), low), ((D, QKV), full), ((D, D), full), ((D, LANES), full), ((LANES, D), full),
        ((owners, *shard), low), ((owners // 2, *shard), low), ((owners // 2, *shard), low),
        ((owners // 2 - 1, *shard), low), ((groups, *shard), low),
    ]
    semaphores = [
        (12,), (count, 2), (count, 2), (2, images), (2, images), (2, 2 * GROUPS, replicas),
        (2, GROUPS, parts), (2, 1, parts), (2, owners // 2), (2, owners // 2 - 1), (2, groups - 1),
    ]
    arrays = (
        keys, back, weights, order, x, qkv, ctx, r, sent, probs, dy, theirs, y, dw_one, dw_two, got_two,
    )
    return pl.pallas_call(
        partial(close_kernel, sizes),
        in_specs=[inner] * 4 + [outer] * 12,
        out_specs=[inner] * 3 + [outer] * 2,
        out_shape=[
            jax.ShapeDtypeStruct((images, ROWS, D), full),
            jax.ShapeDtypeStruct((tokens, D), low),
            jax.ShapeDtypeStruct(shard, full),
            jax.ShapeDtypeStruct(one, low),
            jax.ShapeDtypeStruct(two, low),
        ],
        scratch_shapes=[pltpu.VMEM(*b) for b in buffers]
        + [pltpu.SemaphoreType.DMA(n) for n in semaphores],
        compiler_params=pltpu.CompilerParams(
            vmem_limit_bytes=BIG, collective_id=number, has_side_effects=True
        ),
        cost_estimate=pl.CostEstimate(
            flops=60 * 10**9, bytes_accessed=30 * 10**6, transcendentals=2 * 10**6
        ),
        name="close",
    )(*arrays)


GELU = 0.7978845608028654
CUBE = 0.044715


def gelu_pair(u):
    square = u * u
    bent = jnp.tanh(u * (GELU * CUBE * square + GELU))
    half = 0.5 * bent + 0.5
    value = u * half
    return value, half + value * (1.0 - bent) * (3.0 * GELU * CUBE * square + GELU)


def first_kernel(
    sizes, h_ref, dy_ref, w_ref, wr_ref, sel_ref, master_ref, _, g_ref, slope_ref, dw_ref, second_ref,
    gates, dye_t, flow,
):
    sources = h_ref.shape[0]
    tile = w_ref.shape[3]
    at = pl.program_id(0) * pl.num_programs(1) + pl.program_id(1)

    def moved(g):
        return outward(sizes, tall_part, master_ref, second_ref, flow, g, g - 3)

    @pl.when(at == 0)
    def _():
        greet(all_owners(*sizes[:2]))
        start(moved(3))

    @pl.when(pl.program_id(1) == 0)
    def _():
        for k in range(sources):
            rows = slice(k * CAP, (k + 1) * CAP)
            logits = dot(h_ref[k, 0], wr_ref[...])
            logits = jnp.where(lanes_of(logits.shape) < EXPERTS, logits, -1e30)
            grown = jnp.exp(logits - jnp.max(logits, axis=-1, keepdims=True))
            mine = jnp.sum(grown * sel_ref[0], axis=-1, keepdims=True)
            gate = mine / jnp.sum(grown, axis=-1, keepdims=True)
            gates[rows] = jnp.broadcast_to(gate, (CAP, LANES))
            dye_t[:, rows] = (dy_ref[k, 0].astype(full) * gate).T.astype(low)

    w = w_ref[:, 0].reshape(D, tile)
    for k in range(0, sources, 2):
        rows = slice(k * CAP, (k + 2) * CAP)
        value, slope = gelu_pair(dot(h_ref[k : k + 2, 0].reshape(2 * CAP, D), w))
        g_ref[0, rows] = value.astype(low)
        slope_ref[0, rows] = (slope * gates[rows, :1]).astype(low)
    grad = dot(dye_t[...], g_ref[0]).T
    dw_ref[:, 0] = grad.astype(low).reshape(dw_ref.shape[0], dw_ref.shape[2], D)

    @pl.when(at == pl.num_programs(0) * pl.num_programs(1) - 1)
    def _():
        wait(moved(3))


def slot_spec(sources):
    return pl.BlockSpec((sources, 1, CAP, D), lambda e, f: (0, e, 0, 0))


def expert_first(h, dy, w_in, w_router, select, master, second, sizes, tile, number):
    sources = h.shape[0]
    owners, own, depth, hidden = w_in.shape
    rows = sources * CAP
    per = hidden // owners
    hidden_spec = pl.BlockSpec((1, rows, tile), lambda e, f: (e, 0, f))
    return pl.pallas_call(
        partial(first_kernel, sizes),
        grid=(own, hidden // tile),
        in_specs=[
            slot_spec(sources),
            slot_spec(sources),
            pl.BlockSpec((owners, 1, depth, tile), lambda e, f: (0, e, 0, f)),
            whole_spec(w_router.shape),
            pl.BlockSpec((1, 1, LANES), lambda e, f: (e, 0, 0)),
            pl.BlockSpec(memory_space=pl.ANY),
            pl.BlockSpec(memory_space=pl.ANY),
        ],
        out_specs=[
            hidden_spec,
            hidden_spec,
            pl.BlockSpec((tile // per, 1, per, D), lambda e, f: (f, e, 0, 0)),
            pl.BlockSpec(memory_space=pl.ANY),
        ],
        out_shape=[
            jax.ShapeDtypeStruct((own, rows, hidden), low),
            jax.ShapeDtypeStruct((own, rows, hidden), low),
            jax.ShapeDtypeStruct((owners, own, per, D), low),
            jax.ShapeDtypeStruct(second.shape, low),
        ],
        input_output_aliases={6: 3},
        scratch_shapes=[
            pltpu.VMEM((rows, LANES), full), pltpu.VMEM((D, rows), low), flow_semaphores(sizes, 2),
        ],
        compiler_params=pltpu.CompilerParams(
            dimension_semantics=("arbitrary",) * 2,
            vmem_limit_bytes=BIG,
            collective_id=number,
            has_side_effects=True,
        ),
        cost_estimate=pl.CostEstimate(
            flops=4 * own * rows * D * hidden,
            bytes_accessed=50 * 10**6,
            transcendentals=own * rows * hidden,
        ),
        name="expert_first",
    )(h, dy, w_in, w_router, select, master, second)


def rest_kernel(
    sizes, own, steps, dy_ref, h_ref, g_ref, slope_ref, w_in_ref, w_out_ref, dw_two_ref,
    back_ref, dw_ref, y_ref, two_ref, du, acc, dgates, dgate_rows, h_t, staged, sends, receives, local, flow,
):
    replicas, parts, groups = sizes

    def moved(g):
        return across(sizes, tall_part, dw_two_ref, two_ref, flow, g, g)

    sources = dy_ref.shape[0]
    tile = slope_ref.shape[2]
    at = pl.program_id(0)
    phase, expert, step = at // (own * steps), at // steps % own, at % steps
    w_in = w_in_ref[:, 0].reshape(D, tile)
    w_out = w_out_ref[:, 0].reshape(tile, D)
    chunk = 2 * CAP

    def copy(k, e):
        return pltpu.make_async_remote_copy(
            src_ref=staged.at[k, e],
            dst_ref=back_ref.at[k, e],
            send_sem=sends.at[k, e],
            recv_sem=receives.at[k, e],
            device_id=device(near(groups, k // 2)),
            device_id_type=MESH,
        )

    def mine(k, e):
        return pltpu.make_async_copy(staged.at[k, e], back_ref.at[k, e], local.at[k, e])

    @pl.when(at == 0)
    def _():
        greet(sorted({near(groups, j) for j in range(1, sources // 2)} | partners(sizes)))
        start(moved(0))
        start(moved(1))

    @pl.when((phase != 1) & (step == 0))
    def _():
        acc[...] = jnp.zeros_like(acc)

    @pl.when(phase == 0)
    def _():
        @pl.when(step == 0)
        def _():
            dgates[...] = jnp.zeros_like(dgates)

        for k in range(0, sources, 2):
            rows = slice(k * CAP, (k + 2) * CAP)
            dg = dot_rt(dy_ref[k : k + 2, 0].reshape(chunk, D), w_out)
            change = (dg * slope_ref[0, rows].astype(full)).astype(low)
            du[expert * steps + step, rows] = change
            acc[rows] += dot_rt(change, w_in)
            agreed = dg * g_ref[0, rows].astype(full)
            dgates[rows] += sum(agreed[:, i : i + LANES] for i in range(0, tile, LANES))

        @pl.when(step == steps - 1)
        def _():
            sums = dgates[...]
            high = sums.astype(low)
            rest = (sums - high.astype(full)).astype(low)
            ones = jnp.ones((16, LANES), low)
            dgate_rows[...] = dot_rt(ones, high) + dot_rt(ones, rest)
            for k in range(sources):
                rows = slice(k * CAP, (k + 1) * CAP)
                staged[k, expert, :CAP] = acc[rows].astype(low)
                row = dgate_rows[:, rows]
                high = row.astype(low)
                staged[k, expert, CAP:, :CAP] = high
                staged[k, expert, CAP:, CAP : 2 * CAP] = (row - high.astype(full)).astype(low)
                staged[k, expert, CAP:, 2 * CAP :] = jnp.zeros((16, D - 2 * CAP), low)

        for e in range(own):
            @pl.when((step == steps - 1) & (expert == e))
            def _():
                for k in range(2, sources):
                    copy(k, e).start()
                mine(0, e).start()
                mine(1, e).start()

    @pl.when(at == own * steps)
    def _():
        start(moved(2))
        start(moved(3))

    @pl.when(phase == 1)
    def _():
        @pl.when(step == 0)
        def _():
            for k in range(sources):
                h_t[:, k * CAP : (k + 1) * CAP] = h_ref[k, 0].T

        grad = dot(h_t[...], du[expert * steps + step]).astype(low)
        dw_ref[:, 0] = grad.reshape(dw_ref.shape[0], dw_ref.shape[2], tile)

    @pl.when(phase == 2)
    def _():
        for k in range(0, sources, 2):
            rows = slice(k * CAP, (k + 2) * CAP)
            acc[rows] += dot(g_ref[0, rows], w_out)

        @pl.when(step == steps - 1)
        def _():
            y_ref[:, 0] = acc[...].astype(low).reshape(sources, CAP, D)

    @pl.when(at == 3 * own * steps - 1)
    def _():
        for e in range(own):
            for k in range(2, sources):
                copy(k, e).wait()
            mine(0, e).wait()
            mine(1, e).wait()
        for g in range(GROUPS):
            wait(moved(g))


def expert_rest(dy, h, g, slope, w_in, w_out, dw_two, tile, sizes, number):
    sources, own, _, _ = dy.shape
    owners, _, depth, hidden = w_in.shape
    rows = sources * CAP
    per = hidden // owners
    steps = hidden // tile
    last = own * steps - 1

    def during(phases):
        def find(at):
            if 0 in phases and 2 in phases:
                inside = jnp.where(at // (last + 1) == 1, last, at % (last + 1))
            else:
                inside = jnp.clip(at - phases[0] * (last + 1), 0, last)
            return inside // steps, inside % steps

        return find

    def spec(shape, phases, index, buffers=2):
        return pl.BlockSpec(
            shape, lambda at: index(*during(phases)(at)), pipeline_mode=pl.Buffered(buffers)
        )

    token, hidden_at = (sources, 1, CAP, D), (1, rows, tile)
    whole_expert = lambda e, f: (0, e, 0, 0)
    in_tile = lambda e, f: (0, e, 0, f)
    return pl.pallas_call(
        partial(rest_kernel, sizes, own, steps),
        grid=(3 * own * steps,),
        in_specs=[
            spec(token, (0,), whole_expert, 1),
            spec(token, (1,), whole_expert, 1),
            spec(hidden_at, (0, 2), lambda e, f: (e, 0, f)),
            spec(hidden_at, (0,), lambda e, f: (e, 0, f)),
            spec((owners, 1, depth, tile), (0,), in_tile),
            spec((tile // per, 1, per, D), (0, 2), lambda e, f: (f, e, 0, 0)),
            pl.BlockSpec(memory_space=pl.ANY),
        ],
        out_specs=[
            pl.BlockSpec(memory_space=pl.ANY),
            spec((owners, 1, depth, tile), (1,), in_tile),
            spec(token, (2,), whole_expert),
            pl.BlockSpec(memory_space=pl.ANY),
        ],
        out_shape=[
            jax.ShapeDtypeStruct((sources, own, CAP + 16, D), low),
            jax.ShapeDtypeStruct(w_in.shape, low),
            jax.ShapeDtypeStruct(dy.shape, low),
            pieces_of(sizes, dw_two),
        ],
        scratch_shapes=[
            pltpu.VMEM((own * steps, rows, tile), low),
            pltpu.VMEM((rows, D), full),
            pltpu.VMEM((rows, LANES), full),
            pltpu.VMEM((16, rows), full),
            pltpu.VMEM((D, rows), low),
            pltpu.VMEM((sources, own, CAP + 16, D), low),
            pltpu.SemaphoreType.DMA((sources, own)),
            pltpu.SemaphoreType.DMA((sources, own)),
            pltpu.SemaphoreType.DMA((2, own)),
            flow_semaphores(sizes, GROUPS),
        ],
        compiler_params=pltpu.CompilerParams(
            dimension_semantics=("arbitrary",),
            vmem_limit_bytes=BIG,
            collective_id=number,
            has_side_effects=True,
        ),
        cost_estimate=pl.CostEstimate(
            flops=8 * own * rows * D * hidden, bytes_accessed=60 * 10**6, transcendentals=0
        ),
        name="expert_rest",
    )(dy, h, g, slope, w_in, w_out, dw_two)


ALL = ("replica", "part")


def body(
    tokens,
    choices,
    ln1_gain,
    ln1_bias,
    w_qkv,
    w_proj,
    ln2_gain,
    ln2_bias,
    w_router,
    w_expert_in,
    w_expert_out,
    cotangent,
):
    replicas, parts, groups = (lax.axis_size(name) for name in ("replica", "part", "expert"))
    owners = replicas * parts
    peers = parts * groups
    own = EXPERTS // peers
    images = tokens.shape[0] // SEQ
    count = images * ROWS
    tile = 512 * 16 // peers

    small_rows = w_router.shape[0]
    placed_router = (
        w_router.reshape(small_rows, groups, parts, own).transpose(0, 2, 1, 3).reshape(small_rows, EXPERTS)
    )
    vectors = jnp.stack([ln1_gain, ln1_bias, ln2_gain, ln2_bias], axis=1)
    packed = jnp.concatenate(
        [w_qkv, w_proj, placed_router, vectors, jnp.zeros((small_rows, LANES - EXPERTS - 4), full)],
        axis=1,
    ).astype(low)
    me = lax.axis_index("part") * groups + lax.axis_index("expert")
    sizes = (replicas, parts, groups)

    def padded(rows, fill=0):
        rows = rows.reshape(images, SEQ, rows.shape[1])
        return jnp.pad(rows, ((0, 0), (0, ROWS - SEQ), (0, 0)), constant_values=fill)

    x = padded(tokens)
    dy = padded(cotangent)
    half = parts // 2
    flips = [(i, i ^ half) for i in range(parts)]
    picks = jnp.stack([choices, lax.ppermute(choices, "part", flips)]).reshape(2 * images, SEQ, 2)
    picks = jnp.pad(picks, ((0, 0), (0, ROWS - SEQ), (0, 0)), constant_values=-1)
    picks = picks.reshape(2, count, 2)
    column = jnp.arange(EXPERTS)
    place = (me ^ (column // own)) * own + column % own
    expert = (place // own % groups) * (parts * own) + place // (groups * own) * own + place % own
    lane = jnp.arange(LANES)
    order = jnp.where(lane < EXPERTS, jnp.pad(place, (0, LANES - EXPERTS)), lane)
    order = (lane[:, None] == order[None, :]).astype(low)
    expert = expert[: EXPERTS // 2]
    named = (picks[:, :, :, None] == expert).any(axis=2)
    row = jnp.arange(count)
    earlier = (row[None, :] < row[:, None]).astype(low)
    slots = jnp.einsum("tu,sue->ste", earlier, named.astype(low), preferred_element_type=full)
    keys = jnp.where(named, slots, -1.0)
    key_rows = keys.transpose(0, 2, 1).reshape(2, peers // 2, own, count)
    key_columns = jnp.pad(
        keys, ((0, 0), (0, 0), (0, LANES - EXPERTS // 2)), constant_values=-1
    ).astype(low)

    first_master, second_master = w_expert_in.astype(low), w_expert_out.astype(low)
    dy_slots, weights, first_weight = dispatch(
        key_rows, dy.reshape(count, D), sizes, 0, first_master, packed
    )
    weights = weights.reshape(D, PACKED)
    qkv, ctx, r, sent, probs, first_weight = attend(
        x, weights, order, first_master, first_weight, sizes, 6
    )
    h_slots, theirs, second_weight = dispatch(
        key_rows, sent.reshape(count, SENT), sizes, 1, second_master
    )
    dy_slots = dy_slots.reshape(peers, own, CAP, D)
    h_slots = h_slots.reshape(peers, own, CAP, D)
    select = ((me * own + jnp.arange(own))[:, None, None] == lane[None, None, :]).astype(full)
    g, slope, dw_second, second_weight = expert_first(
        h_slots, dy_slots, first_weight, weights[:, QKV + D :], select, second_master, second_weight,
        sizes, tile, 5,
    )
    back, dw_first, y, got_second = expert_rest(
        dy_slots, h_slots, g, slope, first_weight, second_weight, dw_second, tile, sizes, 2
    )
    back = back.reshape(peers // 2, 2, own, CAP + 16, D)
    y = y.reshape(peers // 2, 2, own, CAP, D)
    dx, output, grads, first_grad, second_grad = close(
        key_columns, back, weights, order, x, qkv, ctx, r, sent, probs, dy, theirs, y,
        dw_first, dw_second, got_second, sizes, 3,
    )
    expert_in_grad = first_grad.reshape(w_expert_in.shape).astype(full)
    expert_out_grad = second_grad.reshape(w_expert_out.shape).astype(full)
    router_grad = (
        grads[:, QKV + D : QKV + D + EXPERTS]
        .reshape(small_rows, parts, groups, own)
        .transpose(0, 2, 1, 3)
        .reshape(small_rows, EXPERTS)
    )
    norms = [grads[:, QKV + D + EXPERTS + i] for i in range(4)]

    def unpadded(rows):
        return rows.reshape(images, ROWS, D)[:, :SEQ].reshape(images * SEQ, D)

    return (
        unpadded(output),
        unpadded(dx),
        norms[0],
        norms[1],
        grads[:, :QKV],
        grads[:, QKV : QKV + D],
        norms[2],
        norms[3],
        router_grad,
        expert_in_grad,
        expert_out_grad,
    )


def solution(mesh):
    dp, groups = mesh.shape["dp"], mesh.shape["expert"]
    parts = min(EXPERTS // groups, dp // 2)
    mesh = Mesh(mesh.devices.reshape(dp // parts, parts, groups), ("replica", "part", "expert"))
    rows = P(("replica", "part", "expert"), None)
    vector, matrix = P(ALL), P(ALL, None)
    experts = P("expert", ALL, None)
    return jax.shard_map(
        body,
        mesh=mesh,
        in_specs=(
            rows, rows, vector, vector, matrix, matrix, vector, vector, matrix, experts, experts, rows,
        ),
        out_specs=(
            rows, rows, vector, vector, matrix, matrix, vector, vector, matrix, experts, experts,
        ),
        check_vma=False,
    )
```

time: 672 us -> 599 us (0.89)
  Pallas kernels: 585 us -> 552 us
  starting transfers between devices: 29.5 us -> 0.23 us
    pallas_call x7 -> x5, Pallas kernels: 487 us -> 378 us  [the longest x2 187 us: dispatch(): pl.pallas_call(partial(open_kernel if opening else dispatch_kernel, sizes...]
    pallas_call x1, Pallas kernels: 98.7 us -> 174 us  [close(): pl.pallas_call(partial(close_kernel, sizes), in_specs=[inner] * 4 + [oute...]
    all_to_all x4 -> x0, starting transfers between devices: 29.3 us -> none  [the longest x2 14.9 us: collect(): pieces = lax.all_to_all(grad, ALL, split_axis=0, concat_axis=0, tiled=True)]
    reduce_sum x2 -> x0, other arithmetic: 11 us -> none  [collect(): return jnp.sum(pieces.astype(full), axis=0)]
    convert_element_type x2 -> x4, other arithmetic: 4.97 us -> 14.6 us  [the longest x1 4.18 us: body(): expert_out_grad = second_grad.reshape(w_expert_out.shape).astype(full)]
  transfers between devices with their start and end apart: 5 -> 1, of which waited for: 0 -> 0; matrix products, arithmetic and copies ran while one was open for 6% -> 3% of each run, Pallas kernels for 89% -> 0%
where the time goes in v5:
time: 599 us; the launch traced here: 590 us
  Pallas kernels  552 us (92%)
  other arithmetic  18.9 us (3%)
  local copies, waits for them, and re-layouts  17.7 us (3%)
    pallas_call x2, Pallas kernels, dispatch(): pl.pallas_call(partial(open_kernel if opening else dispatch_kernel, sizes...  187 us
    pallas_call x1, Pallas kernels, close(): pl.pallas_call(partial(close_kernel, sizes), in_specs=[inner] * 4 + [oute...  174 us
    pallas_call x1, Pallas kernels, expert_rest(): pl.pallas_call(partial(rest_kernel, sizes, own, steps), grid=(3 * own * s...  100 us
    pallas_call x1, Pallas kernels, expert_first(): pl.pallas_call(partial(first_kernel, sizes), grid=(own, hidden // tile),...  50.8 us
    pallas_call x1, Pallas kernels, attend(): pl.pallas_call(partial(attend_kernel, sizes), grid=(images,), in_specs=[i...  39.4 us
  transfers between devices with their start and end apart: 1, of which 0 were waited for; matrix products, arithmetic and copies ran while one was open for 3% of the time, Pallas kernels for 0%

profile of v5, /device:TPU:13, one launch (start us, length us, event | category | flops | bytes accessed | tf_op | source)
XLA Modules:
  0.0 590.1 jit_solution(5152818623386684306)
XLA Ops:
  0.6 0.0 copy-start.2
  0.7 0.2 collective-permute-start
  0.9 0.7 convert_bitcast_fusion.3
  1.6 0.7 convert_bitcast_fusion.2
  2.3 0.7 convert_bitcast_fusion.1
  2.9 0.6 fusion.4.order_ref
  3.6 0.6 compare_convert_fusion.sel_ref
  4.2 0.7 convert_bitcast_fusion
  4.9 0.0 copy-start.5
  4.9 0.0 copy-start.6
  4.9 0.0 copy-start.7
  4.9 0.0 copy-start.3
  4.9 3.9 convert_element_type.33.master_ref
  8.8 0.0 copy-done.2
  8.8 0.3 reshape.129
  9.1 0.0 copy-done.5
  9.1 0.0 copy-done.6
  9.1 0.0 copy-done.7
  9.2 0.1 copy.77
  9.2 0.1 copy.79
  9.3 0.1 copy.80
  9.4 0.1 copy.81
  9.5 0.1 copy.82
  9.6 0.1 copy.83
  9.7 0.0 copy-done.3
  9.7 0.3 reshape.134
  10.0 1.1 pad.22.dy_ref
  11.1 1.2 pad.23.x_ref
  12.3 3.8 convert_element_type.35.master_ref
  16.1 0.8 concatenate.4.shard_ref
  16.9 0.0 collective-permute-done
  16.9 0.0 copy-done.8
  16.9 0.1 reshape.127
  17.0 0.1 eq.53
  17.1 0.1 compare_reduce_fusion
  17.2 0.5 bitcast_select_fusion.1
  17.7 0.5 copy.75
  18.2 0.1 copy.76
  18.3 0.7 copy.84.keys_ref
  19.0 99.9 %open.1 = (bf16[8,2,2,128,512]{4,3,2,1,0:T(8,128)(2,1)}, bf16[16,32,2176]{2,1,0:T(8,128)(2,1)}, bf16[16,2,32,2048]{3,2,1,0:T(8,128)(2,1)}) custom-call(f32[2,8,2,1040]{3,2,1,0:T(2,128)} %copy.84.keys_ref, bf16[1040,512]{1,0:T(8,128)(2,1)} %bitcast.50, bf16[32,2176]{1,0:T(8,128)(2,1)} %concatenate.4.shard_ref, ...), custom_call_target="tpu_custom_call" | custom-call | flops 60000002048 | bytes 5000000 | tf_op jit(solution)/shard_map/open/pallas_call | solution.py:417
  119.0 1.6 slice.44.wr_ref
  120.5 0.3 copy.74
  120.8 39.4 %attend.1 = (bf16[5,208,1536]{2,1,0:T(8,128)(2,1)}, bf16[5,208,512]{2,1,0:T(8,128)(2,1)}, f32[5,208,512]{2,1,0:T(8,128)}, bf16[5,208,640]{2,1,0:T(8,128)(2,1)}, ...) custom-call(bf16[5,208,512]{2,1,0:T(8,128)(2,1)} %pad.23.x_ref, ...), custom_call_target="tpu_custom_call", output_to_operand_aliasing={{5}: (4, {})} | custom-call | flops 8000000000 | bytes 12000000 | tf_op jit(solution)/shard_map/attend/pallas_call | solution.py:148
  160.2 87.3 %dispatch.1 = (bf16[8,2,2,128,512]{4,3,2,1,0:T(8,128)(2,1)}, bf16[1040,640]{1,0:T(8,128)(2,1)}, bf16[16,2,128,512]{3,2,1,0:T(8,128)(2,1)}) custom-call(f32[2,8,2,1040]{3,2,1,0:T(2,128)} %copy.84.keys_ref, bf16[1040,640]{1,0:T(8,128)(2,1)} %bitcast.69, bf16[16,128,512]{2,1,0:T(8,128)(2,1)} %convert_element_type.35.master_ref), custom_call_target="tpu_custom_call" | custom-call | flops 60000002048 | bytes 5000000 | tf_op jit(solution)/shard_map/dispatch/pallas_call | solution.py:417
  247.5 0.2 fusion.3
  247.7 0.9 pad.21.keys_ref
  248.6 50.8 %expert_first.1 = (bf16[2,2048,2048]{2,1,0:T(8,128)(2,1)}, bf16[2,2048,2048]{2,1,0:T(8,128)(2,1)}, bf16[16,2,128,512]{3,2,1,0:T(8,128)(2,1)}, bf16[16,2,128,512]{3,2,1,0:T(8,128)(2,1)}) custom-call(bf16[16,2,128,512]{3,2,1,0:T(8,128)(2,1)} %bitcast.67, bf16[16,2,128,512]{3,2,1,0:T(8,128)(2,1)} %bitcast.64, ...), custom_call_target="tpu_custom_call", output_to_operand_aliasing={{3}: (6, {})} | custom-call | flops 17179869184 | bytes 50000000 | tf_op jit(solution)/shard_map/expert_first/pallas_call | solution.py:811
  299.4 100.1 %expert_rest.1 = (bf16[16,2,144,512]{3,2,1,0:T(8,128)(2,1)}, bf16[16,2,32,2048]{3,2,1,0:T(8,128)(2,1)}, bf16[16,2,128,512]{3,2,1,0:T(8,128)(2,1)}, bf16[1,8,2,128,512]{4,3,2,1,0:T(8,128)(2,1)}) custom-call(bf16[16,2,128,512]{3,2,1,0:T(8,128)(2,1)} %bitcast.65, bf16[16,2,128,512]{3,2,1,0:T(8,128)(2,1)} %bitcast.68, ...), custom_call_target="tpu_custom_call" | custom-call | flops 34359738368 | bytes 60000000 | tf_op jit(solution)/shard_map/expert_rest/pallas_call | solution.py:995
  399.5 174.2 %close.1 = (f32[5,208,512]{2,1,0:T(8,128)}, bf16[1040,512]{1,0:T(8,128)(2,1)}, f32[32,2176]{1,0:T(8,128)}, bf16[8,2,32,2048]{3,2,1,0:T(8,128)(2,1)}, bf16[8,2,128,512]{3,2,1,0:T(8,128)(2,1)}) custom-call(bf16[2,1040,128]{2,1,0:T(8,128)(2,1)} %pad.21.keys_ref, bf16[8,2,2,144,512]{4,3,2,1,0:T(8,128)(2,1)} %bitcast.63, bf16[512,2176]{1,0:T(8,128)(2,1)} %bitcast.61, ...), custom_call_target="tpu_custom_call" | custom-call | flops 60000002048 | bytes 30000000 | tf_op jit(solution)/shard_map/close/pallas_call | solution.py:724
  573.7 1.6 slice.39
  575.4 0.7 slice.43
  576.1 1.5 slice.40
  577.5 1.7 slice_reduce_fusion
  579.2 4.2 bitcast_convert_fusion
  583.4 0.0 copy-done
  583.4 2.7 bitcast_convert_fusion.1
  586.1 0.0 copy-done.1
  586.1 0.2 slice.36
  586.2 1.5 reshape.142
  587.8 0.0 copy-done.4
  587.8 0.1 slice.45
  587.9 1.2 reshape.141
  589.1 0.1 copy.86
  589.2 0.7 copy.88
  (16 shorter events, 0.1 us)
Async XLA Ops:
  0.6 8.2 %copy-start.2 = (bf16[985,512]{1,0:T(8,128)(2,1)S(1)}, bf16[985,512]{1,0:T(8,128)(2,1)}, u32[]{:S(2)}) copy-start(bf16[985,512]{1,0:T(8,128)(2,1)} %param.23) | copy-start | bytes 3025924
  0.7 16.2 %collective-permute-start = (s32[985,2]{0,1:T(2,128)}, s32[985,2]{0,1:T(2,128)S(1)}, u32[]{:S(2)}, u32[]{:S(2)}) collective-permute-start(s32[985,2]{0,1:T(2,128)} %param.13), channel_id=1, source_target_pairs={{0,8},{2,10},{4,12},{6,14},{8,0},{10,2},{12,4},{14,6},{1,9},{3,11}... | collective-permute-start | bytes 23648 | tf_op jit(solution)/shard_map/ppermute | solution.py:1089
  4.9 4.2 copy-start.5
  4.9 4.3 copy-start.6
  4.9 4.3 copy-start.7
  4.9 4.9 copy-start.3
  12.3 4.6 copy-start.8
  577.5 5.8 copy-start
  583.4 2.7 copy-start.1
  586.1 1.7 copy-start.4

commit v6 on v5

--- a/solution.py
+++ b/solution.py
@@ -17,7 +17,6 @@
 HEAD = D // HEADS
 LANES = 128
 QKV = 3 * D
-SENT = D + LANES
 PACKED = QKV + D + LANES
 epsilon = 1e-06
 low = jnp.bfloat16
@@ -57,8 +56,12 @@
     )
 
 
+def columns_of(weights_ref, start_at, end):
+    return weights_ref[:, :, start_at:end].reshape(D, end - start_at)
+
+
 def norm_vectors(weights_ref):
-    rows = weights_ref[:, QKV + D :].astype(full).T
+    rows = columns_of(weights_ref, QKV + D, PACKED).astype(full).T
     return [rows[EXPERTS + i : EXPERTS + i + 1] for i in range(4)]
 
 
@@ -75,61 +78,39 @@
     return grown / jnp.sum(grown, axis=-1, keepdims=True)
 
 
-def attend_kernel(
-    sizes, x_ref, w_ref, order_ref, master_ref, _, qkv_ref, ctx_ref, r_ref, sent_ref, probs_ref, first_ref, flow
-):
-    def moved():
-        return outward(sizes, wide_part, master_ref, first_ref, flow, GROUPS - 1, 0)
-
-    @pl.when(pl.program_id(0) == 0)
-    def _():
-        greet(all_owners(*sizes[:2]))
-        start(moved())
-
-    gain_one, bias_one, gain_two, bias_two = norm_vectors(w_ref)
-    x = x_ref[0].astype(full)
+def attend(i, weights, order, x_ref, qkv_ref, ctx_ref, r_ref, h_ref, probs_ref):
+    gain_one, bias_one, gain_two, bias_two = norm_vectors(weights)
+    x = x_ref[i].astype(full)
     normed, _ = normed_rows(x)
     attn_in = (normed * gain_one + bias_one).astype(low)
-    qkv_ref[0] = dot(attn_in, w_ref[:, :QKV]).astype(low)
+    qkv_ref[i] = dot(attn_in, columns_of(weights, 0, QKV)).astype(low)
     for pair in range(HEADS // 2):
         at = pair * LANES
-        query = halves(qkv_ref[0, :, at : at + LANES])
-        key = qkv_ref[0, :, D + at : D + at + LANES]
-        value = halves(qkv_ref[0, :, 2 * D + at : 2 * D + at + LANES])
+        query = halves(qkv_ref[i, :, at : at + LANES])
+        key = qkv_ref[i, :, D + at : D + at + LANES]
+        value = halves(qkv_ref[i, :, 2 * D + at : 2 * D + at + LANES])
         total = None
-        for i in range(2):
-            part = dot(head_probs(query[i], key).astype(low), value[i])
+        for e in range(2):
+            part = dot(head_probs(query[e], key).astype(low), value[e])
             total = part if total is None else total + part
-        ctx_ref[0, :, at : at + LANES] = total.astype(low)
-    r = x + dot(ctx_ref[0], w_ref[:, QKV : QKV + D])
-    r_ref[0] = r
+        ctx_ref[i, :, at : at + LANES] = total.astype(low)
+    r = x + dot(ctx_ref[i], columns_of(weights, QKV, QKV + D))
+    r_ref[i] = r
     normed, _ = normed_rows(r)
     h = (normed * gain_two + bias_two).astype(low)
-    sent_ref[0, :, :D] = h
-    logits = dot(h, dot(w_ref[:, QKV + D :], order_ref[...]).astype(low))
+    h_ref[i] = h
+    probs_ref[i] = routed(h, weights, order)
+
+
+def routed(h, weights, order):
+    logits = dot(h, dot(columns_of(weights, QKV + D, PACKED), order).astype(low))
     logits = jnp.where(lanes_of(logits.shape) < EXPERTS, logits, -1e30)
     grown = jnp.exp(logits - jnp.max(logits, axis=-1, keepdims=True))
-    probs = grown / jnp.sum(grown, axis=-1, keepdims=True)
-    probs_ref[0] = probs
-    sent_ref[0, :, D:] = pltpu.roll(probs, LANES - EXPERTS // 2, 1).astype(low)
-
-    @pl.when(pl.program_id(0) == pl.num_programs(0) - 1)
-    def _():
-        wait(moved())
-
-
-def image_spec(width):
-    return pl.BlockSpec((1, ROWS, width), lambda i: (i, 0, 0))
+    return grown / jnp.sum(grown, axis=-1, keepdims=True)
 
 
 def whole_spec(shape):
     return pl.BlockSpec(shape, lambda *_: (0,) * len(shape))
-
-
-def params(n):
-    return pltpu.CompilerParams(
-        dimension_semantics=("arbitrary",) * n, vmem_limit_bytes=BIG
-    )
 
 
 def remote_params(n, number):
@@ -139,27 +120,6 @@
         collective_id=number,
         has_side_effects=True,
     )
-
-
-def attend(x, weights, order, master, first, sizes, number):
-    images = x.shape[0]
-    shapes = ((QKV, low), (D, low), (D, full), (SENT, low), (LANES, full))
-    outer = pl.BlockSpec(memory_space=pl.ANY)
-    return pl.pallas_call(
-        partial(attend_kernel, sizes),
-        grid=(images,),
-        in_specs=[image_spec(D), whole_spec(weights.shape), whole_spec(order.shape), outer, outer],
-        out_specs=[image_spec(width) for width, _ in shapes] + [outer],
-        out_shape=[jax.ShapeDtypeStruct((images, ROWS, w), t) for w, t in shapes]
-        + [jax.ShapeDtypeStruct(first.shape, low)],
-        input_output_aliases={4: 5},
-        scratch_shapes=[flow_semaphores(sizes, 1)],
-        compiler_params=remote_params(1, number),
-        cost_estimate=pl.CostEstimate(
-            flops=8 * 10**9, bytes_accessed=12 * 10**6, transcendentals=2 * 10**6
-        ),
-        name="attend",
-    )(x, weights, order, master, first)
 
 
 def device(offset):
@@ -197,8 +157,14 @@
     return (lax.axis_index("replica") ^ offset[0]) * parts + (lax.axis_index("part") ^ offset[1])
 
 
+def in_line(replicas, parts):
+    return [o for o in owners_like(replicas, parts) if o[1] % 4 == 0]
+
+
 CORE = (0, 1, 0)
+ROW = (0, 2, 0)
 GROUPS = 4
+EARLY = 5
 
 
 def all_owners(replicas, parts):
@@ -218,6 +184,11 @@
 def tall_part(ref, at, g):
     depth = ref.shape[-2] // GROUPS
     return ref.at[at, ..., pl.ds(g * depth, depth), :]
+
+
+def small_part(ref, at, g):
+    depth, width = ref.shape[-2] // GROUPS, ref.shape[-1] // 2
+    return ref.at[at, ..., pl.ds(g // 2 * depth, depth), pl.ds(g % 2 * width, width)]
 
 
 def outward(sizes, part_of, source, target, semaphores, g, slot):
@@ -274,8 +245,13 @@
     return dw_ref.at[pl.ds(lax.axis_index("replica") * sizes[1], sizes[1])]
 
 
-def pieces_of(sizes, dw):
-    return jax.ShapeDtypeStruct((sizes[0] - 1, sizes[1], *dw.shape[1:]), low)
+def add(sizes, mine, others, rows, columns):
+    @pl.loop(0, sizes[1])
+    def _(p):
+        total = mine[p, :, rows, columns].astype(full)
+        for r in range(sizes[0] - 1):
+            total = total + others[r, p, :, rows, columns].astype(full)
+        mine[p, :, rows, columns] = total.astype(low)
 
 
 def start(copies):
@@ -296,12 +272,12 @@
     _, count, own, tokens = keys_ref.shape
     slots = lax.broadcasted_iota(jnp.int32, (CAP, tokens), 0).astype(full)
 
-    def build(s, source_ref):
+    def build(s, source):
         copies = []
         for j in [*range(1, count), 0]:
             picks = [(keys_ref[s, j, i : i + 1] == slots).astype(low) for i in range(own)]
             picks = jnp.concatenate(picks, axis=0) if own > 1 else picks[0]
-            rows = dot(picks, source_ref[:, :D]).astype(low)
+            rows = dot(picks, source).astype(low)
             blocks[j, s] = rows.reshape(own, CAP, D)
             if j:
                 copy = remote(
@@ -318,116 +294,205 @@
 
 
 def open_kernel(
-    sizes, keys_ref, rows_ref, shard_ref, master_ref, out_ref, weights_ref, first_ref,
-    blocks, other, hop, sends, receives, local, flow, early, late, here,
+    sizes, keys_ref, cotangent_ref, tokens_ref, order_ref, shard_ref, raw_one_ref, raw_two_ref,
+    x_out, dy_kept, dy_out, h_out, weights_out, first_ref, second_ref, qkv_out, ctx_out, r_out, h_kept, probs_out, theirs_out,
+    master_out,
+    x_ref, dy_ref, dy_blocks, h_blocks, weights, other_dy, other_h, qkv, ctx, r, h, probs, theirs,
+    raw_one, raw_two, master_one, master_two,
+    hop, hops, dy_sends, dy_receives, dy_local, h_sends, h_receives, h_local, early, middle, late, here, keeps,
+    raws, flow,
 ):
     replicas, parts, groups = sizes
     count = keys_ref.shape[1]
+    images = x_ref.shape[0]
     mirror = (0, parts // 2, 0)
     owners = owners_like(replicas, parts)
+    reading = [
+        pltpu.make_async_copy(raw_one_ref, raw_one, raws.at[0]),
+        pltpu.make_async_copy(raw_two_ref, raw_two, raws.at[1]),
+    ]
+    start(reading)
+    for padded, rows_ref in ((dy_ref, cotangent_ref), (x_ref, tokens_ref)):
+        padded[...] = jnp.zeros_like(padded)
+        for i in range(images):
+            padded[i, :SEQ] = rows_ref[i * SEQ : (i + 1) * SEQ].astype(full).astype(low)
     greet(
         sorted({near(groups, j) for j in range(1, count)} | {mirror, *all_owners(replicas, parts)})
     )
-    hops = remote(rows_ref, other, hop.at[0], hop.at[1], mirror)
-    hops.start()
-    mine = weights_ref.at[owner(parts)]
-    gathers = [
-        remote(shard_ref, mine, early.at[0, i], early.at[1, i], o) for i, o in enumerate(owners)
-    ]
-    passes = [remote(shard_ref, mine, late.at[0, 0], late.at[1, 0], CORE)]
-    for i, o in enumerate(owners):
-        slot = weights_ref.at[owner(parts, o)]
-        passes.append(remote(slot, slot, late.at[0, i + 1], late.at[1, i + 1], CORE))
-    start(gathers)
-    passes[0].start()
-    kept = pltpu.make_async_copy(shard_ref, mine, here)
+    swap_dy = remote(dy_ref, other_dy, hop.at[0], hop.at[1], mirror)
+    swap_dy.start()
+    side = lax.axis_index("expert") % 2
+    cut_at = (PACKED // LANES + 1) // 2 * LANES
+
+    def half(ref, which):
+        return ref.at[:, : PACKED - cut_at] if which == 0 else ref.at[:, PACKED - cut_at :]
+
+    def halves_of(o, which):
+        return half(weights.at[owner(parts, o)], which)
+
+    kept = pltpu.make_async_copy(shard_ref, weights.at[owner(parts)], here)
     kept.start()
-    parts_of = [
-        outward(sizes, wide_part, master_ref, first_ref, flow, g, g) for g in range(GROUPS - 1)
-    ]
-    start(parts_of[0])
-    build = swap_slots(groups, keys_ref, blocks, out_ref, sends, receives, local)
-    copies = build(0, rows_ref)
-    start(parts_of[1])
-    for i, copy in enumerate(gathers):
-        copy.wait_recv()
-        passes[i + 1].start()
-    hops.wait_recv()
-    copies += build(1, other)
-    start(parts_of[2])
-    hops.wait_send()
+    to_core = remote(shard_ref, weights.at[owner(parts)], late.at[0, 0, 0], late.at[1, 0, 0], CORE)
+    to_core.start()
+
+    def gathers(which):
+        return [
+            remote(
+                half(shard_ref, which), halves_of((0, 0, 0), which), early.at[0, i], early.at[1, i], o
+            )
+            for i, o in enumerate(owners)
+        ]
+
+    def beside(which):
+        return [
+            remote(
+                halves_of(o, which), halves_of(o, which), middle.at[0, i], middle.at[1, i], (0, 0, 1)
+            )
+            for i, o in enumerate(owners)
+        ]
+
+    def onward(which, slot):
+        return [
+            remote(
+                halves_of(o, which), halves_of(o, which), late.at[0, slot, i + 1], late.at[1, slot, i + 1], CORE
+            )
+            for i, o in enumerate(owners)
+        ]
+
+    for which in range(2):
+        @pl.when(side == which)
+        def _():
+            start(gathers(which))
+
+    one = [outward(sizes, wide_part, master_one, first_ref, flow, g, g) for g in range(GROUPS)]
+    two = [
+        outward(sizes, small_part, master_two, second_ref, flow, g, GROUPS + g)
+        for g in range(EARLY)
+    ]
+    reading[0].wait()
+
+    @pl.loop(0, raw_one.shape[0])
+    def _(e):
+        master_one[e] = raw_one[e].astype(low)
+
+    start(one[0])
+    build_dy = swap_slots(groups, keys_ref, dy_blocks, dy_out, dy_sends, dy_receives, dy_local)
+    build_h = swap_slots(groups, keys_ref, h_blocks, h_out, h_sends, h_receives, h_local)
+    copies = build_dy(0, dy_ref[...].reshape(images * ROWS, D))
+    start(one[1])
+    reading[1].wait()
+
+    @pl.loop(0, raw_two.shape[0])
+    def _(e):
+        master_two[e] = raw_two[e].astype(low)
+
+    for which in range(2):
+        @pl.when(side == which)
+        def _():
+            for a, b, c in zip(gathers(which), beside(which), onward(which, 0)):
+                a.wait_recv()
+                b.start()
+                c.start()
+
+    swap_dy.wait()
+    copies += build_dy(1, other_dy[...].reshape(images * ROWS, D))
+    for which in range(2):
+        @pl.when(side == which)
+        def _():
+            for b, c in zip(beside(1 - which), onward(1 - which, 1)):
+                b.wait_recv()
+                c.start()
+            for a, b, c, d in zip(gathers(which), beside(which), onward(which, 0), onward(1 - which, 1)):
+                a.wait_send()
+                b.wait_send()
+                c.wait()
+                d.wait()
+
+    to_core.wait()
+    kept.wait()
+
+    def hop_of(i):
+        return remote(h.at[i], other_h.at[i], hops.at[0, i], hops.at[1, i], mirror)
+
+    @pl.loop(0, images)
+    def _(i):
+        attend(i, weights, order_ref[...], x_ref, qkv, ctx, r, h, probs)
+        hop_of(i).start()
+
+    start(one[2])
+    start(one[3])
+    keeping = [
+        pltpu.make_async_copy(source, target, keeps.at[i])
+        for i, (source, target) in enumerate(
+            [
+                (weights, weights_out), (qkv, qkv_out), (ctx, ctx_out), (r, r_out), (h, h_kept),
+                (probs, probs_out), (master_two, master_out), (x_ref, x_out), (dy_ref, dy_kept),
+            ]
+        )
+    ]
+    start(keeping)
+    copies += build_h(0, h[...].reshape(images * ROWS, D))
+    start(two[0])
+    start(two[1])
+
+    @pl.loop(0, images)
+    def _(i):
+        hop_of(i).wait()
+        theirs[i] = routed(other_h[i], weights, order_ref[...]).astype(low)
+
+    copies += build_h(1, other_h[...].reshape(images * ROWS, D))
+    for group in two[2:]:
+        start(group)
+    last = pltpu.make_async_copy(theirs, theirs_out, keeps.at[9])
+    last.start()
     wait(copies)
-    for copy in gathers:
-        copy.wait_send()
-    wait(passes)
-    kept.wait()
-    for group in parts_of:
+    wait(keeping)
+    last.wait()
+    for group in one + two:
         wait(group)
 
 
-def dispatch_kernel(
-    sizes, keys_ref, rows_ref, master_ref, out_ref, other_ref, second_ref,
-    blocks, other, hop, sends, receives, local, flow,
-):
+def forward(keys, cotangent, tokens, order, shard, raw_one, raw_two, sizes, number):
     replicas, parts, groups = sizes
-    count = keys_ref.shape[1]
-    mirror = (0, parts // 2, 0)
-    greet(
-        sorted({near(groups, j) for j in range(1, count)} | {mirror, *all_owners(replicas, parts)})
-    )
-    hops = remote(rows_ref, other, hop.at[0], hop.at[1], mirror)
-    hops.start()
-    build = swap_slots(groups, keys_ref, blocks, out_ref, sends, receives, local)
-    copies = build(0, rows_ref)
-    more = [outward(sizes, tall_part, master_ref, second_ref, flow, g, g) for g in range(3)]
-    start(more[0])
-    start(more[1])
-    hops.wait()
-    copies += build(1, other)
-    start(more[2])
-    keep = pltpu.make_async_copy(other, other_ref, local.at[2])
-    keep.start()
-    keep.wait()
-    wait(copies)
-    for group in more:
-        wait(group)
-
-
-def dispatch(keys, rows, sizes, number, master, shard=None):
-    replicas, parts, groups = sizes
-    _, count, own, tokens = keys.shape
-    shape = (count, 2, own, CAP, D)
+    _, count, own, _ = keys.shape
+    images = tokens.shape[0] // SEQ
     owners = replicas * parts
-    opening = number == 0
+    slots = (count, 2, own, CAP, D)
+    rows = lambda width: (images, ROWS, width)
+    shapes = [
+        (rows(D), low), (rows(D), low), (slots, low), (slots, low), ((owners, *shard.shape), low),
+        ((owners, own, *raw_one.shape[1:]), low), ((owners, own, *raw_two.shape[1:]), low),
+        (rows(QKV), low), (rows(D), low), (rows(D), full), (rows(D), low), (rows(LANES), full), (rows(LANES), low),
+        (raw_two.shape, low),
+    ]
+    buffers = [
+        (rows(D), low), (rows(D), low), (slots, low), (slots, low), ((owners, *shard.shape), low), (rows(D), low),
+        (rows(D), low),
+        (rows(QKV), low), (rows(D), low), (rows(D), full), (rows(D), low), (rows(LANES), full), (rows(LANES), low),
+        (raw_one.shape, full), (raw_two.shape, full), (raw_one.shape, low), (raw_two.shape, low),
+    ]
+    semaphores = [
+        (2,), (2, images), (count, 2), (count, 2), (2,), (count, 2), (count, 2), (2,),
+        (2, owners // 2 - 1), (2, owners // 2 - 1), (2, 2, owners // 2), (), (10,), (2,),
+        (2, GROUPS + EARLY, owners),
+    ]
     inner = pl.BlockSpec(memory_space=pltpu.VMEM)
     outer = pl.BlockSpec(memory_space=pl.ANY)
-    whole = jax.ShapeDtypeStruct((owners, own, *master.shape[1:]), low)
-    outs = [jax.ShapeDtypeStruct(shape, low)]
-    semaphores = [(2,), (count, 2), (count, 2), (3,)]
-    scratch = [pltpu.VMEM(shape, low), pltpu.VMEM(rows.shape, low)]
-    scratch += [pltpu.SemaphoreType.DMA(n) for n in semaphores] + [flow_semaphores(sizes, 3)]
-    if opening:
-        arrays = (keys, rows, shard, master)
-        outs += [jax.ShapeDtypeStruct((owners, *shard.shape), low), whole]
-        more = [(2, owners // 2 - 1), (2, owners // 2), ()]
-        scratch += [pltpu.SemaphoreType.DMA(n) for n in more]
-    else:
-        arrays = (keys, rows, master)
-        outs += [jax.ShapeDtypeStruct(rows.shape, low), whole]
     return pl.pallas_call(
-        partial(open_kernel if opening else dispatch_kernel, sizes),
-        in_specs=[inner, inner] + [outer] * (len(arrays) - 2),
-        out_specs=[outer] * len(outs),
-        out_shape=outs,
-        scratch_shapes=scratch,
+        partial(open_kernel, sizes),
+        in_specs=[inner] * 4 + [outer] * 3,
+        out_specs=[outer] * len(shapes),
+        out_shape=[jax.ShapeDtypeStruct(*shape) for shape in shapes],
+        scratch_shapes=[pltpu.VMEM(*b) for b in buffers]
+        + [pltpu.SemaphoreType.DMA(n) for n in semaphores],
         compiler_params=pltpu.CompilerParams(
             vmem_limit_bytes=BIG, collective_id=number, has_side_effects=True
         ),
         cost_estimate=pl.CostEstimate(
-            flops=60 * 10**9, bytes_accessed=5 * 10**6, transcendentals=0
+            flops=60 * 10**9, bytes_accessed=30 * 10**6, transcendentals=2 * 10**6
         ),
-        name="open" if opening else "dispatch",
-    )(*arrays)
+        name="forward",
+    )(keys, cotangent, tokens, order, shard, raw_one, raw_two)
 
 
 def chooser(own, j):
@@ -446,7 +511,7 @@
     probs, dprobs = probs_ref[i], dprobs_ref[rows]
     dlogits = (probs * (dprobs - jnp.sum(probs * dprobs, axis=-1, keepdims=True))).astype(low)
     router_acc[...] += dot_lt(h_ref[i], dlogits)
-    router = dot(w_ref[:, QKV + D :], order_ref[...]).astype(low)
+    router = dot(columns_of(w_ref, QKV + D, PACKED), order_ref[...]).astype(low)
     dh = dh_ref[rows] + dot_rt(dlogits, router)
     normed, factor = normed_rows(r_ref[i])
     norm_acc[2:3] += jnp.sum(dh * normed, axis=0, keepdims=True)
@@ -454,7 +519,7 @@
     dr = dy_ref[i].astype(full) + norm_back(normed, factor, gain_two, dh)
     dattended = dr.astype(low)
     proj_acc[...] += dot_lt(ctx_ref[i], dattended)
-    dctx = dot_rt(dattended, w_ref[:, QKV : QKV + D]).astype(low)
+    dctx = dot_rt(dattended, columns_of(w_ref, QKV, QKV + D)).astype(low)
     for pair in range(HEADS // 2):
         at = pair * LANES
         query = halves(qkv_ref[i, :, at : at + LANES])
@@ -475,21 +540,21 @@
     normed, factor = normed_rows(x_ref[i].astype(full))
     attn_in = (normed * gain_one + bias_one).astype(low)
     qkv_acc[...] += dot_lt(attn_in, dqkv[...])
-    da = dot_rt(dqkv[...], w_ref[:, :QKV])
+    da = dot_rt(dqkv[...], columns_of(w_ref, 0, QKV))
     norm_acc[0:1] += jnp.sum(da * normed, axis=0, keepdims=True)
     norm_acc[1:2] += jnp.sum(da, axis=0, keepdims=True)
     dx_ref[i] = dr + norm_back(normed, factor, gain_one, da)
 
 
 def close_kernel(
-    sizes, keys_ref, back_ref, w_ref, order_ref, x_ref, qkv_ref, ctx_ref, r_ref, sent_ref, probs_ref, dy_ref,
-    theirs_ref, y_ref, dw_one_ref, dw_two_ref, got_two_ref,
-    dx_ref, out_ref, total_ref, one_ref, two_ref,
-    xs, qkvs, ctxs, rs, hs, ps, dys, their_probs, ys, dh, dprobs, sent, got, sent_two, got_two,
-    mine_one, others_one, mine_two, others_two,
-    dqkv, qkv_acc, proj_acc, router_acc, norm_acc, grads, kept, first, second, third,
-    loads, y_sends, y_receives, hops, hops_two, flow, home_one, home_two,
-    core_sems, owner_sems, expert_sems,
+    sizes, keys_ref, back_ref, w_ref, order_ref, x_ref, qkv_ref, ctx_ref, r_ref, h_ref, probs_ref, dy_ref,
+    theirs_ref, y_ref, dw_one_ref,
+    dx_ref, out_ref, total_ref, one_ref,
+    xs, qkvs, ctxs, rs, hs, ps, dys, their_probs, ys, dh, dprobs, sent, got, sent_gates, got_gates, sent_two, got_two,
+    mine_one, others_one,
+    dqkv, qkv_acc, proj_acc, router_acc, norm_acc, grads, kept, first, second, along, third,
+    loads, y_sends, y_receives, hops, gate_hops, hops_two, flow, home_one,
+    core_sems, row_sems, owner_sems, expert_sems,
 ):
     replicas, parts, groups = sizes
     count, _, own, _, _ = y_ref.shape
@@ -503,9 +568,8 @@
     greet(sorted(peers | partners(sizes)))
 
     pairs_of = [
-        (r_ref, rs), (theirs_ref.at[:, D:], their_probs), (x_ref, xs), (qkv_ref, qkvs), (ctx_ref, ctxs),
-        (sent_ref.at[:, :, :D], hs), (probs_ref, ps), (dy_ref, dys),
-        (mine_of(sizes, dw_two_ref), mine_two), (got_two_ref, others_two),
+        (r_ref, rs), (theirs_ref, their_probs), (x_ref, xs), (qkv_ref, qkvs), (ctx_ref, ctxs),
+        (h_ref, hs), (probs_ref, ps), (dy_ref, dys),
         (mine_of(sizes, dw_one_ref), mine_one), (y_ref.at[0], ys.at[0]),
     ]
     loading = [
@@ -524,8 +588,8 @@
     ]
     start(swaps[1])
     start(swaps[0])
-    start(eighths[0])
-    start(eighths[1])
+    for g in range(GROUPS):
+        start(eighths[g])
     start(loading)
 
     def rows_of(i):
@@ -533,7 +597,13 @@
 
     def hop(i):
         rows = rows_of(i)
-        return remote(sent.at[rows], got.at[rows], hops.at[0, i], hops.at[1, i], mirror)
+        return [
+            remote(sent.at[rows], got.at[rows], hops.at[0, i], hops.at[1, i], mirror),
+            remote(sent_gates.at[i], got_gates.at[i], gate_hops.at[0, i], gate_hops.at[1, i], mirror),
+        ]
+
+    near_lanes = lanes_of((2 * half, LANES))
+    near_rows = lax.broadcasted_iota(jnp.int32, (2 * half, LANES), 0)
 
     def hop_two(i):
         rows = rows_of(i)
@@ -570,13 +640,15 @@
     def _(i):
         rows = rows_of(i)
         total, change = gathered(1, rows)
-        sent[rows, :D] = total.astype(low)
+        sent[rows] = total.astype(low)
         high = change.astype(low)
         rest = pltpu.roll(change - high.astype(full), half, 1)
-        sent[rows, D:] = (high.astype(full) + rest).astype(low)
-        hop(i).start()
-
-    start(eighths[2])
+        both = (high.astype(full) + rest).astype(low)
+        sent_gates[i] = dot_rt((near_lanes == near_rows).astype(low), both).astype(low)
+        start(hop(i))
+
+    for g in range(GROUPS, 2 * GROUPS):
+        start(eighths[g])
 
     @pl.loop(0, images)
     def _(i):
@@ -589,35 +661,30 @@
     @pl.loop(0, images)
     def _(i):
         rows = rows_of(i)
-        sent_two[rows] = weighted(1, rows, their_probs[rows]).astype(low)
+        sent_two[rows] = weighted(1, rows, their_probs[i]).astype(low)
         hop_two(i).start()
-
-    start(eighths[3])
 
     @pl.loop(0, images)
     def _(i):
         rows = rows_of(i)
-        hop(i).wait()
-        dh[rows] += got[rows, :D].astype(full)
-        pair = got[rows, D:].astype(full)
-        lane = lanes_of(pair.shape)
-        whole = pair + pltpu.roll(pair, half, 1)
-        dprobs[rows] += jnp.where((lane >= half) & (lane < 2 * half), whole, 0.0)
-
-    for g in range(GROUPS, 2 * GROUPS):
-        start(eighths[g])
-
-    def add(mine, others, columns):
-        @pl.loop(0, parts)
-        def _(p):
-            total = mine[p, :, :, columns].astype(full)
-            for r in range(replicas - 1):
-                total = total + others[r, p, :, :, columns].astype(full)
-            mine[p, :, :, columns] = total.astype(low)
-
-    add(mine_two, others_two, slice(None))
-    homes = homeward(sizes, lambda ref, at, g: ref.at[at], mine_two, two_ref, home_two, 0, 0)
-    start(homes)
+        wait(hop(i))
+        dh[rows] += got[rows].astype(full)
+        place = (near_lanes == half + near_rows % half).astype(low)
+        dprobs[rows] += dot_lt(got_gates[i], place)
+
+    each = mine_one.shape[-1] // GROUPS
+    homes = []
+
+    def send_home(g):
+        wait(eighths[2 * g])
+        wait(eighths[2 * g + 1])
+        add(sizes, mine_one, others_one, slice(None), slice(g * each, (g + 1) * each))
+        copies = homeward(sizes, wide_part, mine_one, one_ref, home_one, g, g)
+        start(copies)
+        homes.extend(copies)
+
+    send_home(0)
+    send_home(1)
     for ref in (qkv_acc, proj_acc, router_acc, norm_acc):
         ref[...] = jnp.zeros_like(ref)
 
@@ -651,20 +718,24 @@
     for i in range(blocks):
         to_core[i].wait()
         kept[i] = (grads[2 * i + core].astype(full) + first[i].astype(full)).astype(low)
+    side = lax.axis_index("part") // 2 % 2
+    to_row = [
+        remote(kept.at[2 * i + 1 - side], second.at[i], row_sems.at[0, i], row_sems.at[1, i], ROW)
+        for i in range(blocks // 2)
+    ]
+    start(to_row)
+    for i in range(blocks // 2):
+        to_row[i].wait()
+        at = 2 * i + side
+        kept[at] = (kept[at].astype(full) + second[i].astype(full)).astype(low)
     to_owner = [
-        remote(kept.at[owner(parts, o) // 2], second.at[i], owner_sems.at[0, i], owner_sems.at[1, i], o)
-        for i, o in enumerate(owners)
+        remote(kept.at[owner(parts, o) // 2], along.at[i], owner_sems.at[0, i], owner_sems.at[1, i], o)
+        for i, o in enumerate(in_line(replicas, parts))
     ]
     start(to_owner)
 
-    each = mine_one.shape[-1] // GROUPS
-    for g in range(GROUPS):
-        wait(eighths[2 * g])
-        wait(eighths[2 * g + 1])
-        add(mine_one, others_one, slice(g * each, (g + 1) * each))
-        copies = homeward(sizes, wide_part, mine_one, one_ref, home_one, g, g)
-        start(copies)
-        homes += copies
+    for g in range(2, GROUPS):
+        send_home(g)
     wait(swaps[0])
 
     @pl.loop(0, images)
@@ -677,7 +748,7 @@
     total = kept[owner(parts) // 2].astype(full)
     for i, copy in enumerate(to_owner):
         copy.wait()
-        total = total + second[i].astype(full)
+        total = total + along[i].astype(full)
     me = lax.axis_index("expert")
     third[me] = total.astype(low)
     to_others = [
@@ -693,44 +764,44 @@
     wait(homes)
 
 
-def close(keys, back, weights, order, x, qkv, ctx, r, sent, probs, dy, theirs, y, dw_one, dw_two, got_two, sizes, number):
+def close(keys, back, weights, order, x, qkv, ctx, r, h, probs, dy, theirs, y, dw_one, sizes, number):
     replicas, parts, groups = sizes
     images = x.shape[0]
     tokens = images * ROWS
     count = y.shape[0]
     owners = replicas * parts
-    shard = (weights.shape[0] // owners, PACKED)
+    shard = weights.shape[1:]
     one = (parts, *dw_one.shape[1:])
-    two = (parts, *dw_two.shape[1:])
+    line = len(in_line(replicas, parts))
     inner = pl.BlockSpec(memory_space=pltpu.VMEM)
     outer = pl.BlockSpec(memory_space=pl.ANY)
     buffers = [
         (x.shape, low), (qkv.shape, low), (ctx.shape, low), (r.shape, full), (x.shape, low),
-        (probs.shape, full), (dy.shape, low), ((tokens, LANES), low), (y.shape, low),
+        (probs.shape, full), (dy.shape, low), (theirs.shape, low), (y.shape, low),
         ((tokens, D), full), ((tokens, LANES), full),
-        ((tokens, SENT), low), ((tokens, SENT), low), ((tokens, D), low), ((tokens, D), low),
-        (one, low), ((replicas - 1, *one), low), (two, low), ((replicas - 1, *two), low),
+        ((tokens, D), low), ((tokens, D), low), ((images, EXPERTS, ROWS), low), ((images, EXPERTS, ROWS), low),
+        ((tokens, D), low), ((tokens, D), low),
+        (one, low), ((replicas - 1, *one), low),
         ((ROWS, QKV), low), ((D, QKV), full), ((D, D), full), ((D, LANES), full), ((LANES, D), full),
         ((owners, *shard), low), ((owners // 2, *shard), low), ((owners // 2, *shard), low),
-        ((owners // 2 - 1, *shard), low), ((groups, *shard), low),
+        ((owners // 4, *shard), low), ((line, *shard), low), ((groups, *shard), low),
     ]
     semaphores = [
-        (12,), (count, 2), (count, 2), (2, images), (2, images), (2, 2 * GROUPS, replicas),
-        (2, GROUPS, parts), (2, 1, parts), (2, owners // 2), (2, owners // 2 - 1), (2, groups - 1),
+        (10,), (count, 2), (count, 2), (2, images), (2, images), (2, images), (2, 2 * GROUPS, replicas),
+        (2, GROUPS, parts), (2, owners // 2), (2, owners // 4), (2, line), (2, groups - 1),
     ]
     arrays = (
-        keys, back, weights, order, x, qkv, ctx, r, sent, probs, dy, theirs, y, dw_one, dw_two, got_two,
+        keys, back, weights, order, x, qkv, ctx, r, h, probs, dy, theirs, y, dw_one,
     )
     return pl.pallas_call(
         partial(close_kernel, sizes),
-        in_specs=[inner] * 4 + [outer] * 12,
-        out_specs=[inner] * 3 + [outer] * 2,
+        in_specs=[inner] * 4 + [outer] * 10,
+        out_specs=[inner] * 3 + [outer],
         out_shape=[
             jax.ShapeDtypeStruct((images, ROWS, D), full),
             jax.ShapeDtypeStruct((tokens, D), low),
             jax.ShapeDtypeStruct(shard, full),
             jax.ShapeDtypeStruct(one, low),
-            jax.ShapeDtypeStruct(two, low),
         ],
         scratch_shapes=[pltpu.VMEM(*b) for b in buffers]
         + [pltpu.SemaphoreType.DMA(n) for n in semaphores],
@@ -765,12 +836,13 @@
     at = pl.program_id(0) * pl.num_programs(1) + pl.program_id(1)
 
     def moved(g):
-        return outward(sizes, tall_part, master_ref, second_ref, flow, g, g - 3)
+        return outward(sizes, small_part, master_ref, second_ref, flow, g, g - EARLY)
 
     @pl.when(at == 0)
     def _():
         greet(all_owners(*sizes[:2]))
-        start(moved(3))
+        for g in range(EARLY, 2 * GROUPS):
+            start(moved(g))
 
     @pl.when(pl.program_id(1) == 0)
     def _():
@@ -795,7 +867,8 @@
 
     @pl.when(at == pl.num_programs(0) * pl.num_programs(1) - 1)
     def _():
-        wait(moved(3))
+        for g in range(EARLY, 2 * GROUPS):
+            wait(moved(g))
 
 
 def slot_spec(sources):
@@ -834,7 +907,7 @@
         ],
         input_output_aliases={6: 3},
         scratch_shapes=[
-            pltpu.VMEM((rows, LANES), full), pltpu.VMEM((D, rows), low), flow_semaphores(sizes, 2),
+            pltpu.VMEM((rows, LANES), full), pltpu.VMEM((D, rows), low), flow_semaphores(sizes, 2 * GROUPS - EARLY),
         ],
         compiler_params=pltpu.CompilerParams(
             dimension_semantics=("arbitrary",) * 2,
@@ -853,12 +926,24 @@
 
 def rest_kernel(
     sizes, own, steps, dy_ref, h_ref, g_ref, slope_ref, w_in_ref, w_out_ref, dw_two_ref,
-    back_ref, dw_ref, y_ref, two_ref, du, acc, dgates, dgate_rows, h_t, staged, sends, receives, local, flow,
+    back_ref, dw_ref, y_ref, two_ref, du, acc, dgates, dgate_rows, h_t, staged, mine_two, others_two,
+    sends, receives, local, flow, home, load,
 ):
     replicas, parts, groups = sizes
 
     def moved(g):
-        return across(sizes, tall_part, dw_two_ref, two_ref, flow, g, g)
+        return across(sizes, tall_part, dw_two_ref, others_two, flow, g, g)
+
+    def homes(g):
+        return homeward(sizes, tall_part, mine_two, two_ref, home, g, g)
+
+    def send_home(g):
+        wait(moved(g))
+        depth = mine_two.shape[2] // GROUPS
+        add(sizes, mine_two, others_two, slice(g * depth, (g + 1) * depth), slice(None))
+        start(homes(g))
+
+    loading = pltpu.make_async_copy(mine_of(sizes, dw_two_ref), mine_two, load)
 
     sources = dy_ref.shape[0]
     tile = slope_ref.shape[2]
@@ -884,6 +969,7 @@
     @pl.when(at == 0)
     def _():
         greet(sorted({near(groups, j) for j in range(1, sources // 2)} | partners(sizes)))
+        loading.start()
         start(moved(0))
         start(moved(1))
 
@@ -932,7 +1018,13 @@
 
     @pl.when(at == own * steps)
     def _():
+        loading.wait()
+        send_home(0)
         start(moved(2))
+
+    @pl.when(at == 2 * own * steps)
+    def _():
+        send_home(1)
         start(moved(3))
 
     @pl.when(phase == 1)
@@ -957,13 +1049,15 @@
 
     @pl.when(at == 3 * own * steps - 1)
     def _():
+        send_home(2)
+        send_home(3)
         for e in range(own):
             for k in range(2, sources):
                 copy(k, e).wait()
             mine(0, e).wait()
             mine(1, e).wait()
         for g in range(GROUPS):
-            wait(moved(g))
+            wait(homes(g))
 
 
 def expert_rest(dy, h, g, slope, w_in, w_out, dw_two, tile, sizes, number):
@@ -1007,14 +1101,14 @@
         out_specs=[
             pl.BlockSpec(memory_space=pl.ANY),
             spec((owners, 1, depth, tile), (1,), in_tile),
-            spec(token, (2,), whole_expert),
+            spec(token, (2,), whole_expert, 1),
             pl.BlockSpec(memory_space=pl.ANY),
         ],
         out_shape=[
             jax.ShapeDtypeStruct((sources, own, CAP + 16, D), low),
             jax.ShapeDtypeStruct(w_in.shape, low),
             jax.ShapeDtypeStruct(dy.shape, low),
-            pieces_of(sizes, dw_two),
+            jax.ShapeDtypeStruct((sizes[1], *dw_two.shape[1:]), low),
         ],
         scratch_shapes=[
             pltpu.VMEM((own * steps, rows, tile), low),
@@ -1023,10 +1117,14 @@
             pltpu.VMEM((16, rows), full),
             pltpu.VMEM((D, rows), low),
             pltpu.VMEM((sources, own, CAP + 16, D), low),
+            pltpu.VMEM((sizes[1], *dw_two.shape[1:]), low),
+            pltpu.VMEM((sizes[0] - 1, sizes[1], *dw_two.shape[1:]), low),
             pltpu.SemaphoreType.DMA((sources, own)),
             pltpu.SemaphoreType.DMA((sources, own)),
             pltpu.SemaphoreType.DMA((2, own)),
-            flow_semaphores(sizes, GROUPS),
+            pltpu.SemaphoreType.DMA((2, GROUPS, sizes[0])),
+            pltpu.SemaphoreType.DMA((2, GROUPS, sizes[1])),
+            pltpu.SemaphoreType.DMA,
         ],
         compiler_params=pltpu.CompilerParams(
             dimension_semantics=("arbitrary",),
@@ -1039,6 +1137,47 @@
         ),
         name="expert_rest",
     )(dy, h, g, slope, w_in, w_out, dw_two)
+
+
+def finish_kernel(out_ref, dx_ref, dense_ref, one_ref, two_ref, output, input_grad, qkv, proj, one, two):
+    one[...] = one_ref[...].astype(full)
+    two[...] = two_ref[...].astype(full)
+    images = dx_ref.shape[0]
+
+    @pl.when(pl.program_id(0) == 0)
+    def _():
+        qkv[...] = dense_ref[:, :QKV]
+        proj[...] = dense_ref[:, QKV : QKV + D]
+        for i in range(images):
+            input_grad[i * SEQ : (i + 1) * SEQ] = dx_ref[i, :SEQ]
+            rows = out_ref[i * ROWS : i * ROWS + SEQ].astype(full)
+            output[i * SEQ : (i + 1) * SEQ] = rows.astype(low)
+
+
+def finish(output, dx, dense, one, two):
+    images = dx.shape[0]
+    tokens = (images * SEQ, D)
+    steps = one.shape[0]
+    widths = [(dense.shape[0], QKV), (dense.shape[0], D)]
+    block = lambda a: pl.BlockSpec((1, *a.shape[1:]), lambda i: (i,) + (0,) * (a.ndim - 1))
+    return pl.pallas_call(
+        finish_kernel,
+        grid=(steps,),
+        in_specs=[whole_spec(a.shape) for a in (output, dx, dense)] + [block(one), block(two)],
+        out_specs=[whole_spec(a) for a in (tokens, tokens, *widths)] + [block(one), block(two)],
+        out_shape=[
+            jax.ShapeDtypeStruct(tokens, low),
+            jax.ShapeDtypeStruct(tokens, full),
+            *(jax.ShapeDtypeStruct(a, full) for a in widths),
+            jax.ShapeDtypeStruct(one.shape, full),
+            jax.ShapeDtypeStruct(two.shape, full),
+        ],
+        compiler_params=pltpu.CompilerParams(
+            dimension_semantics=("arbitrary",), vmem_limit_bytes=BIG
+        ),
+        cost_estimate=pl.CostEstimate(flops=0, bytes_accessed=19 * 10**6, transcendentals=0),
+        name="finish",
+    )(output, dx, dense, one, two)
 
 
 ALL = ("replica", "part")
@@ -1070,7 +1209,7 @@
     placed_router = (
         w_router.reshape(small_rows, groups, parts, own).transpose(0, 2, 1, 3).reshape(small_rows, EXPERTS)
     )
-    vectors = jnp.stack([ln1_gain, ln1_bias, ln2_gain, ln2_bias], axis=1)
+    vectors = jnp.concatenate([ln1_gain, ln1_bias, ln2_gain, ln2_bias]).reshape(4, small_rows).T
     packed = jnp.concatenate(
         [w_qkv, w_proj, placed_router, vectors, jnp.zeros((small_rows, LANES - EXPERTS - 4), full)],
         axis=1,
@@ -1078,12 +1217,6 @@
     me = lax.axis_index("part") * groups + lax.axis_index("expert")
     sizes = (replicas, parts, groups)
 
-    def padded(rows, fill=0):
-        rows = rows.reshape(images, SEQ, rows.shape[1])
-        return jnp.pad(rows, ((0, 0), (0, ROWS - SEQ), (0, 0)), constant_values=fill)
-
-    x = padded(tokens)
-    dy = padded(cotangent)
     half = parts // 2
     flips = [(i, i ^ half) for i in range(parts)]
     picks = jnp.stack([choices, lax.ppermute(choices, "part", flips)]).reshape(2 * images, SEQ, 2)
@@ -1106,35 +1239,28 @@
         keys, ((0, 0), (0, 0), (0, LANES - EXPERTS // 2)), constant_values=-1
     ).astype(low)
 
-    first_master, second_master = w_expert_in.astype(low), w_expert_out.astype(low)
-    dy_slots, weights, first_weight = dispatch(
-        key_rows, dy.reshape(count, D), sizes, 0, first_master, packed
-    )
-    weights = weights.reshape(D, PACKED)
-    qkv, ctx, r, sent, probs, first_weight = attend(
-        x, weights, order, first_master, first_weight, sizes, 6
-    )
-    h_slots, theirs, second_weight = dispatch(
-        key_rows, sent.reshape(count, SENT), sizes, 1, second_master
-    )
+    (
+        x, dy, dy_slots, h_slots, weights, first_weight, second_weight, qkv, ctx, r, h, probs, theirs, second_master,
+    ) = forward(key_rows, cotangent, tokens, order, packed, w_expert_in, w_expert_out, sizes, 0)
     dy_slots = dy_slots.reshape(peers, own, CAP, D)
     h_slots = h_slots.reshape(peers, own, CAP, D)
     select = ((me * own + jnp.arange(own))[:, None, None] == lane[None, None, :]).astype(full)
     g, slope, dw_second, second_weight = expert_first(
-        h_slots, dy_slots, first_weight, weights[:, QKV + D :], select, second_master, second_weight,
+        h_slots, dy_slots, first_weight, weights[:, :, QKV + D :].reshape(D, LANES), select, second_master, second_weight,
         sizes, tile, 5,
     )
-    back, dw_first, y, got_second = expert_rest(
+    back, dw_first, y, second_grad = expert_rest(
         dy_slots, h_slots, g, slope, first_weight, second_weight, dw_second, tile, sizes, 2
     )
     back = back.reshape(peers // 2, 2, own, CAP + 16, D)
     y = y.reshape(peers // 2, 2, own, CAP, D)
-    dx, output, grads, first_grad, second_grad = close(
-        key_columns, back, weights, order, x, qkv, ctx, r, sent, probs, dy, theirs, y,
-        dw_first, dw_second, got_second, sizes, 3,
+    dx, output, grads, first_grad = close(
+        key_columns, back, weights, order, x, qkv, ctx, r, h, probs, dy, theirs, y,
+        dw_first, sizes, 3,
     )
-    expert_in_grad = first_grad.reshape(w_expert_in.shape).astype(full)
-    expert_out_grad = second_grad.reshape(w_expert_out.shape).astype(full)
+    output, input_grad, qkv_grad, proj_grad, expert_in_grad, expert_out_grad = finish(
+        output, dx, grads, first_grad, second_grad
+    )
     router_grad = (
         grads[:, QKV + D : QKV + D + EXPERTS]
         .reshape(small_rows, parts, groups, own)
@@ -1143,21 +1269,18 @@
     )
     norms = [grads[:, QKV + D + EXPERTS + i] for i in range(4)]
 
-    def unpadded(rows):
-        return rows.reshape(images, ROWS, D)[:, :SEQ].reshape(images * SEQ, D)
-
     return (
-        unpadded(output),
-        unpadded(dx),
+        output,
+        input_grad,
         norms[0],
         norms[1],
-        grads[:, :QKV],
-        grads[:, QKV : QKV + D],
+        qkv_grad,
+        proj_grad,
         norms[2],
         norms[3],
         router_grad,
-        expert_in_grad,
-        expert_out_grad,
+        expert_in_grad.reshape(w_expert_in.shape),
+        expert_out_grad.reshape(w_expert_out.shape),
     )
 
 

time: 599 us -> 519 us (0.87)
  Pallas kernels: 552 us -> 493 us
  other arithmetic: 18.9 us -> 6.76 us
  local copies, waits for them, and re-layouts: 17.7 us -> 9.16 us
    pallas_call x1, Pallas kernels: 174 us -> 137 us  [close(): pl.pallas_call(partial(close_kernel, sizes), in_specs=[inner] * 4 + [oute...]
    pallas_call x3 -> x2, Pallas kernels: 227 us -> 197 us  [the longest x1 187 us: forward(): pl.pallas_call(partial(open_kernel, sizes), in_specs=[inner] * 4 + [outer...]
    convert_element_type x4 -> x0, other arithmetic: 14.6 us -> none  [the longest x1 4.18 us: body(): expert_out_grad = second_grad.reshape(w_expert_out.shape).astype(full)]
    pallas_call x1, Pallas kernels: 100 us -> 114 us  [expert_rest(): pl.pallas_call(partial(rest_kernel, sizes, own, steps), grid=(3 * own * s...]
  transfers between devices with their start and end apart: 1 -> 1, of which waited for: 0 -> 0; matrix products, arithmetic and copies ran while one was open for 3% -> 1% of each run, Pallas kernels for 0% -> 0%
where the time goes in v6:
time: 519 us; the launch traced here: 511 us
  Pallas kernels  493 us (95%)
  local copies, waits for them, and re-layouts  9.16 us (2%)
  other arithmetic  6.76 us (1%)
    pallas_call x1, Pallas kernels, forward(): pl.pallas_call(partial(open_kernel, sizes), in_specs=[inner] * 4 + [outer...  187 us
    pallas_call x1, Pallas kernels, close(): pl.pallas_call(partial(close_kernel, sizes), in_specs=[inner] * 4 + [oute...  137 us
    pallas_call x1, Pallas kernels, expert_rest(): pl.pallas_call(partial(rest_kernel, sizes, own, steps), grid=(3 * own * s...  114 us
    pallas_call x1, Pallas kernels, expert_first(): pl.pallas_call(partial(first_kernel, sizes), grid=(own, hidden // tile),...  45.5 us
  transfers between devices with their start and end apart: 1, of which 0 were waited for; matrix products, arithmetic and copies ran while one was open for 1% of the time, Pallas kernels for 0%

profile of v6, /device:TPU:13, one launch (start us, length us, event | category | flops | bytes accessed | tf_op | source)
XLA Modules:
  0.0 510.7 jit_solution(14186750363737546858)
XLA Ops:
  0.6 0.2 collective-permute-start
  0.9 0.6 fusion.4.order_ref
  1.5 0.7 convert.37
  2.2 0.7 convert.38
  2.9 0.7 convert.39
  3.5 0.7 convert.40
  4.2 0.6 compare_convert_fusion.sel_ref
  4.8 0.1 pad_maximum_fusion
  4.9 0.9 convert.34
  5.8 0.8 convert.35
  6.7 0.8 copy.64
  7.5 0.1 copy.67
  7.6 0.1 reshape.114
  7.7 0.1 copy.66
  7.8 0.8 concatenate.9.shard_ref
  8.5 0.0 collective-permute-done
  8.5 0.7 pad_add_fusion
  9.2 0.1 reshape.110
  9.3 0.1 eq.53
  9.5 0.1 compare_reduce_fusion
  9.6 0.5 bitcast_select_fusion.1
  10.1 0.5 copy.62
  10.6 0.1 copy.63
  10.6 0.7 copy.68.keys_ref
  11.4 187.0 %forward.1 = (bf16[5,208,512]{2,1,0:T(8,128)(2,1)}, bf16[5,208,512]{2,1,0:T(8,128)(2,1)}, bf16[8,2,2,128,512]{4,3,2,1,0:T(8,128)(2,1)}, bf16[8,2,2,128,512]{4,3,...) custom-call(f32[2,8,2,1040]{3,2,1,0:T(2,128)} %copy.68.keys_ref, ...), custom_call_target="tpu_custom_call" | custom-call | flops 60000002048 | bytes 30000000 | tf_op jit(solution)/shard_map/forward/pallas_call | solution.py:481
  198.4 1.6 slice.22
  200.0 0.3 copy.61
  200.3 0.2 fusion.3
  200.5 0.9 pad.14.keys_ref
  201.4 45.5 %expert_first.1 = (bf16[2,2048,2048]{2,1,0:T(8,128)(2,1)}, bf16[2,2048,2048]{2,1,0:T(8,128)(2,1)}, bf16[16,2,128,512]{3,2,1,0:T(8,128)(2,1)}, bf16[16,2,128,512]{3,2,1,0:T(8,128)(2,1)}) custom-call(bf16[16,2,128,512]{3,2,1,0:T(8,128)(2,1)} %bitcast.51, bf16[16,2,128,512]{3,2,1,0:T(8,128)(2,1)} %bitcast.49, ...), custom_call_target="tpu_custom_call", output_to_operand_aliasing={{3}: (6, {})} | custom-call | flops 17179869184 | bytes 50000000 | tf_op jit(solution)/shard_map/expert_first/pallas_call | solution.py:884
  246.9 114.0 %expert_rest.1 = (bf16[16,2,144,512]{3,2,1,0:T(8,128)(2,1)}, bf16[16,2,32,2048]{3,2,1,0:T(8,128)(2,1)}, bf16[16,2,128,512]{3,2,1,0:T(8,128)(2,1)}, bf16[8,2,128,512]{3,2,1,0:T(8,128)(2,1)}) custom-call(bf16[16,2,128,512]{3,2,1,0:T(8,128)(2,1)} %bitcast.50, bf16[16,2,128,512]{3,2,1,0:T(8,128)(2,1)} %bitcast.52, ...), custom_call_target="tpu_custom_call" | custom-call | flops 34359738368 | bytes 60000000 | tf_op jit(solution)/shard_map/expert_rest/pallas_call | solution.py:1089
  360.9 136.7 %close.1 = (f32[5,208,512]{2,1,0:T(8,128)}, bf16[1040,512]{1,0:T(8,128)(2,1)}, f32[32,2176]{1,0:T(8,128)}, bf16[8,2,32,2048]{3,2,1,0:T(8,128)(2,1)}) custom-call(bf16[2,1040,128]{2,1,0:T(8,128)(2,1)} %pad.14.keys_ref, bf16[8,2,2,144,512]{4,3,2,1,0:T(8,128)(2,1)} %bitcast.48, bf16[16,32,2176]{2,1,0:T(8,128)(2,1)} %get-tuple-element.46.w_ref, ...), custom_call_target="tpu_custom_call" | custom-call | flops 60000002048 | bytes 30000000 | tf_op jit(solution)/shard_map/close/pallas_call | solution.py:796
  497.6 0.7 slice.27
  498.4 1.6 slice_reduce_fusion
  500.0 0.1 copy.69
  500.1 0.7 copy.71
  500.7 9.7 %finish.1 = (bf16[985,512]{1,0:T(8,128)(2,1)}, f32[985,512]{1,0:T(8,128)}, f32[32,1536]{1,0:T(8,128)}, f32[32,512]{1,0:T(8,128)}, f32[8,2,32,2048]{3,2,1,0:T(8,128)}, /*index=5*/f32[8,2,128,512]{3,2,1,0:T(8,128)}) custom-call(bf16[1040,512]{1,0:T(8,128)(2,1)} %get-tuple-element.64.out_ref, f32[5,208,512]{2,1,0:T(8,128)} %get-tuple-element.65.dx_ref, ...), custom_call_target="tpu_custom_call" | custom-call | bytes 19000000 | tf_op jit(solution)/shard_map/finish/pallas_call | solution.py:1163
  (9 shorter events, 0.1 us)
Async XLA Ops:
  0.6 7.9 %collective-permute-start = (s32[985,2]{0,1:T(2,128)}, s32[985,2]{0,1:T(2,128)S(1)}, u32[]{:S(2)}, u32[]{:S(2)}) collective-permute-start(s32[985,2]{0,1:T(2,128)} %param.13), channel_id=1, source_target_pairs={{0,8},{2,10},{4,12},{6,14},{8,0},{10,2},{12,4},{14,6},{1,9},{3,11}... | collective-permute-start | bytes 23648 | tf_op jit(solution)/shard_map/ppermute | solution.py:1222

commit v7 on v6

--- a/solution.py
+++ b/solution.py
@@ -1139,6 +1139,304 @@
     )(dy, h, g, slope, w_in, w_out, dw_two)
 
 
+def experts_kernel(
+    sizes, own, steps, h_ref, dy_ref, w_in_ref, wr_ref, sel_ref, master_ref, _,
+    back_ref, dw_ref, y_ref, two_ref, second_ref,
+    hidden, slopes, acc, column, dgate_rows, turned, staged, dw_two, others, w_tiles,
+    sends, receives, local, flow, cross, home, tile_sems,
+):
+    replicas, parts, groups = sizes
+    sources = dy_ref.shape[0]
+    tile = hidden.shape[2]
+    owners, _, per, _ = dw_two.shape
+    span = tile // per
+    chunk = 2 * CAP
+    at = pl.program_id(0)
+    total = own * steps
+    phase, expert, step = at // total, at // steps % own, at % steps
+    now = at % total
+    first_of_mine = lax.axis_index("replica") * parts
+
+    def weight_part(g):
+        return outward(sizes, small_part, master_ref, second_ref, flow, g, g - EARLY)
+
+    def tile_copy(t):
+        rows = pl.ds(t % steps * span, span)
+        return pltpu.make_async_copy(
+            second_ref.at[rows, t // steps], w_tiles.at[t % 2], tile_sems.at[t % 2]
+        )
+
+    def rows_of(q, count):
+        return pl.ds(q * (per // count), per // count)
+
+    def crossing(e, q):
+        return [
+            remote(
+                dw_two.at[pl.ds((lax.axis_index("replica") ^ r) * parts, parts), e, rows_of(q, 4)],
+                others.at[r - 1, :, e, rows_of(q, 4)],
+                cross.at[0, 4 * e + q, r], cross.at[1, 4 * e + q, r], (r, 0, 0),
+            )
+            for r in range(1, replicas)
+        ]
+
+    def homes(e, q):
+        here = lax.axis_index("part")
+
+        def source(p):
+            return dw_two.at[first_of_mine + (here ^ p), e, rows_of(q, 2)]
+
+        target = two_ref.at[here, e, rows_of(q, 2)]
+        slot = 2 * e + q
+        copies = [
+            remote(source(p), target, home.at[0, slot, p], home.at[1, slot, p], (0, p, 0))
+            for p in range(1, parts)
+        ]
+        return copies + [pltpu.make_async_copy(source(0), target, home.at[0, slot, 0])]
+
+    def send_home(e, q):
+        wait(crossing(e, 2 * q))
+        wait(crossing(e, 2 * q + 1))
+        rows = slice(q * (per // 2), (q + 1) * (per // 2))
+
+        @pl.loop(0, parts)
+        def _(p):
+            value = dw_two[first_of_mine + p, e, rows].astype(full)
+            for r in range(replicas - 1):
+                value = value + others[r, p, e, rows].astype(full)
+            dw_two[first_of_mine + p, e, rows] = value.astype(low)
+
+        start(homes(e, q))
+
+    def copy(k, e):
+        if k < 2:
+            return pltpu.make_async_copy(staged.at[k, e], back_ref.at[k, e], local.at[k, e])
+        return remote(
+            staged.at[k, e], back_ref.at[k, e], sends.at[k, e], receives.at[k, e], near(groups, k // 2)
+        )
+
+    @pl.when(at == 0)
+    def _():
+        greet(sorted({near(groups, j) for j in range(1, sources // 2)} | {*all_owners(replicas, parts)}))
+        for g in range(EARLY, 2 * GROUPS):
+            start(weight_part(g))
+
+    @pl.when(phase == 0)
+    def _():
+        @pl.when(step == 0)
+        def _():
+            for k in range(sources):
+                rows = slice(k * CAP, (k + 1) * CAP)
+                logits = dot(h_ref[k, 0], wr_ref[...])
+                logits = jnp.where(lanes_of(logits.shape) < EXPERTS, logits, -1e30)
+                grown = jnp.exp(logits - jnp.max(logits, axis=-1, keepdims=True))
+                mine = jnp.sum(grown * sel_ref[0], axis=-1, keepdims=True)
+                gate = mine / jnp.sum(grown, axis=-1, keepdims=True)
+                column[rows] = jnp.broadcast_to(gate, (CAP, LANES))
+                turned[:, rows] = (dy_ref[k, 0].astype(full) * gate).T.astype(low)
+
+        w_in = w_in_ref[:, 0].reshape(D, tile)
+        for k in range(0, sources, 2):
+            rows = slice(k * CAP, (k + 2) * CAP)
+            value, slope = gelu_pair(dot(h_ref[k : k + 2, 0].reshape(chunk, D), w_in))
+            hidden[now, rows] = value.astype(low)
+            slopes[now, rows] = (slope * column[rows, :1]).astype(low)
+        grad = dot(turned[...], hidden[now]).T.astype(low)
+        dw_two[pl.ds(step * span, span), expert] = grad.reshape(span, per, D)
+
+    for e in range(own):
+        @pl.when(at == (e + 1) * steps - 1)
+        def _():
+            if e == 0:
+                start(crossing(0, 0))
+                start(crossing(0, 1))
+            if e == own - 1:
+                for g in range(EARLY, 2 * GROUPS):
+                    wait(weight_part(g))
+                tile_copy(0).start()
+                start(crossing(0, 2))
+                start(crossing(0, 3))
+
+    @pl.when(phase % 2 == 1)
+    def _():
+        tile_copy(now).wait()
+
+        @pl.when(now < total - 1)
+        def _():
+            tile_copy(now + 1).start()
+
+        @pl.when(step == 0)
+        def _():
+            acc[...] = jnp.zeros_like(acc)
+
+    @pl.when(phase == 1)
+    def _():
+        @pl.when(step == 0)
+        def _():
+            column[...] = jnp.zeros_like(column)
+
+        w_in = w_in_ref[:, 0].reshape(D, tile)
+        w_out = w_tiles[now % 2].reshape(tile, D)
+        for k in range(0, sources, 2):
+            rows = slice(k * CAP, (k + 2) * CAP)
+            dg = dot_rt(dy_ref[k : k + 2, 0].reshape(chunk, D), w_out)
+            change = (dg * slopes[now, rows].astype(full)).astype(low)
+            slopes[now, rows] = change
+            acc[rows] += dot_rt(change, w_in)
+            agreed = dg * hidden[now, rows].astype(full)
+            column[rows] += sum(agreed[:, i : i + LANES] for i in range(0, tile, LANES))
+
+        @pl.when(step == steps - 1)
+        def _():
+            sums = column[...]
+            high = sums.astype(low)
+            rest = (sums - high.astype(full)).astype(low)
+            ones = jnp.ones((16, LANES), low)
+            dgate_rows[...] = dot_rt(ones, high) + dot_rt(ones, rest)
+            for k in range(sources):
+                rows = slice(k * CAP, (k + 1) * CAP)
+                staged[k, expert, :CAP] = acc[rows].astype(low)
+                row = dgate_rows[:, rows]
+                high = row.astype(low)
+                staged[k, expert, CAP:, :CAP] = high
+                staged[k, expert, CAP:, CAP : 2 * CAP] = (row - high.astype(full)).astype(low)
+                staged[k, expert, CAP:, 2 * CAP :] = jnp.zeros((16, D - 2 * CAP), low)
+
+        for e in range(own):
+            @pl.when((step == steps - 1) & (expert == e))
+            def _():
+                for k in range(sources):
+                    copy(k, e).start()
+
+    @pl.when(at == total + steps)
+    def _():
+        send_home(0, 0)
+        start(crossing(1, 0))
+        start(crossing(1, 1))
+
+    @pl.when(phase == 2)
+    def _():
+        @pl.when(step == 0)
+        def _():
+            for k in range(sources):
+                turned[:, k * CAP : (k + 1) * CAP] = h_ref[k, 0].T
+
+        grad = dot(turned[...], slopes[now]).astype(low)
+        dw_ref[:, 0] = grad.reshape(dw_ref.shape[0], dw_ref.shape[2], tile)
+
+        @pl.when(now == total - 1)
+        def _():
+            tile_copy(0).start()
+
+    @pl.when(at == 2 * total + 2)
+    def _():
+        send_home(0, 1)
+        start(crossing(1, 2))
+        start(crossing(1, 3))
+
+    @pl.when(phase == 3)
+    def _():
+        w_out = w_tiles[now % 2].reshape(tile, D)
+        for k in range(0, sources, 2):
+            rows = slice(k * CAP, (k + 2) * CAP)
+            acc[rows] += dot(hidden[now, rows], w_out)
+
+        @pl.when(step == steps - 1)
+        def _():
+            y_ref[:, 0] = acc[...].astype(low).reshape(sources, CAP, D)
+
+    @pl.when(at == 4 * total - 1)
+    def _():
+        for e in range(own):
+            for k in range(sources):
+                copy(k, e).wait()
+        send_home(1, 0)
+        send_home(1, 1)
+        for e in range(own):
+            for q in range(2):
+                wait(homes(e, q))
+
+
+def experts(h, dy, w_in, w_router, select, master, second, sizes, tile, number):
+    sources = h.shape[0]
+    owners, own, depth, width = w_in.shape
+    rows = sources * CAP
+    per = width // owners
+    steps = width // tile
+    total = own * steps
+
+    def during(*phases):
+        def find(at):
+            inside = jnp.where(at // total < phases[0], 0, total - 1)
+            for phase in phases:
+                inside = jnp.where(at // total == phase, at % total, inside)
+            return inside // steps, inside % steps
+
+        return find
+
+    def spec(shape, phases, index, buffers=2):
+        return pl.BlockSpec(
+            shape, lambda at: index(*during(*phases)(at)), pipeline_mode=pl.Buffered(buffers)
+        )
+
+    token = (sources, 1, CAP, D)
+    whole_expert = lambda e, f: (0, e, 0, 0)
+    in_tile = lambda e, f: (0, e, 0, f)
+    outer = pl.BlockSpec(memory_space=pl.ANY)
+    two = (sizes[1], own, per, D)
+    return pl.pallas_call(
+        partial(experts_kernel, sizes, own, steps),
+        grid=(4 * total,),
+        in_specs=[
+            spec(token, (0, 2), whole_expert, 1),
+            spec(token, (0, 1), whole_expert, 1),
+            spec((owners, 1, depth, tile), (0, 1), in_tile),
+            whole_spec(w_router.shape),
+            spec((1, 1, LANES), (0,), lambda e, f: (e, 0, 0)),
+            outer,
+            outer,
+        ],
+        out_specs=[
+            outer,
+            spec((owners, 1, depth, tile), (2,), in_tile),
+            spec(token, (3,), whole_expert, 1),
+            outer,
+            outer,
+        ],
+        out_shape=[
+            jax.ShapeDtypeStruct((sources, own, CAP + 16, D), low),
+            jax.ShapeDtypeStruct(w_in.shape, low),
+            jax.ShapeDtypeStruct((sources, own, CAP, D), low),
+            jax.ShapeDtypeStruct(two, low),
+            jax.ShapeDtypeStruct(second.shape, low),
+        ],
+        input_output_aliases={6: 4},
+        scratch_shapes=[
+            pltpu.VMEM((total, rows, tile), low),
+            pltpu.VMEM((total, rows, tile), low),
+            pltpu.VMEM((rows, D), full),
+            pltpu.VMEM((rows, LANES), full),
+            pltpu.VMEM((16, rows), full),
+            pltpu.VMEM((D, rows), low),
+            pltpu.VMEM((sources, own, CAP + 16, D), low),
+            pltpu.VMEM((owners, own, per, D), low),
+            pltpu.VMEM((sizes[0] - 1, *two), low),
+            pltpu.VMEM((2, tile // per, per, D), low),
+            pltpu.SemaphoreType.DMA((sources, own)),
+            pltpu.SemaphoreType.DMA((sources, own)),
+            pltpu.SemaphoreType.DMA((2, own)),
+            flow_semaphores(sizes, 2 * GROUPS - EARLY),
+            pltpu.SemaphoreType.DMA((2, 4 * own, sizes[0])),
+            pltpu.SemaphoreType.DMA((2, 2 * own, sizes[1])),
+            pltpu.SemaphoreType.DMA((2,)),
+        ],
+        compiler_params=remote_params(1, number),
+        cost_estimate=pl.CostEstimate(
+            flops=12 * own * rows * D * width, bytes_accessed=40 * 10**6, transcendentals=own * rows * width
+        ),
+        name="experts",
+    )(h, dy, w_in, w_router, select, master, second)
+
+
 def finish_kernel(out_ref, dx_ref, dense_ref, one_ref, two_ref, output, input_grad, qkv, proj, one, two):
     one[...] = one_ref[...].astype(full)
     two[...] = two_ref[...].astype(full)
@@ -1245,13 +1543,19 @@
     dy_slots = dy_slots.reshape(peers, own, CAP, D)
     h_slots = h_slots.reshape(peers, own, CAP, D)
     select = ((me * own + jnp.arange(own))[:, None, None] == lane[None, None, :]).astype(full)
-    g, slope, dw_second, second_weight = expert_first(
-        h_slots, dy_slots, first_weight, weights[:, :, QKV + D :].reshape(D, LANES), select, second_master, second_weight,
-        sizes, tile, 5,
-    )
-    back, dw_first, y, second_grad = expert_rest(
-        dy_slots, h_slots, g, slope, first_weight, second_weight, dw_second, tile, sizes, 2
-    )
+    routers = weights[:, :, QKV + D :].reshape(D, LANES)
+    if own == 2:
+        back, dw_first, y, second_grad, _ = experts(
+            h_slots, dy_slots, first_weight, routers, select, second_master, second_weight, sizes, tile, 4,
+        )
+    else:
+        g, slope, dw_second, second_weight = expert_first(
+            h_slots, dy_slots, first_weight, routers, select, second_master, second_weight,
+            sizes, tile, 5,
+        )
+        back, dw_first, y, second_grad = expert_rest(
+            dy_slots, h_slots, g, slope, first_weight, second_weight, dw_second, tile, sizes, 2
+        )
     back = back.reshape(peers // 2, 2, own, CAP + 16, D)
     y = y.reshape(peers // 2, 2, own, CAP, D)
     dx, output, grads, first_grad = close(

time: 519 us -> 510 us (0.983)
  Pallas kernels: 493 us -> 484 us
    pallas_call x2 -> x1, Pallas kernels: 160 us -> 152 us  [experts(): pl.pallas_call(partial(experts_kernel, sizes, own, steps), grid=(4 * tota...]
  transfers between devices with their start and end apart: 1 -> 1, of which waited for: 0 -> 0; matrix products, arithmetic and copies ran while one was open for 1% -> 2% of each run, Pallas kernels for 0% -> 0%
where the time goes in v7:
time: 510 us; the launch traced here: 502 us
  Pallas kernels  484 us (95%)
  local copies, waits for them, and re-layouts  9.18 us (2%)
  other arithmetic  6.76 us (1%)
    pallas_call x1, Pallas kernels, forward(): pl.pallas_call(partial(open_kernel, sizes), in_specs=[inner] * 4 + [outer...  187 us
    pallas_call x1, Pallas kernels, experts(): pl.pallas_call(partial(experts_kernel, sizes, own, steps), grid=(4 * tota...  152 us
    pallas_call x1, Pallas kernels, close(): pl.pallas_call(partial(close_kernel, sizes), in_specs=[inner] * 4 + [oute...  135 us
  transfers between devices with their start and end apart: 1, of which 0 were waited for; matrix products, arithmetic and copies ran while one was open for 2% of the time, Pallas kernels for 0%

profile of v7, /device:TPU:13, one launch (start us, length us, event | category | flops | bytes accessed | tf_op | source)
XLA Modules:
  0.0 501.6 jit_solution(9289338063563401622)
XLA Ops:
  0.6 0.2 collective-permute-start
  0.9 0.6 fusion.4.order_ref
  1.5 0.7 convert.37
  2.2 0.7 convert.38
  2.9 0.7 convert.39
  3.5 0.7 convert.40
  4.2 0.6 compare_convert_fusion.sel_ref
  4.8 0.1 pad_maximum_fusion
  4.9 0.9 convert.34
  5.8 0.8 convert.35
  6.7 0.8 copy.64
  7.5 0.1 copy.67
  7.6 0.1 reshape.114
  7.7 0.1 copy.66
  7.8 0.8 concatenate.9.shard_ref
  8.5 0.0 collective-permute-done
  8.5 0.7 pad_add_fusion
  9.2 0.1 reshape.110
  9.3 0.1 eq.53
  9.5 0.1 compare_reduce_fusion
  9.6 0.5 bitcast_select_fusion.1
  10.1 0.5 copy.62
  10.6 0.1 copy.63
  10.6 0.7 copy.68.keys_ref
  11.4 187.0 %forward.1 = (bf16[5,208,512]{2,1,0:T(8,128)(2,1)}, bf16[5,208,512]{2,1,0:T(8,128)(2,1)}, bf16[8,2,2,128,512]{4,3,2,1,0:T(8,128)(2,1)}, bf16[8,2,2,128,512]{4,3,...) custom-call(f32[2,8,2,1040]{3,2,1,0:T(2,128)} %copy.68.keys_ref, ...), custom_call_target="tpu_custom_call" | custom-call | flops 60000002048 | bytes 30000000 | tf_op jit(solution)/shard_map/forward/pallas_call | solution.py:481
  198.4 1.6 slice.22
  200.0 0.3 copy.61
  200.3 0.2 fusion.3
  200.4 0.9 pad.14.keys_ref
  201.3 152.0 %experts.1 = (bf16[16,2,144,512]{3,2,1,0:T(8,128)(2,1)}, bf16[16,2,32,2048]{3,2,1,0:T(8,128)(2,1)}, bf16[16,2,128,512]{3,2,1,0:T(8,128)(2,1)}, bf16[8,2,128,512]{3,2,1,0:T(8,128)(2,1)}, bf16[16,2,128,512]{3,2,1,0:T(8,128)(2,1)}) custom-call(bf16[16,2,128,512]{3,2,1,0:T(8,128)(2,1)} %bitcast.50, ...), custom_call_target="tpu_custom_call", output_to_operand_aliasing={{4}: (6, {})} | custom-call | flops 51539607552 | bytes 40000000 | tf_op jit(solution)/shard_map/experts/pallas_call | solution.py:1386
  353.3 135.0 %close.1 = (f32[5,208,512]{2,1,0:T(8,128)}, bf16[1040,512]{1,0:T(8,128)(2,1)}, f32[32,2176]{1,0:T(8,128)}, bf16[8,2,32,2048]{3,2,1,0:T(8,128)(2,1)}) custom-call(bf16[2,1040,128]{2,1,0:T(8,128)(2,1)} %pad.14.keys_ref, bf16[8,2,2,144,512]{4,3,2,1,0:T(8,128)(2,1)} %bitcast.48, bf16[16,32,2176]{2,1,0:T(8,128)(2,1)} %get-tuple-element.42.w_ref, ...), custom_call_target="tpu_custom_call" | custom-call | flops 60000002048 | bytes 30000000 | tf_op jit(solution)/shard_map/close/pallas_call | solution.py:796
  488.3 0.7 slice.27
  489.1 1.6 slice_reduce_fusion
  490.7 0.1 copy.69
  490.8 0.7 copy.71
  491.5 9.7 %finish.1 = (bf16[985,512]{1,0:T(8,128)(2,1)}, f32[985,512]{1,0:T(8,128)}, f32[32,1536]{1,0:T(8,128)}, f32[32,512]{1,0:T(8,128)}, f32[8,2,32,2048]{3,2,1,0:T(8,128)}, /*index=5*/f32[8,2,128,512]{3,2,1,0:T(8,128)}) custom-call(bf16[1040,512]{1,0:T(8,128)(2,1)} %get-tuple-element.56.out_ref, f32[5,208,512]{2,1,0:T(8,128)} %get-tuple-element.57.dx_ref, ...), custom_call_target="tpu_custom_call" | custom-call | bytes 19000000 | tf_op jit(solution)/shard_map/finish/pallas_call | solution.py:1461
  (9 shorter events, 0.1 us)
Async XLA Ops:
  0.6 7.9 %collective-permute-start = (s32[985,2]{0,1:T(2,128)}, s32[985,2]{0,1:T(2,128)S(1)}, u32[]{:S(2)}, u32[]{:S(2)}) collective-permute-start(s32[985,2]{0,1:T(2,128)} %param.13), channel_id=1, source_target_pairs={{0,8},{2,10},{4,12},{6,14},{8,0},{10,2},{12,4},{14,6},{1,9},{3,11}... | collective-permute-start | bytes 23648 | tf_op jit(solution)/shard_map/ppermute | solution.py:1520

commit v8 on v7

--- a/solution.py
+++ b/solution.py
@@ -1246,15 +1246,10 @@
     for e in range(own):
         @pl.when(at == (e + 1) * steps - 1)
         def _():
-            if e == 0:
-                start(crossing(0, 0))
-                start(crossing(0, 1))
             if e == own - 1:
                 for g in range(EARLY, 2 * GROUPS):
                     wait(weight_part(g))
                 tile_copy(0).start()
-                start(crossing(0, 2))
-                start(crossing(0, 3))
 
     @pl.when(phase % 2 == 1)
     def _():
@@ -1307,12 +1302,6 @@
                 for k in range(sources):
                     copy(k, e).start()
 
-    @pl.when(at == total + steps)
-    def _():
-        send_home(0, 0)
-        start(crossing(1, 0))
-        start(crossing(1, 1))
-
     @pl.when(phase == 2)
     def _():
         @pl.when(step == 0)
@@ -1326,12 +1315,6 @@
         @pl.when(now == total - 1)
         def _():
             tile_copy(0).start()
-
-    @pl.when(at == 2 * total + 2)
-    def _():
-        send_home(0, 1)
-        start(crossing(1, 2))
-        start(crossing(1, 3))
 
     @pl.when(phase == 3)
     def _():
@@ -1343,6 +1326,18 @@
         @pl.when(step == steps - 1)
         def _():
             y_ref[:, 0] = acc[...].astype(low).reshape(sources, CAP, D)
+
+    for number, turn in enumerate(
+        (5, total - 1, total + 2, total + 4, total + 7, 2 * total + 3, 3 * total + 1, 4 * total - 1)
+    ):
+        @pl.when(at == turn)
+        def _():
+            start(crossing(number // 4, number % 4))
+
+    for number, turn in enumerate((total + 6, 2 * total + 6)):
+        @pl.when(at == turn)
+        def _():
+            send_home(0, number)
 
     @pl.when(at == 4 * total - 1)
     def _():
@@ -1390,7 +1385,7 @@
             spec(token, (0, 2), whole_expert, 1),
             spec(token, (0, 1), whole_expert, 1),
             spec((owners, 1, depth, tile), (0, 1), in_tile),
-            whole_spec(w_router.shape),
+            pl.BlockSpec((D, LANES), lambda at: (0, (QKV + D) // LANES)),
             spec((1, 1, LANES), (0,), lambda e, f: (e, 0, 0)),
             outer,
             outer,
@@ -1455,9 +1450,11 @@
 def finish(output, dx, dense, one, two):
     images = dx.shape[0]
     tokens = (images * SEQ, D)
-    steps = one.shape[0]
+    steps = min(4, one.shape[0])
     widths = [(dense.shape[0], QKV), (dense.shape[0], D)]
-    block = lambda a: pl.BlockSpec((1, *a.shape[1:]), lambda i: (i,) + (0,) * (a.ndim - 1))
+    block = lambda a: pl.BlockSpec(
+        (a.shape[0] // steps, *a.shape[1:]), lambda i: (i,) + (0,) * (a.ndim - 1)
+    )
     return pl.pallas_call(
         finish_kernel,
         grid=(steps,),
@@ -1511,7 +1508,8 @@
     packed = jnp.concatenate(
         [w_qkv, w_proj, placed_router, vectors, jnp.zeros((small_rows, LANES - EXPERTS - 4), full)],
         axis=1,
-    ).astype(low)
+    )
+    packed = lax.optimization_barrier(packed).astype(low)
     me = lax.axis_index("part") * groups + lax.axis_index("expert")
     sizes = (replicas, parts, groups)
 
@@ -1543,14 +1541,14 @@
     dy_slots = dy_slots.reshape(peers, own, CAP, D)
     h_slots = h_slots.reshape(peers, own, CAP, D)
     select = ((me * own + jnp.arange(own))[:, None, None] == lane[None, None, :]).astype(full)
-    routers = weights[:, :, QKV + D :].reshape(D, LANES)
+    routers = weights.reshape(D, PACKED)
     if own == 2:
         back, dw_first, y, second_grad, _ = experts(
             h_slots, dy_slots, first_weight, routers, select, second_master, second_weight, sizes, tile, 4,
         )
     else:
         g, slope, dw_second, second_weight = expert_first(
-            h_slots, dy_slots, first_weight, routers, select, second_master, second_weight,
+            h_slots, dy_slots, first_weight, routers[:, QKV + D :], select, second_master, second_weight,
             sizes, tile, 5,
         )
         back, dw_first, y, second_grad = expert_rest(

time: 510 us -> 502 us (0.984)
  transfers between devices with their start and end apart: 1 -> 1, of which waited for: 0 -> 0; matrix products, arithmetic and copies ran while one was open for 2% -> 1% of each run, Pallas kernels for 0% -> 0%
where the time goes in v8:
time: 502 us; the launch traced here: 495 us
  Pallas kernels  481 us (96%)
  local copies, waits for them, and re-layouts  8.54 us (2%)
    pallas_call x1, Pallas kernels, forward(): pl.pallas_call(partial(open_kernel, sizes), in_specs=[inner] * 4 + [outer...  187 us
    pallas_call x1, Pallas kernels, experts(): pl.pallas_call(partial(experts_kernel, sizes, own, steps), grid=(4 * tota...  148 us
    pallas_call x1, Pallas kernels, close(): pl.pallas_call(partial(close_kernel, sizes), in_specs=[inner] * 4 + [oute...  138 us
  transfers between devices with their start and end apart: 1, of which 0 were waited for; matrix products, arithmetic and copies ran while one was open for 1% of the time, Pallas kernels for 0%

profile of v8, /device:TPU:13, one launch (start us, length us, event | category | flops | bytes accessed | tf_op | source)
XLA Modules:
  0.0 494.5 jit_solution(4994303975717427983)
XLA Ops:
  0.6 0.2 collective-permute-start
  0.9 0.6 fusion.4.order_ref
  1.5 0.6 compare_convert_fusion.sel_ref
  2.2 0.8 pad_maximum_fusion
  3.0 0.8 copy.64
  3.8 0.1 copy.67
  3.9 0.1 reshape.111
  3.9 0.1 copy.66
  4.1 1.7 concatenate.7.shard_ref
  5.7 0.0 collective-permute-done
  5.7 0.7 pad_add_fusion
  6.5 0.1 reshape.107
  6.6 0.1 eq.53
  6.7 0.1 compare_reduce_fusion
  6.8 0.5 bitcast_select_fusion.1
  7.3 0.5 copy.62
  7.8 0.1 copy.63
  7.8 0.7 copy.68.keys_ref
  8.6 0.3 copy.61
  8.9 0.2 fusion.3
  9.1 0.9 pad.14.keys_ref
  10.0 187.0 %forward.1 = (bf16[5,208,512]{2,1,0:T(8,128)(2,1)}, bf16[5,208,512]{2,1,0:T(8,128)(2,1)}, bf16[8,2,2,128,512]{4,3,2,1,0:T(8,128)(2,1)}, bf16[8,2,2,128,512]{4,3,...) custom-call(f32[2,8,2,1040]{3,2,1,0:T(2,128)} %copy.68.keys_ref, ...), custom_call_target="tpu_custom_call" | custom-call | flops 60000002048 | bytes 30000000 | tf_op jit(solution)/shard_map/forward/pallas_call | solution.py:481
  197.0 147.5 %experts.1 = (bf16[16,2,144,512]{3,2,1,0:T(8,128)(2,1)}, bf16[16,2,32,2048]{3,2,1,0:T(8,128)(2,1)}, bf16[16,2,128,512]{3,2,1,0:T(8,128)(2,1)}, bf16[8,2,128,512]{3,2,1,0:T(8,128)(2,1)}, bf16[16,2,128,512]{3,2,1,0:T(8,128)(2,1)}) custom-call(bf16[16,2,128,512]{3,2,1,0:T(8,128)(2,1)} %bitcast.50, ...), custom_call_target="tpu_custom_call", output_to_operand_aliasing={{4}: (6, {})} | custom-call | flops 51539607552 | bytes 40000000 | tf_op jit(solution)/shard_map/experts/pallas_call | solution.py:1381
  344.5 138.1 %close.1 = (f32[5,208,512]{2,1,0:T(8,128)}, bf16[1040,512]{1,0:T(8,128)(2,1)}, f32[32,2176]{1,0:T(8,128)}, bf16[8,2,32,2048]{3,2,1,0:T(8,128)(2,1)}) custom-call(bf16[2,1040,128]{2,1,0:T(8,128)(2,1)} %pad.14.keys_ref, bf16[8,2,2,144,512]{4,3,2,1,0:T(8,128)(2,1)} %bitcast.47, bf16[16,32,2176]{2,1,0:T(8,128)(2,1)} %get-tuple-element.42.w_ref, ...), custom_call_target="tpu_custom_call" | custom-call | flops 60000002048 | bytes 30000000 | tf_op jit(solution)/shard_map/close/pallas_call | solution.py:796
  482.6 0.7 slice.23
  483.4 1.6 slice_reduce_fusion
  485.0 0.1 copy.69
  485.1 0.7 copy.71
  485.8 8.3 %finish.1 = (bf16[985,512]{1,0:T(8,128)(2,1)}, f32[985,512]{1,0:T(8,128)}, f32[32,1536]{1,0:T(8,128)}, f32[32,512]{1,0:T(8,128)}, f32[8,2,32,2048]{3,2,1,0:T(8,128)}, /*index=5*/f32[8,2,128,512]{3,2,1,0:T(8,128)}) custom-call(bf16[1040,512]{1,0:T(8,128)(2,1)} %get-tuple-element.56.out_ref, f32[5,208,512]{2,1,0:T(8,128)} %get-tuple-element.57.dx_ref, ...), custom_call_target="tpu_custom_call" | custom-call | bytes 19000000 | tf_op jit(solution)/shard_map/finish/pallas_call | solution.py:1458
  (9 shorter events, 0.1 us)
Async XLA Ops:
  0.6 5.1 %collective-permute-start = (s32[985,2]{0,1:T(2,128)}, s32[985,2]{0,1:T(2,128)S(1)}, u32[]{:S(2)}, u32[]{:S(2)}) collective-permute-start(s32[985,2]{0,1:T(2,128)} %param.13), channel_id=1, source_target_pairs={{0,8},{2,10},{4,12},{6,14},{8,0},{10,2},{12,4},{14,6},{1,9},{3,11}... | collective-permute-start | bytes 23648 | tf_op jit(solution)/shard_map/ppermute | solution.py:1518

commit v9 on v8

--- a/solution.py
+++ b/solution.py
@@ -1432,7 +1432,10 @@
     )(h, dy, w_in, w_router, select, master, second)
 
 
-def finish_kernel(out_ref, dx_ref, dense_ref, one_ref, two_ref, output, input_grad, qkv, proj, one, two):
+def finish_kernel(
+    sizes, out_ref, dx_ref, dense_ref, one_ref, two_ref,
+    output, input_grad, qkv, proj, router, norms, one, two,
+):
     one[...] = one_ref[...].astype(full)
     two[...] = two_ref[...].astype(full)
     images = dx_ref.shape[0]
@@ -1441,22 +1444,34 @@
     def _():
         qkv[...] = dense_ref[:, :QKV]
         proj[...] = dense_ref[:, QKV : QKV + D]
+        _, parts, groups = sizes
+        own = EXPERTS // (parts * groups)
+        tile = dense_ref[:, QKV + D :]
+        place = lax.broadcasted_iota(jnp.int32, (LANES, EXPERTS), 0)
+        expert = lanes_of((LANES, EXPERTS))
+        group, part = expert // (parts * own), expert // own % parts
+        moved = place == (part * groups + group) * own + expert % own
+        router[...] = jnp.dot(
+            tile, moved.astype(full), preferred_element_type=full, precision=lax.Precision.HIGHEST
+        )
+        norms[...] = tile.T[EXPERTS : EXPERTS + 8]
         for i in range(images):
             input_grad[i * SEQ : (i + 1) * SEQ] = dx_ref[i, :SEQ]
             rows = out_ref[i * ROWS : i * ROWS + SEQ].astype(full)
             output[i * SEQ : (i + 1) * SEQ] = rows.astype(low)
 
 
-def finish(output, dx, dense, one, two):
+def finish(output, dx, dense, one, two, sizes):
     images = dx.shape[0]
     tokens = (images * SEQ, D)
     steps = min(4, one.shape[0])
-    widths = [(dense.shape[0], QKV), (dense.shape[0], D)]
+    depth = dense.shape[0]
+    widths = [(depth, QKV), (depth, D), (depth, EXPERTS), (8, depth)]
     block = lambda a: pl.BlockSpec(
         (a.shape[0] // steps, *a.shape[1:]), lambda i: (i,) + (0,) * (a.ndim - 1)
     )
     return pl.pallas_call(
-        finish_kernel,
+        partial(finish_kernel, sizes),
         grid=(steps,),
         in_specs=[whole_spec(a.shape) for a in (output, dx, dense)] + [block(one), block(two)],
         out_specs=[whole_spec(a) for a in (tokens, tokens, *widths)] + [block(one), block(two)],
@@ -1560,17 +1575,9 @@
         key_columns, back, weights, order, x, qkv, ctx, r, h, probs, dy, theirs, y,
         dw_first, sizes, 3,
     )
-    output, input_grad, qkv_grad, proj_grad, expert_in_grad, expert_out_grad = finish(
-        output, dx, grads, first_grad, second_grad
+    output, input_grad, qkv_grad, proj_grad, router_grad, norms, expert_in_grad, expert_out_grad = finish(
+        output, dx, grads, first_grad, second_grad, sizes
     )
-    router_grad = (
-        grads[:, QKV + D : QKV + D + EXPERTS]
-        .reshape(small_rows, parts, groups, own)
-        .transpose(0, 2, 1, 3)
-        .reshape(small_rows, EXPERTS)
-    )
-    norms = [grads[:, QKV + D + EXPERTS + i] for i in range(4)]
-
     return (
         output,
         input_grad,

time: 502 us -> 501 us (level)
  no operation moved by 1% of the time
where the time goes in v9:
time: 501 us; the launch traced here: 493 us
  Pallas kernels  481 us (96%)
  local copies, waits for them, and re-layouts  6.78 us (1%)
    pallas_call x1, Pallas kernels, forward(): pl.pallas_call(partial(open_kernel, sizes), in_specs=[inner] * 4 + [outer...  187 us
    pallas_call x1, Pallas kernels, experts(): pl.pallas_call(partial(experts_kernel, sizes, own, steps), grid=(4 * tota...  148 us
    pallas_call x1, Pallas kernels, close(): pl.pallas_call(partial(close_kernel, sizes), in_specs=[inner] * 4 + [oute...  138 us
  transfers between devices with their start and end apart: 1, of which 0 were waited for; matrix products, arithmetic and copies ran while one was open for 1% of the time, Pallas kernels for 0%

profile of v9, /device:TPU:13, one launch (start us, length us, event | category | flops | bytes accessed | tf_op | source)
XLA Modules:
  0.0 492.9 jit_solution(7979634804979847306)
XLA Ops:
  0.6 0.2 collective-permute-start
  0.9 0.6 fusion.4.order_ref
  1.5 0.6 compare_convert_fusion.sel_ref
  2.2 0.8 pad_maximum_fusion
  3.0 0.8 copy.57
  3.8 0.1 copy.60
  3.9 0.1 reshape.105
  3.9 0.1 copy.59
  4.1 1.7 concatenate.7.shard_ref
  5.7 0.0 collective-permute-done
  5.7 0.7 pad_add_fusion
  6.5 0.1 reshape.101
  6.6 0.1 eq.53
  6.7 0.1 compare_reduce_fusion
  6.8 0.5 bitcast_select_fusion.1
  7.3 0.5 copy.55
  7.8 0.1 copy.56
  7.8 0.7 copy.61.keys_ref
  8.6 0.3 copy.54
  8.9 0.2 fusion.3
  9.1 0.9 pad.14.keys_ref
  10.0 187.0 %forward.1 = (bf16[5,208,512]{2,1,0:T(8,128)(2,1)}, bf16[5,208,512]{2,1,0:T(8,128)(2,1)}, bf16[8,2,2,128,512]{4,3,2,1,0:T(8,128)(2,1)}, bf16[8,2,2,128,512]{4,3,...) custom-call(f32[2,8,2,1040]{3,2,1,0:T(2,128)} %copy.61.keys_ref, ...), custom_call_target="tpu_custom_call" | custom-call | flops 60000002048 | bytes 30000000 | tf_op jit(solution)/shard_map/forward/pallas_call | solution.py:481
  197.0 147.6 %experts.1 = (bf16[16,2,144,512]{3,2,1,0:T(8,128)(2,1)}, bf16[16,2,32,2048]{3,2,1,0:T(8,128)(2,1)}, bf16[16,2,128,512]{3,2,1,0:T(8,128)(2,1)}, bf16[8,2,128,512]{3,2,1,0:T(8,128)(2,1)}, bf16[16,2,128,512]{3,2,1,0:T(8,128)(2,1)}) custom-call(bf16[16,2,128,512]{3,2,1,0:T(8,128)(2,1)} %bitcast.52, ...), custom_call_target="tpu_custom_call", output_to_operand_aliasing={{4}: (6, {})} | custom-call | flops 51539607552 | bytes 40000000 | tf_op jit(solution)/shard_map/experts/pallas_call | solution.py:1381
  344.6 138.1 %close.1 = (f32[5,208,512]{2,1,0:T(8,128)}, bf16[1040,512]{1,0:T(8,128)(2,1)}, f32[32,2176]{1,0:T(8,128)}, bf16[8,2,32,2048]{3,2,1,0:T(8,128)(2,1)}) custom-call(bf16[2,1040,128]{2,1,0:T(8,128)(2,1)} %pad.14.keys_ref, bf16[8,2,2,144,512]{4,3,2,1,0:T(8,128)(2,1)} %bitcast.49, bf16[16,32,2176]{2,1,0:T(8,128)(2,1)} %get-tuple-element.44.w_ref, ...), custom_call_target="tpu_custom_call" | custom-call | flops 60000002048 | bytes 30000000 | tf_op jit(solution)/shard_map/close/pallas_call | solution.py:796
  482.7 8.4 %finish.1 = (bf16[985,512]{1,0:T(8,128)(2,1)}, f32[985,512]{1,0:T(8,128)}, f32[32,1536]{1,0:T(8,128)}, f32[32,512]{1,0:T(8,128)}, f32[32,32]{1,0:T(8,128)}, /*in...) custom-call(bf16[1040,512]{1,0:T(8,128)(2,1)} %get-tuple-element.58.out_ref, ...), custom_call_target="tpu_custom_call" | custom-call | bytes 19000000 | tf_op jit(solution)/shard_map/finish/pallas_call | solution.py:1473
  491.1 1.4 slice_bitcast_fusion
  (8 shorter events, 0.1 us)
Async XLA Ops:
  0.6 5.1 %collective-permute-start = (s32[985,2]{0,1:T(2,128)}, s32[985,2]{0,1:T(2,128)S(1)}, u32[]{:S(2)}, u32[]{:S(2)}) collective-permute-start(s32[985,2]{0,1:T(2,128)} %param.13), channel_id=1, source_target_pairs={{0,8},{2,10},{4,12},{6,14},{8,0},{10,2},{12,4},{14,6},{1,9},{3,11}... | collective-permute-start | bytes 23648 | tf_op jit(solution)/shard_map/ppermute | solution.py:1533
